TPU v7x, 512 devices: a whole 4x4x16 slice. The times are simulated.
512 devices in a mesh: seq: 32 (over x, z_lo), head: 8 (over y, core), enc: 2 (over z_hi).
Axes of the slice: x: 4, y: 4, z: 16 (z_hi: 2, z_lo: 8; z = z_hi * 8 + z_lo), core: 2. Of those that a mesh axis runs over, the one named last changes fastest.
Arguments:
- queries: bfloat16 [10240, 4096], P('seq', ('head', 'enc')), may hold values from -2000 to 2000
- keys: bfloat16 [10240, 4096], P('seq', ('head', 'enc')), may hold values from -2000 to 2000
- values: bfloat16 [10240, 4096], P('seq', ('head', 'enc')), may hold values from -6 to 6
- out_weight: bfloat16 [4096, 5120], P(('head', 'enc'), 'seq'), may hold values from -0.1875 to 0.1875
- q_gain: float32 [4096], P(('head', 'enc')), may hold values from 0.75 to 3
- k_gain: float32 [4096], P(('head', 'enc')), may hold values from 0.75 to 3
- gate: float32 [5120], P(('head', 'enc')), may hold values from 1 to 8
- valid_count: int32 [1], replicated, may hold values from 5120 to 10240
Outputs:
- update: bfloat16 [10240, 5120], P('seq', ('head', 'enc'))
Inputs may be any that keep to these rules, and one draw needn't show every extreme that they name: Key positions from valid_count[0] on are padding and take no weight.
All inputs are finite; a program needn't handle non-finite values.
Results may differ from a plain program's by a relative error of at most 0.015.
The roundings to bfloat16 on the way count: a program that leaves them out, or rounds other values in their place, can miss the bound.
Values may be sent and summed in bfloat16 or wider, within the bound.
No kernel may reach another device: no remote copies, remote signals or barrier semaphores. Data moves between devices by JAX's collectives and lax.ppermute only.
A program may use at most 64 MiB of HBM per device.

v0:
```python
import jax
import jax.numpy as jnp
from jax import lax
from jax.sharding import PartitionSpec as P

HEAD_DIM = 128


epsilon = 1e-06
lowest_score = -1e30


def normalize(matrix, squares, gain_row, feature_count):
    inverse_rms = lax.rsqrt(squares / feature_count + epsilon)
    return (matrix.astype(jnp.float32) * inverse_rms[:, None] * gain_row[None, :]).astype(
        jnp.bfloat16
    )


def absorb(carried, query_heads, key_block, value_block, offset, key_limit):
    running_sum, running_max, running_mass = carried
    scale_factor = query_heads.shape[2] ** (-0.5)
    scores = (
        jnp.einsum("qhd,khd->hqk", query_heads, key_block, preferred_element_type=jnp.float32)
        * scale_factor
    )
    position = offset + jnp.arange(key_block.shape[0], dtype=jnp.int32)
    usable = (position < key_limit)[None, None, :]
    masked = jnp.where(usable, scores, lowest_score)
    new_max = jnp.maximum(running_max, jnp.max(masked, axis=2))
    weights = jnp.where(usable, jnp.exp(masked - new_max[:, :, None]), 0.0)
    factor = jnp.exp(running_max - new_max)
    running_mass = running_mass * factor + jnp.sum(weights, axis=2)
    running_sum = running_sum * factor[:, :, None] + jnp.einsum(
        "hqk,khd->hqd",
        weights.astype(jnp.bfloat16),
        value_block,
        preferred_element_type=jnp.float32,
    )
    return (running_sum, new_max, running_mass)


def absorb_blocks(carried, query_heads, key_rows, value_rows, key_limit):
    row_total = key_rows.shape[0]
    block_size = 512
    block_count = row_total // block_size
    key_blocks = key_rows.reshape((block_count, block_size) + key_rows.shape[1:])
    value_blocks = value_rows.reshape((block_count, block_size) + value_rows.shape[1:])

    def absorb_block(running, triple):
        block_number, key_block, value_block = triple
        return (
            absorb(
                running, query_heads, key_block, value_block, block_number * block_size, key_limit
            ),
            None,
        )

    numbers = jnp.arange(block_count, dtype=jnp.int32)
    carried, _ = lax.scan(absorb_block, carried, (numbers, key_blocks, value_blocks))
    return carried


def visit(carried, query_heads, key_rows, value_rows, key_limit):
    return absorb_blocks(carried, query_heads, key_rows, value_rows, key_limit)


def local(queries, keys, values, out_weight, q_gain, k_gain, gate, valid_count):
    row_count = queries.shape[0]
    local_heads = queries.shape[1] // HEAD_DIM
    feature_count = queries.shape[1] * lax.axis_size(("head", "enc"))
    key_limit = valid_count[0]
    query_squares = jnp.sum(jnp.square(queries.astype(jnp.float32)), axis=1)
    key_squares = jnp.sum(jnp.square(keys.astype(jnp.float32)), axis=1)
    query_totals, key_totals = lax.psum((query_squares, key_squares), ("head", "enc"))
    query_heads = normalize(queries, query_totals, q_gain, feature_count).reshape(
        row_count, local_heads, HEAD_DIM
    )
    key_heads = normalize(keys, key_totals, k_gain, feature_count).reshape(
        row_count, local_heads, HEAD_DIM
    )
    value_heads = values.reshape(row_count, local_heads, HEAD_DIM)
    initial = (
        jnp.zeros((local_heads, row_count, HEAD_DIM), jnp.float32),
        jnp.full((local_heads, row_count), lowest_score, jnp.float32),
        jnp.zeros((local_heads, row_count), jnp.float32),
    )
    running_sum, running_max, running_mass = visit(
        initial,
        query_heads,
        lax.all_gather(key_heads, "seq", axis=0, tiled=True),
        lax.all_gather(value_heads, "seq", axis=0, tiled=True),
        key_limit,
    )
    attended = (running_sum / running_mass[:, :, None]).transpose(1, 0, 2)
    attended = attended.reshape(row_count, local_heads * HEAD_DIM).astype(jnp.bfloat16)
    terms = jnp.dot(
        attended,
        lax.all_gather(out_weight, "seq", axis=1, tiled=True),
        preferred_element_type=jnp.float32,
    )
    summed = lax.psum_scatter(
        terms.astype(jnp.bfloat16), ("head", "enc"), scatter_dimension=1, tiled=True
    ).astype(jnp.float32)
    return (gate[None, :] * summed).astype(jnp.bfloat16)


def solution(mesh):
    placed = (
        P("seq", ("head", "enc")),
        P("seq", ("head", "enc")),
        P("seq", ("head", "enc")),
        P(("head", "enc"), "seq"),
        P(("head", "enc")),
        P(("head", "enc")),
        P(("head", "enc")),
        P(),
    )
    return jax.shard_map(
        local, mesh=mesh, in_specs=placed, out_specs=P("seq", ("head", "enc")), check_vma=False
    )
```

profile of v0, /device:TPU:6, one launch (start us, length us, event | category | flops | bytes accessed | tf_op | source)
XLA Modules:
  0.0 957.6 jit_solution(13073559487828346287)
XLA Ops:
  6.5 1.1 fusion.11
  7.6 1.1 fusion.14
  8.7 78.0 %all-reduce = (f32[320]{0:T(512)S(1)}, f32[320]{0:T(512)S(1)}) all-reduce(f32[320]{0:T(512)S(1)} %fusion.11, f32[320]{0:T(512)S(1)} %fusion.14), channel_id=1, replica_groups=mesh['seq'=32,'head'=8,'enc'=2] {'head','enc'}, use_global_device_ids=true, to_apply=%region_1.0 | all-reduce | flops 640 | bytes 5120 | tf_op jit(solution)/shard_map/psum | solution.py:75
  86.7 1.0 fusion.13
  87.7 0.7 reshape.32
  88.5 1.6 reshape.35
  90.2 0.7 all-gather.8.cloned.1.call-update
  91.1 214.2 %all-gather.4.cloned.1.call-done = bf16[10240,2,128]{2,1,0:T(2,128)(2,1)} async-done(((bf16[320,2,128]{2,1,0:T(2,128)(2,1)}), bf16[10240,2,128]{2,1,0:T(2,128)(2,1)}) %all-gather.4.cloned.1.call-update) | async-done | bytes 5242896 | tf_op jit(solution)/shard_map/all_gather | solution.py:91
  305.4 242.4 %all-gather.6.cloned.1.call-done = bf16[10240,2,128]{2,1,0:T(2,128)(2,1)} async-done(((bf16[320,2,128]{2,1,0:T(2,128)(2,1)}), bf16[10240,2,128]{2,1,0:T(2,128)(2,1)}) %all-gather.6.cloned.1.call-update) | async-done | bytes 5242896 | tf_op jit(solution)/shard_map/all_gather | solution.py:92
  547.8 92.4 %while.15 = (s32[]{:T(128)}, f32[2,320,128]{2,1,0:T(8,128)S(1)}, f32[2,320]{1,0:T(2,128)S(1)}, f32[2,320]{1,0:T(2,128)S(1)}, s32[20]{0:T(128)S(1)}, /*index=5*/s...) while((s32[]{:T(128)}, f32[2,320,128]{2,1,0:T(8,128)S(1)}, ...), condition=%wide.region_7.8_spmd.clone, body=%wide.region_4.7_spmd.clone.sunk | while | flops 170971264 | bytes 6367397 | solution.py:60
  549.0 0.7 add_compare_fusion.2
  549.7 1.4 constant_dynamic-slice_fusion.3
  552.4 0.6 dynamic_slice.19
  553.6 0.7 add_compare_fusion.2
  554.3 1.4 constant_dynamic-slice_fusion.3
  558.2 0.7 add_compare_fusion.2
  558.9 1.4 constant_dynamic-slice_fusion.3
  562.9 0.7 add_compare_fusion.2
  563.5 1.4 constant_dynamic-slice_fusion.3
  566.3 0.6 dynamic_slice.19
  567.5 0.7 add_compare_fusion.2
  568.2 1.4 constant_dynamic-slice_fusion.3
  570.9 0.6 dynamic_slice.19
  572.1 0.7 add_compare_fusion.2
  572.8 1.4 constant_dynamic-slice_fusion.3
  575.5 0.6 dynamic_slice.19
  576.7 0.7 add_compare_fusion.2
  577.4 1.4 constant_dynamic-slice_fusion.3
  580.1 0.6 dynamic_slice.19
  581.4 0.7 add_compare_fusion.2
  582.0 1.4 constant_dynamic-slice_fusion.3
  584.7 0.6 dynamic_slice.19
  586.0 0.7 add_compare_fusion.2
  586.6 1.4 constant_dynamic-slice_fusion.3
  589.4 0.6 dynamic_slice.19
  590.6 0.7 add_compare_fusion.2
  591.3 1.4 constant_dynamic-slice_fusion.3
  594.0 0.6 dynamic_slice.19
  595.2 0.7 add_compare_fusion.2
  595.9 1.4 constant_dynamic-slice_fusion.3
  599.9 0.7 add_compare_fusion.2
  600.5 1.4 constant_dynamic-slice_fusion.3
  604.5 0.7 add_compare_fusion.2
  605.1 1.4 constant_dynamic-slice_fusion.3
  609.1 0.7 add_compare_fusion.2
  609.8 1.4 constant_dynamic-slice_fusion.3
  613.7 0.7 add_compare_fusion.2
  614.4 1.4 constant_dynamic-slice_fusion.3
  618.3 0.7 add_compare_fusion.2
  619.0 1.4 constant_dynamic-slice_fusion.3
  623.0 0.7 add_compare_fusion.2
  623.6 1.4 constant_dynamic-slice_fusion.3
  627.6 0.7 add_compare_fusion.2
  628.3 1.4 constant_dynamic-slice_fusion.3
  632.2 0.7 add_compare_fusion.2
  632.9 1.4 constant_dynamic-slice_fusion.3
  636.8 0.7 add_compare_fusion.2
  637.5 1.4 constant_dynamic-slice_fusion.3
  640.2 136.3 %all-gather.8.cloned.1.call-done = bf16[256,5120]{0,1:T(8,128)(2,1)} async-done(((bf16[256,160]{0,1:T(8,128)(2,1)}), bf16[256,5120]{0,1:T(8,128)(2,1)}) %all-gather.8.cloned.1.call-update) | async-done | bytes 2621456 | tf_op jit(solution)/shard_map/all_gather | solution.py:99
  776.5 2.9 convolution_convert_fusion
  779.4 3.6 copy.29
  783.1 166.1 %reduce-scatter.4.cloned.1.call-done = bf16[320,320]{1,0:T(8,128)(2,1)} async-done(((bf16[5120,320]{1,0:T(8,128)(2,1)}), bf16[320,320]{1,0:T(8,128)(2,1)}) %reduce-scatter.4.cloned.1.call-update) | async-done | bytes 204816
  949.2 1.1 copy.30
  950.4 0.7 multiply_convert_fusion
  (153 shorter events, 33.0 us)
Async XLA Ops:
  6.5 84.5 %copy-start.1 = (bf16[320,256]{1,0:T(8,128)(2,1)S(1)}, bf16[320,256]{1,0:T(8,128)(2,1)}, u32[]{:S(2)}) copy-start(bf16[320,256]{1,0:T(8,128)(2,1)} %param.10) | copy-start | bytes 491524
  6.5 84.5 %copy-start.3 = (f32[256]{0:T(256)S(1)}, f32[256]{0:T(256)}, u32[]{:S(2)}) copy-start(f32[256]{0:T(256)} %param.14) | copy-start | bytes 3076
  6.5 298.8 %all-gather.4.cloned.1.call-start = ((), (), s32[]{:S(2)}) async-start(), calls=%async_computation.1 | async-start | bytes 5406720 | tf_op jit(solution)/shard_map/all_gather | solution.py:91
  88.5 459.3 %all-gather.6.cloned.1.call-start = ((), (), s32[]{:S(2)}) async-start(), calls=%async_computation.2 | async-start | bytes 5406720 | tf_op jit(solution)/shard_map/all_gather | solution.py:92
  90.2 686.3 %all-gather.8.cloned.1.call-start = ((), (), s32[]{:S(2)}) async-start(), calls=%async_computation.3 | async-start | bytes 2703360 | tf_op jit(solution)/shard_map/all_gather | solution.py:99
  90.9 858.3 %reduce-scatter.4.cloned.1.call-start = ((), (), s32[]{:S(2)}) async-start(), calls=%async_computation.4 | async-start | bytes 4177920
  640.2 136.3 %copy-start = (f32[2,320,128]{2,1,0:T(8,128)}, f32[2,320,128]{2,1,0:T(8,128)S(1)}, u32[]{:S(2)}) copy-start(f32[2,320,128]{2,1,0:T(8,128)S(1)} %get-tuple-element.53) | copy-start | bytes 983044
  783.1 167.3 %copy-start.2 = (f32[320]{0:T(512)S(1)}, f32[320]{0:T(512)}, u32[]{:S(2)}) copy-start(f32[320]{0:T(512)} %param.16) | copy-start | bytes 3844
Sparse Core Ops, SparseCore 0:
  88.6 216.7 all-gather.3
  307.4 240.2 all-gather.5
  549.9 226.6 all-gather.7
  783.2 165.9 reduce-scatter.3
where the time goes:
time: 959 us; the launch traced here: 958 us
  waiting for transfers between devices  760 us (79%)
  blocking collectives  78 us (8%)
  local copies, waits for them, and re-layouts  46.8 us (5%)
  other arithmetic  25.5 us (3%)
  matrix products  20.2 us (2%)
  loops' own time  14.1 us (1%)
  between operations  13.2 us (1%)
    all_gather x1, waiting for transfers between devices, local(): lax.all_gather(value_heads, 'seq', axis=0, tiled=True)  242 us
    all_gather x1, waiting for transfers between devices, local(): lax.all_gather(key_heads, 'seq', axis=0, tiled=True)  214 us
    unnamed x5, waiting for transfers between devices  167 us
    all_gather x1, waiting for transfers between devices, local(): lax.all_gather(out_weight, 'seq', axis=1, tiled=True)  136 us
    psum x1, blocking collectives, local(): lax.psum((query_squares, key_squares), ('head', 'enc'))  78 us
    dynamic_slice x40, local copies, waits for them, and re-layouts, absorb_blocks(): lax.scan(absorb_block, carried, (numbers, key_blocks, value_blocks))  39.7 us
  transfers between devices with their start and end apart: 4, of which 4 were waited for; matrix products, arithmetic and copies ran while one was open for 8% of the time, Pallas kernels for 0%

commit v1 on v0

v1 whole, which is shorter than its diff:
```python
import functools
import math

import jax
import jax.numpy as jnp
from jax import lax
from jax.experimental import pallas as pl
from jax.experimental.pallas import tpu as pltpu
from jax.sharding import Mesh
from jax.sharding import PartitionSpec as P

HEAD_DIM = 128
EPSILON = 1e-06
BIAS = -1e30
F32 = jnp.float32
BF16 = jnp.bfloat16
AXES = ("x", "zl", "y", "core", "zh")
SIZES = (4, 8, 4, 2, 2)
SWAP = ((0, 1), (1, 0))


def attention_kernel(
    limit_ref, q_ref, kv_ref, inverse_ref, gain_ref, out_ref, kt_ref, ve_ref, *, heads, keys
):
    tile = q_ref.shape[0]
    factor = HEAD_DIM**-0.5 * math.log2(math.e)

    @pl.when(pl.program_id(0) == 0)
    def _():
        position = lax.broadcasted_iota(jnp.int32, (HEAD_DIM, keys), 1)
        row = lax.broadcasted_iota(jnp.int32, (HEAD_DIM, keys), 0)
        bias = jnp.where((position >= limit_ref[0]) & (row == 0), BIAS, 0.0).astype(BF16)
        for h in range(heads):
            columns = slice(h * HEAD_DIM, (h + 1) * HEAD_DIM)
            raw = kv_ref[:, columns].T.astype(F32)
            kt_ref[h, :HEAD_DIM, :] = (raw * inverse_ref[...] * gain_ref[columns, :]).astype(BF16)
            kt_ref[h, HEAD_DIM:, :] = bias
            ve_ref[h, :, :HEAD_DIM] = kv_ref[:, (heads + h) * HEAD_DIM : (heads + h + 1) * HEAD_DIM]
            ve_ref[h, :, HEAD_DIM:] = jnp.ones((keys, HEAD_DIM), BF16)

    lane = lax.broadcasted_iota(jnp.int32, (tile, HEAD_DIM), 1)
    first = jnp.where(lane == 0, 1.0, 0.0).astype(BF16)
    stats = jnp.zeros((tile, HEAD_DIM), F32)
    for h in range(heads):
        query = jnp.concatenate([q_ref[:, h * HEAD_DIM : (h + 1) * HEAD_DIM], first], axis=1)
        scores = jnp.dot(query, kt_ref[h], preferred_element_type=F32)
        top = (jnp.max(scores, axis=1, keepdims=True) * factor).astype(BF16).astype(F32)
        weights = jnp.exp2(scores * factor - top).astype(BF16)
        summed = jnp.dot(weights, ve_ref[h], preferred_element_type=F32)
        out_ref[:, h * HEAD_DIM : (h + 1) * HEAD_DIM] = summed[:, :HEAD_DIM].astype(BF16)
        mass = summed[:, HEAD_DIM:]
        high = mass.astype(BF16).astype(F32)
        stats = jnp.where(lane == 3 * h, top, stats)
        stats = jnp.where(lane == 3 * h + 1, high, stats)
        stats = jnp.where(lane == 3 * h + 2, mass - high, stats)
    out_ref[:, heads * HEAD_DIM :] = stats.astype(BF16)


def attention(limit, queries, keys_values, inverse, gain):
    rows, width = queries.shape
    keys = keys_values.shape[0]
    heads = width // HEAD_DIM
    tile = 256
    return pl.pallas_call(
        functools.partial(attention_kernel, heads=heads, keys=keys),
        grid=(rows // tile,),
        in_specs=[
            pl.BlockSpec(memory_space=pltpu.SMEM),
            pl.BlockSpec((tile, width), lambda i: (i, 0)),
            pl.BlockSpec((keys, 2 * width), lambda i: (0, 0)),
            pl.BlockSpec((1, keys), lambda i: (0, 0)),
            pl.BlockSpec((width, 1), lambda i: (0, 0)),
        ],
        out_specs=pl.BlockSpec((tile, width + HEAD_DIM), lambda i: (i, 0)),
        out_shape=jax.ShapeDtypeStruct((rows, width + HEAD_DIM), BF16),
        scratch_shapes=[
            pltpu.VMEM((heads, 2 * HEAD_DIM, keys), BF16),
            pltpu.VMEM((heads, keys, 2 * HEAD_DIM), BF16),
        ],
        compiler_params=pltpu.CompilerParams(vmem_limit_bytes=48 << 20),
        cost_estimate=pl.CostEstimate(
            flops=8 * rows * keys * width, bytes_accessed=4 << 20, transcendentals=rows * keys * heads
        ),
    )(limit, queries, keys_values, inverse, gain)


def join_kernel(parts_ref, out_ref, *, heads):
    count = parts_ref.shape[0]
    base = heads * HEAD_DIM
    for h in range(heads):
        tops = [parts_ref[i, :, base + 3 * h : base + 3 * h + 1].astype(F32) for i in range(count)]
        highest = functools.reduce(jnp.maximum, tops)
        total = jnp.zeros(out_ref.shape[:1] + (HEAD_DIM,), F32)
        mass = jnp.zeros_like(highest)
        for i in range(count):
            share = jnp.exp2(tops[i] - highest)
            part = parts_ref[i, :, base + 3 * h + 1 : base + 3 * h + 2].astype(F32)
            part = part + parts_ref[i, :, base + 3 * h + 2 : base + 3 * h + 3].astype(F32)
            mass = mass + share * part
            total = total + share * parts_ref[i, :, h * HEAD_DIM : (h + 1) * HEAD_DIM].astype(F32)
        out_ref[:, h * HEAD_DIM : (h + 1) * HEAD_DIM] = (total * (1.0 / mass)).astype(BF16)


def join(parts, width):
    return pl.pallas_call(
        functools.partial(join_kernel, heads=width // HEAD_DIM),
        out_shape=jax.ShapeDtypeStruct((parts.shape[1], width), BF16),
        compiler_params=pltpu.CompilerParams(vmem_limit_bytes=32 << 20),
    )(parts)


def project_kernel(place_ref, own_ref, zh_ref, core_ref, both_ref, weight_ref, out_ref):
    rows = out_ref.shape[1]
    core, zh = place_ref[0], place_ref[1]
    for r in range(2):
        total = jnp.zeros((rows, weight_ref.shape[2]), F32)
        for ref, a, b in (
            (own_ref, core, zh),
            (zh_ref, core, 1 - zh),
            (core_ref, 1 - core, zh),
            (both_ref, 1 - core, 1 - zh),
        ):
            block = weight_ref[a * 4 + b * 2 + r, 0]
            total = total + lax.dot_general(
                ref[...], block, (((1,), (1,)), ((), ())), preferred_element_type=F32
            )
        out_ref[0, :, r * weight_ref.shape[2] : (r + 1) * weight_ref.shape[2]] = total.astype(BF16)


def project(place, pieces, weights):
    rows, width = pieces[0].shape
    blocks, groups, columns, _ = weights.shape
    whole = pl.BlockSpec((rows, width), lambda i: (0, 0))
    return pl.pallas_call(
        project_kernel,
        grid=(groups,),
        in_specs=[pl.BlockSpec(memory_space=pltpu.SMEM)]
        + [whole] * 4
        + [pl.BlockSpec((blocks, 1, columns, width), lambda i: (0, i, 0, 0))],
        out_specs=pl.BlockSpec((1, rows, 2 * columns), lambda i: (i, 0, 0)),
        out_shape=jax.ShapeDtypeStruct((groups, rows, 2 * columns), BF16),
        compiler_params=pltpu.CompilerParams(vmem_limit_bytes=32 << 20),
    )(place, *pieces, weights)


def weight_routes():
    routes = []
    for zl in range(8):
        c, z, r = zl // 4, zl // 2 % 2, zl % 2
        for a in range(2):
            for b in range(2):
                routes.append(((zl * 2 + a) * 2 + b, ((a * 4 + b * 2 + r) * 2 + c) * 2 + z))
    return routes


def local(queries, keys, values, out_weight, q_gain, k_gain, gate, valid_count):
    rows, width = queries.shape
    features = width * 16
    gathered = lax.all_gather(jnp.concatenate([keys, values], axis=1), "zl", axis=0, tiled=True)
    weights = lax.ppermute(out_weight.T, ("zl", "core", "zh"), weight_routes())

    squares = jnp.stack(
        [
            jnp.sum(jnp.square(queries.astype(F32)), axis=1),
            jnp.sum(jnp.square(keys.astype(F32)), axis=1),
        ]
    )
    near = lax.all_to_all(
        jnp.broadcast_to(squares[None], (8, 2, rows)), ("y", "core"), 0, 0, tiled=True
    )
    near = jnp.sum(near, axis=0)
    spread = lax.all_to_all(
        jnp.broadcast_to(near[None], (16, 2, rows)), ("zl", "zh"), 0, 0, tiled=True
    )
    totals = jnp.sum(spread.reshape(8, 2, 2, rows), axis=1)
    inverse = lax.rsqrt(totals / features + EPSILON)
    key_inverse = inverse[:, 1].reshape(1, 8 * rows)
    query_inverse = lax.dynamic_index_in_dim(inverse, lax.axis_index("zl"), keepdims=False)[0]
    query_norm = (queries.astype(F32) * query_inverse[:, None] * q_gain[None, :]).astype(BF16)
    query_all = lax.all_gather(query_norm, "x", axis=0, tiled=True)
    weights = lax.all_gather(weights, "x", axis=0, tiled=False)
    weights = lax.all_gather(weights, "zl", axis=0, tiled=False)

    limit = valid_count - lax.axis_index("x") * (8 * rows)
    parts = attention(limit, query_all, gathered, key_inverse, k_gain[:, None])
    parts = lax.all_to_all(parts.reshape(4, rows, width + HEAD_DIM), "x", 0, 0, tiled=True)
    own = join(parts, width)
    across = lax.ppermute(own, "zh", SWAP)
    beside = lax.ppermute(own, "core", SWAP)
    both = lax.ppermute(across, "core", SWAP)
    place = jnp.stack([lax.axis_index("core"), lax.axis_index("zh")]).astype(jnp.int32)
    terms = project(place, (own, across, beside, both), weights)
    terms = lax.all_to_all(terms, "y", 0, 0, tiled=True)
    summed = jnp.sum(terms.astype(F32), axis=0)
    return (gate[None, :] * summed).astype(BF16)


def solution(mesh):
    fine = Mesh(mesh.devices.reshape(SIZES), AXES)
    tokens, features = ("x", "zl"), ("y", "core", "zh")
    placed = (
        P(tokens, features),
        P(tokens, features),
        P(tokens, features),
        P(features, tokens),
        P(features),
        P(features),
        P(features),
        P(),
    )
    return jax.shard_map(
        local, mesh=fine, in_specs=placed, out_specs=P(tokens, features), check_vma=False
    )
```

time: 959 us -> 209 us (0.22)
  waiting for transfers between devices: 760 us -> 55.3 us
  local copies, waits for them, and re-layouts: 46.8 us -> 5.07 us
  starting transfers between devices: 0.12 us -> 33.5 us
  other arithmetic: 25.5 us -> 5.04 us
  matrix products: 20.2 us -> 0 us
  Pallas kernels: 0 us -> 17.7 us
  loops' own time: 14.1 us -> 0 us
    all_gather x3 -> x2, waiting for transfers between devices: 593 us -> 25.6 us  [the longest x1 25.6 us: local(): weights = lax.all_gather(weights, 'zl', axis=0, tiled=False)]
    unnamed x5 -> x2, waiting for transfers between devices: 167 us -> 0.03 us
    psum x1 -> x0, blocking collectives: 78 us -> none  [local(): lax.psum((query_squares, key_squares), ('head', 'enc'))]
    all_to_all x0 -> x3, blocking collectives: none -> 48.5 us  [the longest x1 18.3 us: local(): terms = lax.all_to_all(terms, 'y', 0, 0, tiled=True)]
    dynamic_slice x40 -> x0, local copies, waits for them, and re-layouts: 39.7 us -> none  [absorb_blocks(): lax.scan(absorb_block, carried, (numbers, key_blocks, value_blocks))]
    all_gather x0 -> x2, blocking collectives: none -> 29.1 us  [the longest x1 15.7 us: local(): weights = lax.all_gather(weights, 'x', axis=0, tiled=False)]
    all_to_all x0 -> x1, starting transfers between devices: none -> 21.2 us  [local(): lax.all_to_all(jnp.broadcast_to(near[None], (16, 2, rows)), ('zl', 'zh'),...]
    dot_general x41 -> x0, matrix products: 20.2 us -> none  [the longest x20 8.81 us: absorb(): jnp.einsum('qhd,khd->hqk', query_heads, key_block, preferred_element_type...]
  transfers between devices with their start and end apart: 4 -> 7, of which waited for: 4 -> 3; matrix products, arithmetic and copies ran while one was open for 8% -> 2% of each run, Pallas kernels for 0% -> 7%
where the time goes in v1:
time: 209 us; the launch traced here: 208 us
  blocking collectives  77.6 us (37%)
  waiting for transfers between devices  55.3 us (26%)
  starting transfers between devices  33.5 us (16%)
  Pallas kernels  17.7 us (8%)
  between operations  14.2 us (7%)
  local copies, waits for them, and re-layouts  5.07 us (2%)
  other arithmetic  5.04 us (2%)
    all_gather x1, waiting for transfers between devices, local(): weights = lax.all_gather(weights, 'zl', axis=0, tiled=False)  25.6 us
    all_to_all x1, starting transfers between devices, local(): lax.all_to_all(jnp.broadcast_to(near[None], (16, 2, rows)), ('zl', 'zh'),...  21.2 us
    all_to_all x1, blocking collectives, local(): terms = lax.all_to_all(terms, 'y', 0, 0, tiled=True)  18.3 us
    ppermute x1, waiting for transfers between devices, local(): across = lax.ppermute(own, 'zh', SWAP)  17.5 us
    all_to_all x1, blocking collectives, local(): lax.all_to_all(parts.reshape(4, rows, width + HEAD_DIM), 'x', 0, 0, tiled...  16.5 us
    all_gather x1, blocking collectives, local(): weights = lax.all_gather(weights, 'x', axis=0, tiled=False)  15.7 us
    all_to_all x1, blocking collectives, local(): lax.all_to_all(jnp.broadcast_to(squares[None], (8, 2, rows)), ('y', 'core...  13.7 us
    all_gather x1, blocking collectives, local(): query_all = lax.all_gather(query_norm, 'x', axis=0, tiled=True)  13.4 us
  transfers between devices with their start and end apart: 7, of which 3 were waited for; matrix products, arithmetic and copies ran while one was open for 2% of the time, Pallas kernels for 7%

profile of v1, /device:TPU:6, one launch (start us, length us, event | category | flops | bytes accessed | tf_op | source)
XLA Modules:
  0.0 208.4 jit_solution(10526405090444712149)
XLA Ops:
  6.5 0.0 copy-start.2
  6.5 0.0 copy-start.4
  6.5 0.0 all-gather.5.cloned.1.call-start
  6.5 1.8 pad_maximum_fusion
  8.3 0.0 all-gather.5.cloned.1.call-update
  8.3 0.0 all-gather.7.cloned.1.call-start
  8.4 1.5 collective-permute-start.3
  9.9 0.0 collective-permute-done.3
  9.9 15.7 %all-gather = bf16[640,256]{1,0:T(8,128)(2,1)} all-gather(bf16[160,256]{1,0:T(8,128)(2,1)S(1)} %collective-permute-done.3), channel_id=2, replica_groups=mesh['x'=4,'zl'=8,'y'=4,'core'=2,'zh'=2] {'x'}, dimensions={0}, use_global_device_ids=true | all-gather | bytes 409600 | tf_op jit(solution)/shard_map/all_gather | solution.py:181
  25.7 0.0 all-gather.7.cloned.1.call-update
  25.7 1.1 fusion
  26.8 1.1 multiply_reduce_fusion
  27.9 13.7 %all_to_all.20 = f32[8,2,320]{2,1,0:T(2,128)S(1)} all-to-all(f32[8,2,320]{2,1,0:T(2,128)S(1)} %broadcast_in_dim.6), channel_id=1, replica_groups=mesh['x'=4,'zl'=8,'y'=4,'core'=2,'zh'=2] {'y','core'}, dimensions={0} | all-to-all | bytes 40960 | tf_op jit(solution)/shard_map/all_to_all | solution.py:168
  41.7 0.6 broadcast_in_dim.7
  42.3 21.2 %all-to-all-start.1 = ((f32[16,2,320]{2,1,0:T(2,128)}), f32[16,2,320]{2,1,0:T(2,128)S(1)}, u32[]{:S(2)}, u32[]{:S(2)}) async-start(f32[16,2,320]{2,1,0:T(2,128)} %broadcast_in_dim.7), calls=%async_computation.1 | async-start | bytes 98304 | tf_op jit(solution)/shard_map/all_to_all | solution.py:172
  64.1 0.8 copy.16.gain_ref
  65.0 12.1 %all-to-all-done.1 = f32[16,2,320]{2,1,0:T(2,128)S(1)} async-done(((f32[16,2,320]{2,1,0:T(2,128)}), f32[16,2,320]{2,1,0:T(2,128)S(1)}, u32[]{:S(2)}, u32[]{:S(2)}) %all-to-all-start.1) | async-done | bytes 40992 | tf_op jit(solution)/shard_map/all_to_all | solution.py:172
  77.1 0.1 reshape_squeeze.3.inverse_ref
  77.2 0.0 copy-done.2
  77.2 0.0 copy-done.4
  77.2 0.1 fusion.2
  77.3 13.4 %all_gather.18.q_ref = bf16[1280,256]{1,0:T(8,128)(2,1)S(1)} all-gather(bf16[320,256]{1,0:T(8,128)(2,1)S(1)} %fusion.2), channel_id=1, replica_groups=mesh['x'=4,'zl'=8,'y'=4,'core'=2,'zh'=2] {'x'}, dimensions={0}, use_global_device_ids=true | all-gather | bytes 819200 | tf_op jit(solution)/shard_map/all_gather | solution.py:180
  90.7 0.0 all-gather.5.cloned.1.call-done.kv_ref
  90.7 0.0 copy-start.1
  90.7 1.7 copy-done.1
  92.5 13.2 %shard_map.82 = bf16[1280,384]{1,0:T(8,128)(2,1)S(1)} custom-call(s32[1]{0:T(128)S(6)} %sub.7.limit_ref, bf16[1280,256]{1,0:T(8,128)(2,1)S(1)} %all_gather.18.q_ref, bf16[2560,512]{1,0:T(8,128)(2,1)S(1)} %copy-done.1, f32[1,2560]{1,0:T(1,128)S(1)} %reshape_squeeze.3.inverse_ref, f32[256,1]{1,0:T(8,128)S(1)} %copy.16.gain_ref), custom_call_target="tpu_custom_call" | custom-call | flops 6710886400 | bytes 4194304 | tf_op jit(solution)/shard_map/pallas_call | solution.py:64
  105.7 16.5 %all_to_all.21.parts_ref = bf16[4,320,384]{2,1,0:T(8,128)(2,1)S(1)} all-to-all(bf16[4,320,384]{2,1,0:T(8,128)(2,1)S(1)} %bitcast.13), channel_id=1, replica_groups=mesh['x'=4,'zl'=8,'y'=4,'core'=2,'zh'=2] {'x'}, dimensions={0} | all-to-all | bytes 1966080 | tf_op jit(solution)/shard_map/all_to_all | solution.py:186
  122.2 1.4 shard_map.83.own_ref
  123.6 6.9 %collective-permute-start = (bf16[320,256]{1,0:T(8,128)(2,1)S(1)}, bf16[320,256]{1,0:T(8,128)(2,1)S(1)}, u32[]{:S(2)}, u32[]{:S(2)}) collective-permute-start(bf16[320,256]{1,0:T(8,128)(2,1)S(1)} %shard_map.83.own_ref), channel_id=1, source_target_pairs={{0,1},{1,0},{2,3},{3,2},{4,5},{5,4},{6,7},{7,6},{8,9},{9,8},{10,11... | collective-permute-start | bytes 491528 | tf_op jit(solution)/shard_map/ppermute | solution.py:188
  130.5 1.9 collective-permute-start.1
  132.4 17.5 %collective-permute-done.zh_ref = bf16[320,256]{1,0:T(8,128)(2,1)S(1)} collective-permute-done((bf16[320,256]{1,0:T(8,128)(2,1)S(1)}, bf16[320,256]{1,0:T(8,128)(2,1)S(1)}, u32[]{:S(2)}, u32[]{:S(2)}) %collective-permute-start) | collective-permute-done | bytes 163872 | tf_op jit(solution)/shard_map/ppermute | solution.py:188
  149.9 1.9 collective-permute-start.2
  151.9 0.1 pad_add_fusion.place_ref
  151.9 25.6 %all-gather.7.cloned.1.call-done = bf16[32,160,256]{2,1,0:T(8,128)(2,1)} async-done(((bf16[4,160,256]{2,1,0:T(8,128)(2,1)}), bf16[32,160,256]{2,1,0:T(8,128)(2,1)}) %all-gather.7.cloned.1.call-update) | async-done | bytes 2621456 | tf_op jit(solution)/shard_map/all_gather | solution.py:182
  177.5 0.0 collective-permute-done.1.core_ref
  177.5 0.0 collective-permute-done.2.both_ref
  177.6 0.0 copy-start
  177.6 1.7 copy-done
  179.3 3.1 %shard_map.84 = bf16[4,320,320]{2,1,0:T(8,128)(2,1)S(1)} custom-call(s32[2]{0:T(128)S(1)} %pad_add_fusion.place_ref, bf16[320,256]{1,0:T(8,128)(2,1)S(1)} %shard_map.83.own_ref, bf16[320,256]{1,0:T(8,128)(2,1)S(1)} %collective-permute-done.zh_ref, bf16[320,256]{1,0:T(8,128)(2,1)S(1)} %collective-permute-done.1.core_ref, ...), custom_call_target="tpu_custom_call" | custom-call | tf_op jit(solution)/shard_map/pallas_call | solution.py:134
  182.4 0.0 copy-start.3
  182.4 18.3 %all_to_all.22 = bf16[4,320,320]{2,1,0:T(8,128)(2,1)S(1)} all-to-all(bf16[4,320,320]{2,1,0:T(8,128)(2,1)S(1)} %shard_map.84), channel_id=1, replica_groups=mesh['x'=4,'zl'=8,'y'=4,'core'=2,'zh'=2] {'y'}, dimensions={0} | all-to-all | bytes 1638400 | tf_op jit(solution)/shard_map/all_to_all | solution.py:193
  200.7 0.2 convert_reduce_fusion
  200.8 0.0 copy-done.3
  200.8 0.7 multiply_convert_fusion
  (9 shorter events, 0.1 us)
Async XLA Ops:
  6.5 70.7 %copy-start.2 = (bf16[320,256]{1,0:T(8,128)(2,1)S(1)}, bf16[320,256]{1,0:T(8,128)(2,1)}, u32[]{:S(2)}) copy-start(bf16[320,256]{1,0:T(8,128)(2,1)} %param.8) | copy-start | bytes 491524
  6.5 70.7 %copy-start.4 = (f32[256]{0:T(256)S(1)}, f32[256]{0:T(256)}, u32[]{:S(2)}) copy-start(f32[256]{0:T(256)} %param.12) | copy-start | bytes 3076
  6.5 84.2 %all-gather.5.cloned.1.call-start = ((), (), s32[]{:S(2)}) async-start(), calls=%async_computation.4 | async-start | bytes 2949120 | tf_op jit(solution)/shard_map/all_gather | solution.py:159
  8.3 169.2 %all-gather.7.cloned.1.call-start = ((), (), s32[]{:S(2)}) async-start(), calls=%async_computation.5 | async-start | bytes 2949120 | tf_op jit(solution)/shard_map/all_gather | solution.py:182
  8.4 1.6 collective-permute-start.3
  42.3 34.7 %all-to-all-start.1 = ((f32[16,2,320]{2,1,0:T(2,128)}), f32[16,2,320]{2,1,0:T(2,128)S(1)}, u32[]{:S(2)}, u32[]{:S(2)}) async-start(f32[16,2,320]{2,1,0:T(2,128)} %broadcast_in_dim.7), calls=%async_computation.1 | async-start | bytes 98304 | tf_op jit(solution)/shard_map/all_to_all | solution.py:172
  90.7 1.7 copy-start.1
  123.6 26.4 %collective-permute-start = (bf16[320,256]{1,0:T(8,128)(2,1)S(1)}, bf16[320,256]{1,0:T(8,128)(2,1)S(1)}, u32[]{:S(2)}, u32[]{:S(2)}) collective-permute-start(bf16[320,256]{1,0:T(8,128)(2,1)S(1)} %shard_map.83.own_ref), channel_id=1, source_target_pairs={{0,1},{1,0},{2,3},{3,2},{4,5},{5,4},{6,7},{7,6},{8,9},{9,8},{10,11... | collective-permute-start | bytes 491528 | tf_op jit(solution)/shard_map/ppermute | solution.py:188
  130.5 47.1 %collective-permute-start.1 = (bf16[320,256]{1,0:T(8,128)(2,1)S(1)}, bf16[320,256]{1,0:T(8,128)(2,1)S(1)}, u32[]{:S(2)}, u32[]{:S(2)}) collective-permute-start(bf16[320,256]{1,0:T(8,128)(2,1)S(1)} %shard_map.83.own_ref), channel_id=1, source_target_pairs={{0,2},{2,0},{1,3},{3,1},{4,6},{6,4},{5,7},{7,5},{8,10},{10,8},{9,1... | collective-permute-start | bytes 491528 | tf_op jit(solution)/shard_map/ppermute | solution.py:189
  149.9 27.6 %collective-permute-start.2 = (bf16[320,256]{1,0:T(8,128)(2,1)S(1)}, bf16[320,256]{1,0:T(8,128)(2,1)S(1)}, u32[]{:S(2)}, u32[]{:S(2)}) collective-permute-start(bf16[320,256]{1,0:T(8,128)(2,1)S(1)} %collective-permute-done.zh_ref), channel_id=1, source_target_pairs={{0,2},{2,0},{1,3},{3,1},{4,6},{6,4},{5,7},{7,5},{8,10},{10,8},{9,1... | collective-permute-start | bytes 491528 | tf_op jit(solution)/shard_map/ppermute | solution.py:190
  177.6 1.7 copy-start
  182.4 18.4 %copy-start.3 = (f32[320]{0:T(512)S(1)}, f32[320]{0:T(512)}, u32[]{:S(2)}) copy-start(f32[320]{0:T(512)} %param.14) | copy-start | bytes 3844
Sparse Core Ops, SparseCore 0:
  9.4 81.0 all-gather.4
  92.6 84.9 all-gather.6

commit v2 on v1

--- a/solution.py
+++ b/solution.py
@@ -3,6 +3,7 @@
 
 import jax
 import jax.numpy as jnp
+import numpy as np
 from jax import lax
 from jax.experimental import pallas as pl
 from jax.experimental.pallas import tpu as pltpu
@@ -17,19 +18,19 @@
 AXES = ("x", "zl", "y", "core", "zh")
 SIZES = (4, 8, 4, 2, 2)
 SWAP = ((0, 1), (1, 0))
+RING = [0, 2, 4, 6, 7, 5, 3, 1]
 
 
 def attention_kernel(
-    limit_ref, q_ref, kv_ref, inverse_ref, gain_ref, out_ref, kt_ref, ve_ref, *, heads, keys
+    q_ref, kv_ref, inverse_ref, bias_ref, gain_ref, out_ref, kt_ref, ve_ref, *, heads, keys
 ):
-    tile = q_ref.shape[0]
+    tile = q_ref.shape[1]
     factor = HEAD_DIM**-0.5 * math.log2(math.e)
 
     @pl.when(pl.program_id(0) == 0)
     def _():
-        position = lax.broadcasted_iota(jnp.int32, (HEAD_DIM, keys), 1)
         row = lax.broadcasted_iota(jnp.int32, (HEAD_DIM, keys), 0)
-        bias = jnp.where((position >= limit_ref[0]) & (row == 0), BIAS, 0.0).astype(BF16)
+        bias = jnp.where(row == 0, bias_ref[...], 0.0).astype(BF16)
         for h in range(heads):
             columns = slice(h * HEAD_DIM, (h + 1) * HEAD_DIM)
             raw = kv_ref[:, columns].T.astype(F32)
@@ -42,46 +43,47 @@
     first = jnp.where(lane == 0, 1.0, 0.0).astype(BF16)
     stats = jnp.zeros((tile, HEAD_DIM), F32)
     for h in range(heads):
-        query = jnp.concatenate([q_ref[:, h * HEAD_DIM : (h + 1) * HEAD_DIM], first], axis=1)
+        query = jnp.concatenate([q_ref[0, :, h * HEAD_DIM : (h + 1) * HEAD_DIM], first], axis=1)
         scores = jnp.dot(query, kt_ref[h], preferred_element_type=F32)
         top = (jnp.max(scores, axis=1, keepdims=True) * factor).astype(BF16).astype(F32)
         weights = jnp.exp2(scores * factor - top).astype(BF16)
         summed = jnp.dot(weights, ve_ref[h], preferred_element_type=F32)
-        out_ref[:, h * HEAD_DIM : (h + 1) * HEAD_DIM] = summed[:, :HEAD_DIM].astype(BF16)
+        out_ref[0, :, h * HEAD_DIM : (h + 1) * HEAD_DIM] = summed[:, :HEAD_DIM].astype(BF16)
         mass = summed[:, HEAD_DIM:]
         high = mass.astype(BF16).astype(F32)
         stats = jnp.where(lane == 3 * h, top, stats)
         stats = jnp.where(lane == 3 * h + 1, high, stats)
         stats = jnp.where(lane == 3 * h + 2, mass - high, stats)
-    out_ref[:, heads * HEAD_DIM :] = stats.astype(BF16)
-
-
-def attention(limit, queries, keys_values, inverse, gain):
-    rows, width = queries.shape
+    out_ref[0, :, heads * HEAD_DIM :] = stats.astype(BF16)
+
+
+def attention(queries, keys_values, inverse, bias, gain, rows):
+    blocks, _, width = queries.shape
     keys = keys_values.shape[0]
     heads = width // HEAD_DIM
-    tile = 256
     return pl.pallas_call(
         functools.partial(attention_kernel, heads=heads, keys=keys),
-        grid=(rows // tile,),
+        grid=(blocks,),
         in_specs=[
-            pl.BlockSpec(memory_space=pltpu.SMEM),
-            pl.BlockSpec((tile, width), lambda i: (i, 0)),
+            pl.BlockSpec((1, rows, width), lambda i: (i, 0, 0)),
             pl.BlockSpec((keys, 2 * width), lambda i: (0, 0)),
+            pl.BlockSpec((1, keys), lambda i: (0, 0)),
             pl.BlockSpec((1, keys), lambda i: (0, 0)),
             pl.BlockSpec((width, 1), lambda i: (0, 0)),
         ],
-        out_specs=pl.BlockSpec((tile, width + HEAD_DIM), lambda i: (i, 0)),
-        out_shape=jax.ShapeDtypeStruct((rows, width + HEAD_DIM), BF16),
+        out_specs=pl.BlockSpec((1, rows, width + HEAD_DIM), lambda i: (i, 0, 0)),
+        out_shape=jax.ShapeDtypeStruct((blocks, rows, width + HEAD_DIM), BF16),
         scratch_shapes=[
             pltpu.VMEM((heads, 2 * HEAD_DIM, keys), BF16),
             pltpu.VMEM((heads, keys, 2 * HEAD_DIM), BF16),
         ],
         compiler_params=pltpu.CompilerParams(vmem_limit_bytes=48 << 20),
         cost_estimate=pl.CostEstimate(
-            flops=8 * rows * keys * width, bytes_accessed=4 << 20, transcendentals=rows * keys * heads
+            flops=8 * blocks * rows * keys * width,
+            bytes_accessed=4 << 20,
+            transcendentals=blocks * rows * keys * heads,
         ),
-    )(limit, queries, keys_values, inverse, gain)
+    )(queries, keys_values, inverse, bias, gain)
 
 
 def join_kernel(parts_ref, out_ref, *, heads):
@@ -120,7 +122,8 @@
             (core_ref, 1 - core, zh),
             (both_ref, 1 - core, 1 - zh),
         ):
-            block = weight_ref[a * 4 + b * 2 + r, 0]
+            pair = a * 2 + b
+            block = weight_ref[pair if r == 0 else 7 - pair, 0]
             total = total + lax.dot_general(
                 ref[...], block, (((1,), (1,)), ((), ())), preferred_element_type=F32
             )
@@ -156,7 +159,9 @@
 def local(queries, keys, values, out_weight, q_gain, k_gain, gate, valid_count):
     rows, width = queries.shape
     features = width * 16
-    gathered = lax.all_gather(jnp.concatenate([keys, values], axis=1), "zl", axis=0, tiled=True)
+    gathered = lax.all_gather(
+        jnp.concatenate([keys, values], axis=1), "zl", axis=0, tiled=True, axis_index_groups=[RING]
+    )
     weights = lax.ppermute(out_weight.T, ("zl", "core", "zh"), weight_routes())
 
     squares = jnp.stack(
@@ -169,21 +174,24 @@
         jnp.broadcast_to(squares[None], (8, 2, rows)), ("y", "core"), 0, 0, tiled=True
     )
     near = jnp.sum(near, axis=0)
-    spread = lax.all_to_all(
-        jnp.broadcast_to(near[None], (16, 2, rows)), ("zl", "zh"), 0, 0, tiled=True
-    )
-    totals = jnp.sum(spread.reshape(8, 2, 2, rows), axis=1)
+    totals = near + lax.ppermute(near, "zh", SWAP)
     inverse = lax.rsqrt(totals / features + EPSILON)
-    key_inverse = inverse[:, 1].reshape(1, 8 * rows)
-    query_inverse = lax.dynamic_index_in_dim(inverse, lax.axis_index("zl"), keepdims=False)[0]
-    query_norm = (queries.astype(F32) * query_inverse[:, None] * q_gain[None, :]).astype(BF16)
-    query_all = lax.all_gather(query_norm, "x", axis=0, tiled=True)
-    weights = lax.all_gather(weights, "x", axis=0, tiled=False)
-    weights = lax.all_gather(weights, "zl", axis=0, tiled=False)
-
-    limit = valid_count - lax.axis_index("x") * (8 * rows)
-    parts = attention(limit, query_all, gathered, key_inverse, k_gain[:, None])
-    parts = lax.all_to_all(parts.reshape(4, rows, width + HEAD_DIM), "x", 0, 0, tiled=True)
+    key_inverse = lax.all_to_all(
+        jnp.broadcast_to(inverse[1][None], (8, rows)), "zl", 0, 0, tiled=True
+    )
+    key_inverse = jnp.concatenate([key_inverse[z] for z in RING])[None, :]
+    query_norm = (queries.astype(F32) * inverse[0][:, None] * q_gain[None, :]).astype(BF16)
+    along_x = lax.all_gather(jnp.concatenate([query_norm, weights]), "x", axis=0, tiled=False)
+    weights = lax.all_gather(
+        along_x[:, rows:], "zl", axis=0, tiled=False, axis_index_groups=[RING]
+    )
+
+    limit = valid_count[0] - lax.axis_index("x") * (8 * rows)
+    starts = np.repeat(np.asarray(RING, np.int32) * rows, rows)
+    position = jnp.asarray(starts + np.tile(np.arange(rows, dtype=np.int32), 8))
+    bias = jnp.where(position < limit, 0.0, BIAS).astype(F32)[None, :]
+    parts = attention(along_x, gathered, key_inverse, bias, k_gain[:, None], rows)
+    parts = lax.all_to_all(parts, "x", 0, 0, tiled=True)
     own = join(parts, width)
     across = lax.ppermute(own, "zh", SWAP)
     beside = lax.ppermute(own, "core", SWAP)

time: 209 us -> 203 us (0.971)
  blocking collectives: 77.6 us -> 57.5 us
  starting transfers between devices: 33.5 us -> 53.5 us
  waiting for transfers between devices: 55.3 us -> 47.5 us
    ppermute x0 -> x1, starting transfers between devices: none -> 15.7 us  [local(): totals = near + lax.ppermute(near, 'zh', SWAP)]
    all_gather x2 -> x1, blocking collectives: 29.1 us -> 13.7 us  [local(): lax.all_gather(jnp.concatenate([query_norm, weights]), 'x', axis=0, tiled...]
    ppermute x1, waiting for transfers between devices: 17.5 us -> 8.89 us  [local(): across = lax.ppermute(own, 'zh', SWAP)]
    ppermute x1, starting transfers between devices: 6.89 us -> 12.1 us  [local(): across = lax.ppermute(own, 'zh', SWAP)]
    all_to_all x1, blocking collectives: 13.7 us -> 9.67 us  [local(): lax.all_to_all(jnp.broadcast_to(squares[None], (8, 2, rows)), ('y', 'core...]
  transfers between devices with their start and end apart: 7 -> 8, of which waited for: 3 -> 5; matrix products, arithmetic and copies ran while one was open for 2% -> 2% of each run, Pallas kernels for 7% -> 7%
where the time goes in v2:
time: 203 us; the launch traced here: 201 us
  blocking collectives  57.5 us (28%)
  starting transfers between devices  53.5 us (26%)
  waiting for transfers between devices  47.5 us (23%)
  Pallas kernels  17.3 us (9%)
  between operations  14.2 us (7%)
  other arithmetic  5.94 us (3%)
  local copies, waits for them, and re-layouts  5.17 us (3%)
    all_gather x1, waiting for transfers between devices, local(): lax.all_gather(along_x[:, rows:], 'zl', axis=0, tiled=False, axis_index_g...  26.8 us
    all_to_all x1, starting transfers between devices, local(): lax.all_to_all(jnp.broadcast_to(inverse[1][None], (8, rows)), 'zl', 0, 0,...  20.3 us
    all_to_all x1, blocking collectives, local(): terms = lax.all_to_all(terms, 'y', 0, 0, tiled=True)  18.3 us
    all_to_all x1, blocking collectives, local(): parts = lax.all_to_all(parts, 'x', 0, 0, tiled=True)  15.9 us
    ppermute x1, starting transfers between devices, local(): totals = near + lax.ppermute(near, 'zh', SWAP)  15.7 us
    all_gather x1, blocking collectives, local(): lax.all_gather(jnp.concatenate([query_norm, weights]), 'x', axis=0, tiled...  13.7 us
    pallas_call x1, Pallas kernels, attention(): pl.pallas_call(functools.partial(attention_kernel, heads=heads, keys=keys...  12.8 us
    ppermute x1, starting transfers between devices, local(): across = lax.ppermute(own, 'zh', SWAP)  12.1 us
  transfers between devices with their start and end apart: 8, of which 5 were waited for; matrix products, arithmetic and copies ran while one was open for 2% of the time, Pallas kernels for 7%

profile of v2, /device:TPU:6, one launch (start us, length us, event | category | flops | bytes accessed | tf_op | source)
XLA Modules:
  0.0 201.2 jit_solution(9772104729562411598)
XLA Ops:
  6.5 0.0 copy-start.2
  6.5 0.0 copy-start.4
  6.5 0.0 all-gather.5.cloned.1.call-start
  6.5 1.8 pad_maximum_fusion
  8.3 0.0 all-gather.5.cloned.1.call-update
  8.3 0.0 all-gather.7.cloned.1.call-start
  8.4 1.1 fusion
  9.5 1.1 multiply_reduce_fusion
  10.6 9.7 %all_to_all.21 = f32[8,2,320]{2,1,0:T(2,128)S(1)} all-to-all(f32[8,2,320]{2,1,0:T(2,128)S(1)} %broadcast_in_dim.30), channel_id=1, replica_groups=mesh['x'=4,'zl'=8,'y'=4,'core'=2,'zh'=2] {'y','core'}, dimensions={0} | all-to-all | bytes 40960 | tf_op jit(solution)/shard_map/all_to_all | solution.py:173
  20.3 15.7 %collective-permute-start = (f32[2,320]{1,0:T(2,128)S(1)}, f32[2,320]{1,0:T(2,128)S(1)}, u32[]{:S(2)}, u32[]{:S(2)}) collective-permute-start(f32[2,320]{1,0:T(2,128)S(1)} %reduce_sum.38), channel_id=1, source_target_pairs={{0,1},{1,0},{2,3},{3,2},{4,5},{5,4},{6,7},{7,6},{8,9},{9,8},{10,11... | collective-permute-start | bytes 7688 | tf_op jit(solution)/shard_map/ppermute | solution.py:177
  36.0 1.5 collective-permute-start.1
  37.5 0.1 collective-permute-done
  37.7 1.0 fusion.2
  38.7 0.0 collective-permute-done.1
  38.7 13.7 %all-gather = bf16[1920,256]{1,0:T(8,128)(2,1)S(1)} all-gather(bf16[480,256]{1,0:T(8,128)(2,1)S(1)} %pad_maximum_fusion.1), channel_id=2, replica_groups=mesh['x'=4,'zl'=8,'y'=4,'core'=2,'zh'=2] {'x'}, dimensions={0}, use_global_device_ids=true | all-gather | bytes 1228800 | tf_op jit(solution)/shard_map/all_gather | solution.py:184
  52.5 0.7 slice.65
  53.2 0.0 all-gather.7.cloned.1.call-update
  53.9 0.6 broadcast_in_dim.31
  54.5 20.3 %all-to-all-start.1 = ((f32[8,1,320]{2,1,0:T(1,128)}), f32[8,1,320]{2,1,0:T(1,128)S(1)}, u32[]{:S(2)}, u32[]{:S(2)}) async-start(f32[8,1,320]{2,1,0:T(1,128)} %broadcast_in_dim.31), calls=%async_computation.1 | async-start | bytes 24576 | tf_op jit(solution)/shard_map/all_to_all | solution.py:179
  74.8 0.0 copy-done.2
  74.9 0.0 copy-done.4
  74.9 0.1 copy.14.gain_ref
  75.0 10.5 %all-to-all-done.1 = f32[8,1,320]{2,1,0:T(1,128)S(1)} async-done(((f32[8,1,320]{2,1,0:T(1,128)}), f32[8,1,320]{2,1,0:T(1,128)S(1)}, u32[]{:S(2)}, u32[]{:S(2)}) %all-to-all-start.1) | async-done | bytes 10272 | tf_op jit(solution)/shard_map/all_to_all | solution.py:179
  85.5 0.1 concatenate.11
  85.6 1.2 all-gather.5.cloned.1.call-done.kv_ref
  86.8 0.0 copy-start.1
  86.8 1.7 copy-done.1
  88.6 12.8 %shard_map.91 = bf16[4,320,384]{2,1,0:T(8,128)(2,1)S(1)} custom-call(bf16[4,480,256]{2,1,0:T(8,128)(2,1)S(1)} %bitcast.10, bf16[2560,512]{1,0:T(8,128)(2,1)S(1)} %copy-done.1, f32[1,2560]{1,0:T(1,128)S(1)} %broadcast_in_dim.32.inverse_ref, f32[1,2560]{1,0:T(1,128)S(1)} %broadcast_in_dim.35.bias_ref, f32[256,1]{1,0:T(8,128)S(1)} %copy.14.gain_ref), custom_call_target="tpu_custom_call" | custom-call | flops 6710886400 | bytes 4194304 | tf_op jit(solution)/shard_map/pallas_call | solution.py:64
  101.4 15.9 %all_to_all.22.parts_ref = bf16[4,320,384]{2,1,0:T(8,128)(2,1)S(1)} all-to-all(bf16[4,320,384]{2,1,0:T(8,128)(2,1)S(1)} %shard_map.91), channel_id=1, replica_groups=mesh['x'=4,'zl'=8,'y'=4,'core'=2,'zh'=2] {'x'}, dimensions={0} | all-to-all | bytes 1966080 | tf_op jit(solution)/shard_map/all_to_all | solution.py:194
  117.2 1.4 shard_map.92.own_ref
  118.6 12.1 %collective-permute-start.2 = (bf16[320,256]{1,0:T(8,128)(2,1)S(1)}, bf16[320,256]{1,0:T(8,128)(2,1)S(1)}, u32[]{:S(2)}, u32[]{:S(2)}) collective-permute-start(bf16[320,256]{1,0:T(8,128)(2,1)S(1)} %shard_map.92.own_ref), channel_id=1, source_target_pairs={{0,1},{1,0},{2,3},{3,2},{4,5},{5,4},{6,7},{7,6},{8,9},{9,8},{10,11... | collective-permute-start | bytes 491528 | tf_op jit(solution)/shard_map/ppermute | solution.py:196
  130.7 1.9 collective-permute-start.3
  132.6 8.9 %collective-permute-done.2.zh_ref = bf16[320,256]{1,0:T(8,128)(2,1)S(1)} collective-permute-done((bf16[320,256]{1,0:T(8,128)(2,1)S(1)}, bf16[320,256]{1,0:T(8,128)(2,1)S(1)}, u32[]{:S(2)}, u32[]{:S(2)}) %collective-permute-start.2) | collective-permute-done | bytes 163872 | tf_op jit(solution)/shard_map/ppermute | solution.py:196
  141.5 1.9 collective-permute-start.4
  143.4 0.1 pad_add_fusion.place_ref
  143.5 26.8 %all-gather.7.cloned.1.call-done = bf16[32,160,256]{2,1,0:T(8,128)(2,1)} async-done(((bf16[4,160,256]{2,1,0:T(8,128)(2,1)}), bf16[32,160,256]{2,1,0:T(8,128)(2,1)}) %all-gather.7.cloned.1.call-update) | async-done | bytes 2621456 | tf_op jit(solution)/shard_map/all_gather | solution.py:185
  170.3 0.0 collective-permute-done.3.core_ref
  170.3 0.0 collective-permute-done.4.both_ref
  170.3 0.0 copy-start
  170.3 1.7 copy-done
  172.1 3.1 %shard_map.93 = bf16[4,320,320]{2,1,0:T(8,128)(2,1)S(1)} custom-call(s32[2]{0:T(128)S(1)} %pad_add_fusion.place_ref, bf16[320,256]{1,0:T(8,128)(2,1)S(1)} %shard_map.92.own_ref, bf16[320,256]{1,0:T(8,128)(2,1)S(1)} %collective-permute-done.2.zh_ref, bf16[320,256]{1,0:T(8,128)(2,1)S(1)} %collective-permute-done.3.core_ref, ...), custom_call_target="tpu_custom_call" | custom-call | tf_op jit(solution)/shard_map/pallas_call | solution.py:137
  175.2 0.0 copy-start.3
  175.2 18.3 %all_to_all.23 = bf16[4,320,320]{2,1,0:T(8,128)(2,1)S(1)} all-to-all(bf16[4,320,320]{2,1,0:T(8,128)(2,1)S(1)} %shard_map.93), channel_id=1, replica_groups=mesh['x'=4,'zl'=8,'y'=4,'core'=2,'zh'=2] {'y'}, dimensions={0} | all-to-all | bytes 1638400 | tf_op jit(solution)/shard_map/all_to_all | solution.py:201
  193.5 0.2 convert_reduce_fusion
  193.6 0.0 copy-done.3
  193.6 0.7 multiply_convert_fusion
  (12 shorter events, 0.2 us)
Async XLA Ops:
  6.5 68.3 %copy-start.2 = (s32[2560]{0:T(1024)S(1)}, s32[2560]{0:T(1024)}, u32[]{:S(2)}) copy-start(s32[2560]{0:T(1024)} %constant.25.clone) | copy-start | bytes 30724
  6.5 68.3 %copy-start.4 = (f32[256]{0:T(256)S(1)}, f32[256]{0:T(256)}, u32[]{:S(2)}) copy-start(f32[256]{0:T(256)} %param.14) | copy-start | bytes 3076
  6.5 80.3 %all-gather.5.cloned.1.call-start = ((), (), s32[]{:S(2)}) async-start(), calls=%async_computation.4 | async-start | bytes 2949120 | tf_op jit(solution)/shard_map/all_gather | solution.py:162
  8.3 162.0 %all-gather.7.cloned.1.call-start = ((), (), s32[]{:S(2)}) async-start(), calls=%async_computation.5 | async-start | bytes 2949120 | tf_op jit(solution)/shard_map/all_gather | solution.py:185
  20.3 17.4 %collective-permute-start = (f32[2,320]{1,0:T(2,128)S(1)}, f32[2,320]{1,0:T(2,128)S(1)}, u32[]{:S(2)}, u32[]{:S(2)}) collective-permute-start(f32[2,320]{1,0:T(2,128)S(1)} %reduce_sum.38), channel_id=1, source_target_pairs={{0,1},{1,0},{2,3},{3,2},{4,5},{5,4},{6,7},{7,6},{8,9},{9,8},{10,11... | collective-permute-start | bytes 7688 | tf_op jit(solution)/shard_map/ppermute | solution.py:177
  36.0 2.7 %collective-permute-start.1 = (bf16[160,256]{1,0:T(8,128)(2,1)}, bf16[160,256]{1,0:T(8,128)(2,1)S(1)}, u32[]{:S(2)}, u32[]{:S(2)}) collective-permute-start(bf16[160,256]{1,0:T(8,128)(2,1)} %bitcast.12), channel_id=1, source_target_pairs={{0,0},{1,32},{2,64},{3,96},{16,16},{17,48},{18,80},{19,112},{32,1}... | collective-permute-start | bytes 245768 | tf_op jit(solution)/shard_map/ppermute | solution.py:165
  54.5 31.0 %all-to-all-start.1 = ((f32[8,1,320]{2,1,0:T(1,128)}), f32[8,1,320]{2,1,0:T(1,128)S(1)}, u32[]{:S(2)}, u32[]{:S(2)}) async-start(f32[8,1,320]{2,1,0:T(1,128)} %broadcast_in_dim.31), calls=%async_computation.1 | async-start | bytes 24576 | tf_op jit(solution)/shard_map/all_to_all | solution.py:179
  86.8 1.7 copy-start.1
  118.6 22.9 %collective-permute-start.2 = (bf16[320,256]{1,0:T(8,128)(2,1)S(1)}, bf16[320,256]{1,0:T(8,128)(2,1)S(1)}, u32[]{:S(2)}, u32[]{:S(2)}) collective-permute-start(bf16[320,256]{1,0:T(8,128)(2,1)S(1)} %shard_map.92.own_ref), channel_id=1, source_target_pairs={{0,1},{1,0},{2,3},{3,2},{4,5},{5,4},{6,7},{7,6},{8,9},{9,8},{10,11... | collective-permute-start | bytes 491528 | tf_op jit(solution)/shard_map/ppermute | solution.py:196
  130.7 39.6 %collective-permute-start.3 = (bf16[320,256]{1,0:T(8,128)(2,1)S(1)}, bf16[320,256]{1,0:T(8,128)(2,1)S(1)}, u32[]{:S(2)}, u32[]{:S(2)}) collective-permute-start(bf16[320,256]{1,0:T(8,128)(2,1)S(1)} %shard_map.92.own_ref), channel_id=1, source_target_pairs={{0,2},{2,0},{1,3},{3,1},{4,6},{6,4},{5,7},{7,5},{8,10},{10,8},{9,1... | collective-permute-start | bytes 491528 | tf_op jit(solution)/shard_map/ppermute | solution.py:197
  141.5 28.8 %collective-permute-start.4 = (bf16[320,256]{1,0:T(8,128)(2,1)S(1)}, bf16[320,256]{1,0:T(8,128)(2,1)S(1)}, u32[]{:S(2)}, u32[]{:S(2)}) collective-permute-start(bf16[320,256]{1,0:T(8,128)(2,1)S(1)} %collective-permute-done.2.zh_ref), channel_id=1, source_target_pairs={{0,2},{2,0},{1,3},{3,1},{4,6},{6,4},{5,7},{7,5},{8,10},{10,8},{9,1... | collective-permute-start | bytes 491528 | tf_op jit(solution)/shard_map/ppermute | solution.py:198
  170.3 1.7 copy-start
  175.2 18.5 %copy-start.3 = (f32[320]{0:T(512)S(1)}, f32[320]{0:T(512)}, u32[]{:S(2)}) copy-start(f32[320]{0:T(512)} %param.15) | copy-start | bytes 3844
Sparse Core Ops, SparseCore 0:
  9.4 77.3 all-gather.4
  88.9 81.3 all-gather.6

commit v3 on v2

--- a/solution.py
+++ b/solution.py
@@ -57,8 +57,8 @@
     out_ref[0, :, heads * HEAD_DIM :] = stats.astype(BF16)
 
 
-def attention(queries, keys_values, inverse, bias, gain, rows):
-    blocks, _, width = queries.shape
+def attention(queries, keys_values, inverse, bias, gain):
+    blocks, rows, width = queries.shape
     keys = keys_values.shape[0]
     heads = width // HEAD_DIM
     return pl.pallas_call(
@@ -123,7 +123,7 @@
             (both_ref, 1 - core, 1 - zh),
         ):
             pair = a * 2 + b
-            block = weight_ref[pair if r == 0 else 7 - pair, 0]
+            block = weight_ref[0, pair if r == 0 else 7 - pair]
             total = total + lax.dot_general(
                 ref[...], block, (((1,), (1,)), ((), ())), preferred_element_type=F32
             )
@@ -132,14 +132,14 @@
 
 def project(place, pieces, weights):
     rows, width = pieces[0].shape
-    blocks, groups, columns, _ = weights.shape
+    groups, blocks, columns, _ = weights.shape
     whole = pl.BlockSpec((rows, width), lambda i: (0, 0))
     return pl.pallas_call(
         project_kernel,
         grid=(groups,),
         in_specs=[pl.BlockSpec(memory_space=pltpu.SMEM)]
         + [whole] * 4
-        + [pl.BlockSpec((blocks, 1, columns, width), lambda i: (0, i, 0, 0))],
+        + [pl.BlockSpec((1, blocks, columns, width), lambda i: (i, 0, 0, 0))],
         out_specs=pl.BlockSpec((1, rows, 2 * columns), lambda i: (i, 0, 0)),
         out_shape=jax.ShapeDtypeStruct((groups, rows, 2 * columns), BF16),
         compiler_params=pltpu.CompilerParams(vmem_limit_bytes=32 << 20),
@@ -156,6 +156,23 @@
     return routes
 
 
+def pack(factors, width):
+    high = lax.reduce_precision(factors, 8, 7)
+    middle = lax.reduce_precision(factors - high, 8, 7)
+    low = factors - high - middle
+    lines = -(-factors.shape[0] // width)
+    terms = jnp.stack([high, middle, low]).astype(BF16)
+    terms = jnp.pad(terms, ((0, 0), (0, lines * width - factors.shape[0])))
+    return jnp.pad(terms.reshape(3 * lines, width), ((0, 16 - 3 * lines), (0, 0)))
+
+
+def unpack(packed, count):
+    blocks, _, width = packed.shape
+    lines = -(-count // width)
+    terms = packed[:, : 3 * lines].astype(F32).reshape(blocks, 3, lines * width)
+    return (terms[:, 0] + terms[:, 1] + terms[:, 2])[:, :count]
+
+
 def local(queries, keys, values, out_weight, q_gain, k_gain, gate, valid_count):
     rows, width = queries.shape
     features = width * 16
@@ -176,21 +193,19 @@
     near = jnp.sum(near, axis=0)
     totals = near + lax.ppermute(near, "zh", SWAP)
     inverse = lax.rsqrt(totals / features + EPSILON)
-    key_inverse = lax.all_to_all(
-        jnp.broadcast_to(inverse[1][None], (8, rows)), "zl", 0, 0, tiled=True
-    )
-    key_inverse = jnp.concatenate([key_inverse[z] for z in RING])[None, :]
     query_norm = (queries.astype(F32) * inverse[0][:, None] * q_gain[None, :]).astype(BF16)
-    along_x = lax.all_gather(jnp.concatenate([query_norm, weights]), "x", axis=0, tiled=False)
-    weights = lax.all_gather(
-        along_x[:, rows:], "zl", axis=0, tiled=False, axis_index_groups=[RING]
-    )
+    query_all = lax.all_gather(query_norm, "x", axis=0, tiled=False)
+    packed = jnp.concatenate([weights, pack(inverse[1], width)])
+    along_zl = lax.all_gather(packed, "zl", axis=0, tiled=False, axis_index_groups=[RING])
+    columns = weights.shape[0]
+    key_inverse = unpack(along_zl[:, columns:], rows).reshape(1, 8 * rows)
+    weights = lax.all_gather(along_zl[:, :columns], "x", axis=0, tiled=False)
 
     limit = valid_count[0] - lax.axis_index("x") * (8 * rows)
     starts = np.repeat(np.asarray(RING, np.int32) * rows, rows)
     position = jnp.asarray(starts + np.tile(np.arange(rows, dtype=np.int32), 8))
     bias = jnp.where(position < limit, 0.0, BIAS).astype(F32)[None, :]
-    parts = attention(along_x, gathered, key_inverse, bias, k_gain[:, None], rows)
+    parts = attention(query_all, gathered, key_inverse, bias, k_gain[:, None])
     parts = lax.all_to_all(parts, "x", 0, 0, tiled=True)
     own = join(parts, width)
     across = lax.ppermute(own, "zh", SWAP)

time: 203 us -> 204 us (level)
  blocking collectives: 57.5 us -> 122 us
  waiting for transfers between devices: 47.5 us -> 11.8 us
  starting transfers between devices: 53.5 us -> 25.8 us
    all_gather x1 -> x2, blocking collectives: 13.7 us -> 66.5 us  [the longest x1 53.5 us: local(): lax.all_gather(packed, 'zl', axis=0, tiled=False, axis_index_groups=[RING])]
    all_gather x1, waiting for transfers between devices: 26.8 us -> 0.01 us  [local(): weights = lax.all_gather(along_zl[:, :columns], 'x', axis=0, tiled=False)]
    all_to_all x1 -> x0, starting transfers between devices: 20.3 us -> none  [local(): lax.all_to_all(jnp.broadcast_to(inverse[1][None], (8, rows)), 'zl', 0, 0,...]
    all_to_all x1 -> x0, waiting for transfers between devices: 10.5 us -> none  [local(): lax.all_to_all(jnp.broadcast_to(inverse[1][None], (8, rows)), 'zl', 0, 0,...]
    all_to_all x1, blocking collectives: 15.9 us -> 25.8 us  [local(): parts = lax.all_to_all(parts, 'x', 0, 0, tiled=True)]
    ppermute x1, starting transfers between devices: 12.1 us -> 4.62 us  [local(): across = lax.ppermute(own, 'zh', SWAP)]
  transfers between devices with their start and end apart: 8 -> 7, of which waited for: 5 -> 3; matrix products, arithmetic and copies ran while one was open for 2% -> 2% of each run, Pallas kernels for 7% -> 7%
where the time goes in v3:
time: 204 us; the launch traced here: 200 us
  blocking collectives  122 us (60%)
  starting transfers between devices  25.8 us (13%)
  Pallas kernels  17.1 us (8%)
  between operations  14.3 us (7%)
  waiting for transfers between devices  11.8 us (6%)
  other arithmetic  5.15 us (3%)
  local copies, waits for them, and re-layouts  4.72 us (2%)
    all_gather x1, blocking collectives, local(): lax.all_gather(packed, 'zl', axis=0, tiled=False, axis_index_groups=[RING])  53.5 us
    all_to_all x1, blocking collectives, local(): parts = lax.all_to_all(parts, 'x', 0, 0, tiled=True)  25.8 us
    all_to_all x1, blocking collectives, local(): terms = lax.all_to_all(terms, 'y', 0, 0, tiled=True)  19.7 us
    ppermute x1, starting transfers between devices, local(): totals = near + lax.ppermute(near, 'zh', SWAP)  15.7 us
    all_gather x1, blocking collectives, local(): query_all = lax.all_gather(query_norm, 'x', axis=0, tiled=False)  13 us
    pallas_call x1, Pallas kernels, attention(): pl.pallas_call(functools.partial(attention_kernel, heads=heads, keys=keys...  12.8 us
    ppermute x1, waiting for transfers between devices, local(): across = lax.ppermute(own, 'zh', SWAP)  10.3 us
    all_to_all x1, blocking collectives, local(): lax.all_to_all(jnp.broadcast_to(squares[None], (8, 2, rows)), ('y', 'core...  9.67 us
  transfers between devices with their start and end apart: 7, of which 3 were waited for; matrix products, arithmetic and copies ran while one was open for 2% of the time, Pallas kernels for 7%

profile of v3, /device:TPU:6, one launch (start us, length us, event | category | flops | bytes accessed | tf_op | source)
XLA Modules:
  0.0 200.5 jit_solution(15614476048068605223)
XLA Ops:
  6.5 0.0 copy-start.3
  6.5 0.0 copy-start.2
  6.5 0.0 copy-start.5
  6.5 0.0 copy-start.6
  6.5 0.0 all-gather.6.cloned.1.call-start
  6.6 1.8 pad_maximum_fusion
  8.4 0.0 all-gather.6.cloned.1.call-update
  8.4 0.0 all-gather.8.cloned.1.call-start
  8.5 1.1 fusion
  9.6 1.1 multiply_reduce_fusion
  10.7 9.7 %all_to_all.15 = f32[8,2,320]{2,1,0:T(2,128)S(1)} all-to-all(f32[8,2,320]{2,1,0:T(2,128)S(1)} %broadcast_in_dim.22), channel_id=1, replica_groups=mesh['x'=4,'zl'=8,'y'=4,'core'=2,'zh'=2] {'y','core'}, dimensions={0} | all-to-all | bytes 40960 | tf_op jit(solution)/shard_map/all_to_all | solution.py:190
  20.4 15.7 %collective-permute-start = (f32[2,320]{1,0:T(2,128)S(1)}, f32[2,320]{1,0:T(2,128)S(1)}, u32[]{:S(2)}, u32[]{:S(2)}) collective-permute-start(f32[2,320]{1,0:T(2,128)S(1)} %reduce_sum.38), channel_id=1, source_target_pairs={{0,1},{1,0},{2,3},{3,2},{4,5},{5,4},{6,7},{7,6},{8,9},{9,8},{10,11... | collective-permute-start | bytes 7688 | tf_op jit(solution)/shard_map/ppermute | solution.py:194
  36.1 1.5 collective-permute-start.1
  37.6 0.1 collective-permute-done
  37.8 0.0 collective-permute-done.1
  37.9 53.5 %all-gather.1 = bf16[1408,256]{1,0:T(8,128)(2,1)S(1)} all-gather(bf16[176,256]{1,0:T(8,128)(2,1)S(1)} %fusion.4), channel_id=3, replica_groups={{0,32,64,96,112,80,48,16},{1,33,65,97,113,81,49,17},{2,34,66,98,114,82,..., dimensions={0}, use_global_device_ids=true | all-gather | bytes 811008 | tf_op jit(solution)/shard_map/all_gather | solution.py:199
  91.3 0.9 slice.41
  92.2 0.0 all-gather.8.cloned.1.call-update
  92.9 0.0 copy-done.3
  92.9 0.0 copy-done.5
  93.0 0.1 copy.17.gain_ref
  93.1 0.0 copy-done.2
  93.1 0.0 copy-done.6
  93.1 0.1 fusion.2
  93.2 13.0 %all-gather = bf16[1280,256]{1,0:T(8,128)(2,1)S(1)} all-gather(bf16[320,256]{1,0:T(8,128)(2,1)S(1)} %fusion.2), channel_id=2, replica_groups=mesh['x'=4,'zl'=8,'y'=4,'core'=2,'zh'=2] {'x'}, dimensions={0}, use_global_device_ids=true | all-gather | bytes 819200 | tf_op jit(solution)/shard_map/all_gather | solution.py:197
  106.4 0.1 reshape.21.inverse_ref
  106.5 0.0 all-gather.6.cloned.1.call-done.kv_ref
  106.5 0.0 copy-start.1
  106.5 1.7 copy-done.1
  108.2 12.8 %shard_map.91 = bf16[4,320,384]{2,1,0:T(8,128)(2,1)S(1)} custom-call(bf16[4,320,256]{2,1,0:T(8,128)(2,1)S(1)} %bitcast.13, bf16[2560,512]{1,0:T(8,128)(2,1)S(1)} %copy-done.1, f32[1,2560]{1,0:T(1,128)S(1)} %reshape.21.inverse_ref, f32[1,2560]{1,0:T(1,128)S(1)} %broadcast_in_dim.25.bias_ref, f32[256,1]{1,0:T(8,128)S(1)} %copy.17.gain_ref), custom_call_target="tpu_custom_call" | custom-call | flops 6710886400 | bytes 4194304 | tf_op jit(solution)/shard_map/pallas_call | solution.py:64
  121.0 25.8 %all_to_all.16.parts_ref = bf16[4,320,384]{2,1,0:T(8,128)(2,1)S(1)} all-to-all(bf16[4,320,384]{2,1,0:T(8,128)(2,1)S(1)} %shard_map.91), channel_id=1, replica_groups=mesh['x'=4,'zl'=8,'y'=4,'core'=2,'zh'=2] {'x'}, dimensions={0} | all-to-all | bytes 1966080 | tf_op jit(solution)/shard_map/all_to_all | solution.py:209
  146.8 1.4 shard_map.92.own_ref
  148.2 4.6 %collective-permute-start.2 = (bf16[320,256]{1,0:T(8,128)(2,1)S(1)}, bf16[320,256]{1,0:T(8,128)(2,1)S(1)}, u32[]{:S(2)}, u32[]{:S(2)}) collective-permute-start(bf16[320,256]{1,0:T(8,128)(2,1)S(1)} %shard_map.92.own_ref), channel_id=1, source_target_pairs={{0,1},{1,0},{2,3},{3,2},{4,5},{5,4},{6,7},{7,6},{8,9},{9,8},{10,11... | collective-permute-start | bytes 491528 | tf_op jit(solution)/shard_map/ppermute | solution.py:211
  152.8 1.9 collective-permute-start.3
  154.7 10.3 %collective-permute-done.2.zh_ref = bf16[320,256]{1,0:T(8,128)(2,1)S(1)} collective-permute-done((bf16[320,256]{1,0:T(8,128)(2,1)S(1)}, bf16[320,256]{1,0:T(8,128)(2,1)S(1)}, u32[]{:S(2)}, u32[]{:S(2)}) %collective-permute-start.2) | collective-permute-done | bytes 163872 | tf_op jit(solution)/shard_map/ppermute | solution.py:211
  165.1 1.9 collective-permute-start.4
  167.0 0.1 pad_add_fusion.place_ref
  167.1 0.0 all-gather.8.cloned.1.call-done
  167.1 0.0 collective-permute-done.3.core_ref
  167.1 1.3 collective-permute-done.4.both_ref
  168.3 0.0 copy-start
  168.3 1.7 copy-done
  170.1 2.9 %shard_map.93 = bf16[4,320,320]{2,1,0:T(8,128)(2,1)S(1)} custom-call(s32[2]{0:T(128)S(1)} %pad_add_fusion.place_ref, bf16[320,256]{1,0:T(8,128)(2,1)S(1)} %shard_map.92.own_ref, bf16[320,256]{1,0:T(8,128)(2,1)S(1)} %collective-permute-done.2.zh_ref, bf16[320,256]{1,0:T(8,128)(2,1)S(1)} %collective-permute-done.3.core_ref, ...), custom_call_target="tpu_custom_call" | custom-call | tf_op jit(solution)/shard_map/pallas_call | solution.py:137
  173.0 0.0 copy-start.4
  173.0 19.7 %all_to_all.17 = bf16[4,320,320]{2,1,0:T(8,128)(2,1)S(1)} all-to-all(bf16[4,320,320]{2,1,0:T(8,128)(2,1)S(1)} %shard_map.93), channel_id=1, replica_groups=mesh['x'=4,'zl'=8,'y'=4,'core'=2,'zh'=2] {'y'}, dimensions={0} | all-to-all | bytes 1638400 | tf_op jit(solution)/shard_map/all_to_all | solution.py:216
  192.7 0.2 convert_reduce_fusion
  192.9 0.0 copy-done.4
  192.9 0.7 multiply_convert_fusion
  (17 shorter events, 0.2 us)
Async XLA Ops:
  6.5 86.4 %copy-start.3 = (s32[2560]{0:T(1024)S(1)}, s32[2560]{0:T(1024)}, u32[]{:S(2)}) copy-start(s32[2560]{0:T(1024)} %constant.28.clone) | copy-start | bytes 30724
  6.5 86.6 %copy-start.2 = (bf16[320,256]{1,0:T(8,128)(2,1)S(1)}, bf16[320,256]{1,0:T(8,128)(2,1)}, u32[]{:S(2)}) copy-start(bf16[320,256]{1,0:T(8,128)(2,1)} %param.9) | copy-start | bytes 491524
  6.5 86.4 %copy-start.5 = (f32[256]{0:T(256)S(1)}, f32[256]{0:T(256)}, u32[]{:S(2)}) copy-start(f32[256]{0:T(256)} %param.14) | copy-start | bytes 3076
  6.5 86.6 %copy-start.6 = (f32[256]{0:T(256)S(1)}, f32[256]{0:T(256)}, u32[]{:S(2)}) copy-start(f32[256]{0:T(256)} %param.13) | copy-start | bytes 3076
  6.5 99.9 %all-gather.6.cloned.1.call-start = ((), (), s32[]{:S(2)}) async-start(), calls=%async_computation.3 | async-start | bytes 2949120 | tf_op jit(solution)/shard_map/all_gather | solution.py:179
  8.4 158.6 %all-gather.8.cloned.1.call-start = ((), (), s32[]{:S(2)}) async-start(), calls=%async_computation.4 | async-start | bytes 3276800 | tf_op jit(solution)/shard_map/all_gather | solution.py:202
  20.4 17.4 %collective-permute-start = (f32[2,320]{1,0:T(2,128)S(1)}, f32[2,320]{1,0:T(2,128)S(1)}, u32[]{:S(2)}, u32[]{:S(2)}) collective-permute-start(f32[2,320]{1,0:T(2,128)S(1)} %reduce_sum.38), channel_id=1, source_target_pairs={{0,1},{1,0},{2,3},{3,2},{4,5},{5,4},{6,7},{7,6},{8,9},{9,8},{10,11... | collective-permute-start | bytes 7688 | tf_op jit(solution)/shard_map/ppermute | solution.py:194
  36.1 1.7 collective-permute-start.1
  106.5 1.7 copy-start.1
  148.2 16.9 %collective-permute-start.2 = (bf16[320,256]{1,0:T(8,128)(2,1)S(1)}, bf16[320,256]{1,0:T(8,128)(2,1)S(1)}, u32[]{:S(2)}, u32[]{:S(2)}) collective-permute-start(bf16[320,256]{1,0:T(8,128)(2,1)S(1)} %shard_map.92.own_ref), channel_id=1, source_target_pairs={{0,1},{1,0},{2,3},{3,2},{4,5},{5,4},{6,7},{7,6},{8,9},{9,8},{10,11... | collective-permute-start | bytes 491528 | tf_op jit(solution)/shard_map/ppermute | solution.py:211
  152.8 14.3 %collective-permute-start.3 = (bf16[320,256]{1,0:T(8,128)(2,1)S(1)}, bf16[320,256]{1,0:T(8,128)(2,1)S(1)}, u32[]{:S(2)}, u32[]{:S(2)}) collective-permute-start(bf16[320,256]{1,0:T(8,128)(2,1)S(1)} %shard_map.92.own_ref), channel_id=1, source_target_pairs={{0,2},{2,0},{1,3},{3,1},{4,6},{6,4},{5,7},{7,5},{8,10},{10,8},{9,1... | collective-permute-start | bytes 491528 | tf_op jit(solution)/shard_map/ppermute | solution.py:212
  165.1 3.3 %collective-permute-start.4 = (bf16[320,256]{1,0:T(8,128)(2,1)S(1)}, bf16[320,256]{1,0:T(8,128)(2,1)S(1)}, u32[]{:S(2)}, u32[]{:S(2)}) collective-permute-start(bf16[320,256]{1,0:T(8,128)(2,1)S(1)} %collective-permute-done.2.zh_ref), channel_id=1, source_target_pairs={{0,2},{2,0},{1,3},{3,1},{4,6},{6,4},{5,7},{7,5},{8,10},{10,8},{9,1... | collective-permute-start | bytes 491528 | tf_op jit(solution)/shard_map/ppermute | solution.py:213
  168.3 1.7 copy-start
  173.0 19.9 %copy-start.4 = (f32[320]{0:T(512)S(1)}, f32[320]{0:T(512)}, u32[]{:S(2)}) copy-start(f32[320]{0:T(512)} %param.15) | copy-start | bytes 3844
Sparse Core Ops, SparseCore 0:
  9.5 89.8 all-gather.5
  101.4 51.3 all-gather.7

commit v4 on v2

v4 whole, which is shorter than its diff:
```python
import functools
import math

import jax
import jax.numpy as jnp
import numpy as np
from jax import lax
from jax.experimental import pallas as pl
from jax.experimental.pallas import tpu as pltpu
from jax.sharding import Mesh
from jax.sharding import PartitionSpec as P

HEAD_DIM = 128
EPSILON = 1e-06
BIAS = -1e30
F32 = jnp.float32
BF16 = jnp.bfloat16
AXES = ("xh", "xl", "zl", "y", "core", "zh")
SIZES = (2, 2, 8, 4, 2, 2)
X = ("xh", "xl")
SWAP = ((0, 1), (1, 0))
RING = [0, 2, 4, 6, 7, 5, 3, 1]


def attention_kernel(
    q_ref, kv_ref, inverse_ref, bias_ref, gain_ref, out_ref, kt_ref, ve_ref, *, rows, keys
):
    factor = HEAD_DIM**-0.5 * math.log2(math.e)
    odd = pl.program_id(0) % 2

    @pl.when(pl.program_id(0) == 0)
    def _():
        row = lax.broadcasted_iota(jnp.int32, (HEAD_DIM, keys), 0)
        bias = jnp.where(row == 0, bias_ref[...], 0.0).astype(BF16)
        for h in range(2):
            columns = slice(h * HEAD_DIM, (h + 1) * HEAD_DIM)
            raw = kv_ref[:, columns].T.astype(F32)
            kt_ref[h, :HEAD_DIM, :] = (raw * inverse_ref[...] * gain_ref[columns, :]).astype(BF16)
            kt_ref[h, HEAD_DIM:, :] = bias
            ve_ref[h, :, :HEAD_DIM] = kv_ref[:, (2 + h) * HEAD_DIM : (3 + h) * HEAD_DIM]
            ve_ref[h, :, HEAD_DIM:] = jnp.ones((keys, HEAD_DIM), BF16)

    lane = lax.broadcasted_iota(jnp.int32, (rows, HEAD_DIM), 1)
    first = jnp.where(lane == 0, 1.0, 0.0).astype(BF16)
    base = 3 * odd
    start = pl.multiple_of(odd * rows, 16)
    for h in range(2):
        query = jnp.concatenate([q_ref[0, h * rows : (h + 1) * rows, :], first], axis=1)
        scores = jnp.dot(query, kt_ref[h], preferred_element_type=F32)
        top = (jnp.max(scores, axis=1, keepdims=True) * factor).astype(BF16).astype(F32)
        weights = jnp.exp2(scores * factor - top).astype(BF16)
        summed = jnp.dot(weights, ve_ref[h], preferred_element_type=F32)
        out_ref[h, pl.ds(start, rows), :] = summed[:, :HEAD_DIM].astype(BF16)
        mass = summed[:, HEAD_DIM:]
        high = mass.astype(BF16).astype(F32)
        stats = jnp.where(lane == base, top, mass - high)
        stats = jnp.where(lane == base + 1, high, stats)
        kept = jnp.where(lane < base, out_ref[h, 2 * rows :, :].astype(F32), stats)
        out_ref[h, 2 * rows :, :] = kept.astype(BF16)


def attention(queries, keys_values, inverse, bias, gain, rows):
    blocks = queries.shape[0]
    keys = keys_values.shape[0]
    return pl.pallas_call(
        functools.partial(attention_kernel, rows=rows, keys=keys),
        grid=(blocks,),
        in_specs=[
            pl.BlockSpec((1, 2 * rows, HEAD_DIM), lambda i: (i, 0, 0)),
            pl.BlockSpec((keys, 4 * HEAD_DIM), lambda i: (0, 0)),
            pl.BlockSpec((1, keys), lambda i: (0, 0)),
            pl.BlockSpec((1, keys), lambda i: (0, 0)),
            pl.BlockSpec((2 * HEAD_DIM, 1), lambda i: (0, 0)),
        ],
        out_specs=pl.BlockSpec((2, 3 * rows, HEAD_DIM), lambda i: (i // 2, 0, 0)),
        out_shape=jax.ShapeDtypeStruct((blocks, 3 * rows, HEAD_DIM), BF16),
        scratch_shapes=[
            pltpu.VMEM((2, 2 * HEAD_DIM, keys), BF16),
            pltpu.VMEM((2, keys, 2 * HEAD_DIM), BF16),
        ],
        compiler_params=pltpu.CompilerParams(vmem_limit_bytes=48 << 20),
        cost_estimate=pl.CostEstimate(
            flops=16 * blocks * rows * keys * HEAD_DIM,
            bytes_accessed=4 << 20,
            transcendentals=2 * blocks * rows * keys,
        ),
    )(queries, keys_values, inverse, bias, gain)


def join_kernel(parts_ref, out_ref, *, rows):
    count = parts_ref.shape[0]
    for j in range(2):
        columns = [
            [parts_ref[i, 2 * rows :, 3 * j + n : 3 * j + n + 1].astype(F32) for n in range(3)]
            for i in range(count)
        ]
        highest = functools.reduce(jnp.maximum, [c[0] for c in columns])
        total = jnp.zeros((rows, HEAD_DIM), F32)
        mass = jnp.zeros_like(highest)
        for i in range(count):
            share = jnp.exp2(columns[i][0] - highest)
            mass = mass + share * (columns[i][1] + columns[i][2])
            total = total + share * parts_ref[i, j * rows : (j + 1) * rows, :].astype(F32)
        out_ref[j * rows : (j + 1) * rows, :] = (total * (1.0 / mass)).astype(BF16)


def join(parts, rows):
    return pl.pallas_call(
        functools.partial(join_kernel, rows=rows),
        out_shape=jax.ShapeDtypeStruct((2 * rows, HEAD_DIM), BF16),
        compiler_params=pltpu.CompilerParams(vmem_limit_bytes=32 << 20),
    )(parts)


def project_kernel(place_ref, own_ref, zh_ref, core_ref, both_ref, weight_ref, out_ref):
    rows, columns = out_ref.shape[2], weight_ref.shape[2]
    core, zh = place_ref[0], place_ref[1]
    for r in range(2):
        total = jnp.zeros((2 * rows, columns), F32)
        for ref, a, b in (
            (own_ref, core, zh),
            (zh_ref, core, 1 - zh),
            (core_ref, 1 - core, zh),
            (both_ref, 1 - core, 1 - zh),
        ):
            pair = a * 2 + b
            block = weight_ref[pair if r == 0 else 7 - pair, 0]
            total = total + lax.dot_general(
                ref[...], block, (((1,), (1,)), ((), ())), preferred_element_type=F32
            )
        for j in range(2):
            out_ref[j, 0, :, r * columns : (r + 1) * columns] = total[
                j * rows : (j + 1) * rows
            ].astype(BF16)


def project(place, pieces, weights):
    rows = pieces[0].shape[0] // 2
    blocks, groups, columns, depth = weights.shape
    whole = pl.BlockSpec((2 * rows, depth), lambda i: (0, 0))
    return pl.pallas_call(
        project_kernel,
        grid=(groups,),
        in_specs=[pl.BlockSpec(memory_space=pltpu.SMEM)]
        + [whole] * 4
        + [pl.BlockSpec((blocks, 1, columns, depth), lambda i: (0, i, 0, 0))],
        out_specs=pl.BlockSpec((2, 1, rows, 2 * columns), lambda i: (0, i, 0, 0)),
        out_shape=jax.ShapeDtypeStruct((2, groups, rows, 2 * columns), BF16),
        compiler_params=pltpu.CompilerParams(vmem_limit_bytes=32 << 20),
    )(place, *pieces, weights)


def weight_routes():
    routes = []
    for zl in range(8):
        c, z, r = zl // 4, zl // 2 % 2, zl % 2
        for a in range(2):
            for b in range(2):
                routes.append(((zl * 2 + a) * 2 + b, ((a * 4 + b * 2 + r) * 2 + c) * 2 + z))
    return routes


def local(queries, keys, values, out_weight, q_gain, k_gain, gate, valid_count):
    rows, width = queries.shape
    features = width * 16
    gathered = lax.all_gather(
        jnp.concatenate([keys, values], axis=1), "zl", axis=0, tiled=True, axis_index_groups=[RING]
    )
    weights = lax.ppermute(out_weight.T, ("zl", "core", "zh"), weight_routes())

    squares = jnp.stack(
        [
            jnp.sum(jnp.square(queries.astype(F32)), axis=1),
            jnp.sum(jnp.square(keys.astype(F32)), axis=1),
        ]
    )
    near = lax.all_to_all(
        jnp.broadcast_to(squares[None], (8, 2, rows)), ("y", "core"), 0, 0, tiled=True
    )
    near = jnp.sum(near, axis=0)
    totals = near + lax.ppermute(near, "zh", SWAP)
    inverse = lax.rsqrt(totals / features + EPSILON)
    key_inverse = lax.all_to_all(
        jnp.broadcast_to(inverse[1][None], (8, rows)), "zl", 0, 0, tiled=True
    )
    key_inverse = jnp.concatenate([key_inverse[z] for z in RING])[None, :]
    query_norm = (queries.astype(F32) * inverse[0][:, None] * q_gain[None, :]).astype(BF16)
    heads = [query_norm[:, :HEAD_DIM], query_norm[:, HEAD_DIM:]]
    to_even = jnp.concatenate(heads + [weights[:, :HEAD_DIM]])
    to_odd = jnp.concatenate(heads + [weights[:, HEAD_DIM:]])
    along_x = lax.all_to_all(
        jnp.stack([to_even, to_odd, to_even, to_odd]), X, 0, 0, tiled=True
    )
    weights = lax.all_gather(
        along_x[:, 2 * rows :], "zl", axis=0, tiled=False, axis_index_groups=[RING]
    )

    place_x = lax.axis_index("xh") * 2 + lax.axis_index("xl")
    limit = valid_count[0] - place_x * (8 * rows)
    starts = np.repeat(np.asarray(RING, np.int32) * rows, rows)
    position = jnp.asarray(starts + np.tile(np.arange(rows, dtype=np.int32), 8))
    bias = jnp.where(position < limit, 0.0, BIAS).astype(F32)[None, :]
    parts = attention(along_x, gathered, key_inverse, bias, k_gain[:, None], rows)
    parts = lax.all_to_all(parts, X, 0, 0, tiled=True)
    own = join(parts, rows)
    across = lax.ppermute(own, "zh", SWAP)
    beside = lax.ppermute(own, "core", SWAP)
    both = lax.ppermute(across, "core", SWAP)
    place = jnp.stack([lax.axis_index("core"), lax.axis_index("zh")]).astype(jnp.int32)
    terms = project(place, (own, across, beside, both), weights)
    terms = lax.all_to_all(terms.reshape(8, rows, -1), ("xl", "y"), 0, 0, tiled=True)
    summed = jnp.sum(terms.astype(F32), axis=0)
    return (gate[None, :] * summed).astype(BF16)


def solution(mesh):
    fine = Mesh(mesh.devices.reshape(SIZES), AXES)
    tokens, features = ("xh", "xl", "zl"), ("y", "core", "zh")
    placed = (
        P(tokens, features),
        P(tokens, features),
        P(tokens, features),
        P(features, tokens),
        P(features),
        P(features),
        P(features),
        P(),
    )
    return jax.shard_map(
        local, mesh=fine, in_specs=placed, out_specs=P(tokens, features), check_vma=False
    )
```

time: 203 us -> 203 us (level)
  the two profiles are of different devices: /device:TPU:6 before, /device:TPU:32 now
where the time goes in v4:
time: 203 us
  blocking collectives  73.4 us (36%)
  starting transfers between devices  51.8 us (26%)
  waiting for transfers between devices  33.3 us (16%)
  Pallas kernels  18.8 us (9%)
  between operations  14.2 us (7%)
  other arithmetic  6.2 us (3%)
  local copies, waits for them, and re-layouts  5.05 us (2%)
    all_to_all x1, blocking collectives, local(): lax.all_to_all(terms.reshape(8, rows, -1), ('xl', 'y'), 0, 0, tiled=True)  31.4 us
    all_to_all x1, starting transfers between devices, local(): lax.all_to_all(jnp.broadcast_to(inverse[1][None], (8, rows)), 'zl', 0, 0,...  20.8 us
    ppermute x1, waiting for transfers between devices, local(): across = lax.ppermute(own, 'zh', SWAP)  20.4 us
    all_to_all x1, blocking collectives, local(): parts = lax.all_to_all(parts, X, 0, 0, tiled=True)  18.1 us
    ppermute x1, starting transfers between devices, local(): totals = near + lax.ppermute(near, 'zh', SWAP)  14.8 us
    all_to_all x1, blocking collectives, local(): lax.all_to_all(jnp.stack([to_even, to_odd, to_even, to_odd]), X, 0, 0, ti...  14.3 us
    pallas_call x1, Pallas kernels, attention(): pl.pallas_call(functools.partial(attention_kernel, rows=rows, keys=keys),...  12.9 us
    ppermute x1, starting transfers between devices, local(): across = lax.ppermute(own, 'zh', SWAP)  10.7 us
  transfers between devices with their start and end apart: 8, of which 5 were waited for; matrix products, arithmetic and copies ran while one was open for 2% of the time, Pallas kernels for 7%

profile of v4, /device:TPU:32, one launch (start us, length us, event | category | flops | bytes accessed | tf_op | source)
XLA Modules:
  0.0 202.8 jit_solution(4122983487653562813)
XLA Ops:
  6.5 0.0 all-gather.4.cloned.1.call-start
  6.5 1.7 pad_maximum_fusion.1
  8.3 0.0 all-gather.4.cloned.1.call-update
  8.3 0.0 all-gather.6.cloned.1.call-start
  8.3 1.1 fusion
  9.4 1.1 multiply_reduce_fusion
  10.5 9.7 %all_to_all.26 = f32[8,2,320]{2,1,0:T(2,128)S(1)} all-to-all(f32[8,2,320]{2,1,0:T(2,128)S(1)} %broadcast_in_dim.30), channel_id=1, replica_groups=mesh['xh'=2,'xl'=2,'zl'=8,'y'=4,'core'=2,'zh'=2] {'y','core'}, dimensions={0} | all-to-all | bytes 40960 | tf_op jit(solution)/shard_map/all_to_all | solution.py:177
  20.2 14.8 %collective-permute-start = (f32[2,320]{1,0:T(2,128)S(1)}, f32[2,320]{1,0:T(2,128)S(1)}, u32[]{:S(2)}, u32[]{:S(2)}) collective-permute-start(f32[2,320]{1,0:T(2,128)S(1)} %reduce_sum.38), channel_id=1, source_target_pairs={{0,1},{1,0},{2,3},{3,2},{4,5},{5,4},{6,7},{7,6},{8,9},{9,8},{10,11... | collective-permute-start | bytes 7688 | tf_op jit(solution)/shard_map/ppermute | solution.py:181
  35.0 1.5 collective-permute-start.1
  36.6 0.1 collective-permute-done
  36.8 1.0 fusion.2
  37.8 0.0 collective-permute-done.1
  37.8 0.0 copy-start.2
  37.9 0.0 copy-start.4
  37.9 0.1 pad_maximum_fusion
  38.0 14.3 %all_to_all.27.q_ref = bf16[4,800,128]{2,1,0:T(8,128)(2,1)S(1)} all-to-all(bf16[4,800,128]{2,1,0:T(8,128)(2,1)S(1)} %pad_maximum_fusion), channel_id=1, replica_groups=mesh['xh'=2,'xl'=2,'zl'=8,'y'=4,'core'=2,'zh'=2] {'xh','xl'}, dimensions={0} | all-to-all | bytes 1638400 | tf_op jit(solution)/shard_map/all_to_all | solution.py:191
  52.3 0.7 slice.85
  53.0 0.0 all-gather.6.cloned.1.call-update
  53.6 0.6 broadcast_in_dim.31
  54.2 20.8 %all-to-all-start.2 = ((f32[8,1,320]{2,1,0:T(1,128)}), f32[8,1,320]{2,1,0:T(1,128)S(1)}, u32[]{:S(2)}, u32[]{:S(2)}) async-start(f32[8,1,320]{2,1,0:T(1,128)} %broadcast_in_dim.31), calls=%async_computation.2 | async-start | bytes 24576 | tf_op jit(solution)/shard_map/all_to_all | solution.py:183
  75.1 0.0 copy-done.2
  75.1 0.0 copy-done.4
  75.1 0.1 copy.14.gain_ref
  75.2 8.9 %all-to-all-done.2 = f32[8,1,320]{2,1,0:T(1,128)S(1)} async-done(((f32[8,1,320]{2,1,0:T(1,128)}), f32[8,1,320]{2,1,0:T(1,128)S(1)}, u32[]{:S(2)}, u32[]{:S(2)}) %all-to-all-start.2) | async-done | bytes 10272 | tf_op jit(solution)/shard_map/all_to_all | solution.py:183
  84.2 0.1 concatenate.15
  84.3 2.5 %all-gather.4.cloned.1.call-done.kv_ref = bf16[2560,512]{1,0:T(8,128)(2,1)} async-done(((bf16[320,512]{1,0:T(8,128)(2,1)}), bf16[2560,512]{1,0:T(8,128)(2,1)}) %all-gather.4.cloned.1.call-update) | async-done | bytes 2621456 | tf_op jit(solution)/shard_map/all_gather | solution.py:166
  86.9 0.0 copy-start.1
  86.9 1.7 copy-done.1
  88.6 12.9 %shard_map.91 = bf16[4,960,128]{2,1,0:T(8,128)(2,1)S(1)} custom-call(bf16[4,800,128]{2,1,0:T(8,128)(2,1)S(1)} %all_to_all.27.q_ref, bf16[2560,512]{1,0:T(8,128)(2,1)S(1)} %copy-done.1, f32[1,2560]{1,0:T(1,128)S(1)} %broadcast_in_dim.32.inverse_ref, f32[1,2560]{1,0:T(1,128)S(1)} %broadcast_in_dim.35.bias_ref, f32[256,1]{1,0:T(8,128)S(1)} %copy.14.gain_ref), custom_call_target="tpu_custom_call" | custom-call | flops 6710886400 | bytes 4194304 | tf_op jit(solution)/shard_map/pallas_call | solution.py:65
  101.5 18.1 %all_to_all.28.parts_ref = bf16[4,960,128]{2,1,0:T(8,128)(2,1)S(1)} all-to-all(bf16[4,960,128]{2,1,0:T(8,128)(2,1)S(1)} %shard_map.91), channel_id=1, replica_groups=mesh['xh'=2,'xl'=2,'zl'=8,'y'=4,'core'=2,'zh'=2] {'xh','xl'}, dimensions={0} | all-to-all | bytes 1966080 | tf_op jit(solution)/shard_map/all_to_all | solution.py:204
  119.6 1.4 shard_map.92.own_ref
  121.0 10.7 %collective-permute-start.2 = (bf16[640,128]{1,0:T(8,128)(2,1)S(1)}, bf16[640,128]{1,0:T(8,128)(2,1)S(1)}, u32[]{:S(2)}, u32[]{:S(2)}) collective-permute-start(bf16[640,128]{1,0:T(8,128)(2,1)S(1)} %shard_map.92.own_ref), channel_id=1, source_target_pairs={{0,1},{1,0},{2,3},{3,2},{4,5},{5,4},{6,7},{7,6},{8,9},{9,8},{10,11... | collective-permute-start | bytes 491528 | tf_op jit(solution)/shard_map/ppermute | solution.py:206
  131.7 1.9 collective-permute-start.3
  133.6 20.4 %collective-permute-done.2.zh_ref = bf16[640,128]{1,0:T(8,128)(2,1)S(1)} collective-permute-done((bf16[640,128]{1,0:T(8,128)(2,1)S(1)}, bf16[640,128]{1,0:T(8,128)(2,1)S(1)}, u32[]{:S(2)}, u32[]{:S(2)}) %collective-permute-start.2) | collective-permute-done | bytes 163872 | tf_op jit(solution)/shard_map/ppermute | solution.py:206
  154.1 1.9 collective-permute-start.4
  156.0 0.1 pad_add_fusion.place_ref
  156.1 0.0 all-gather.6.cloned.1.call-done
  156.1 0.0 collective-permute-done.3.core_ref
  156.1 1.3 collective-permute-done.4.both_ref
  157.3 0.0 copy-start
  157.3 1.3 copy-done
  158.6 4.5 %shard_map.93 = bf16[2,4,320,320]{3,2,1,0:T(8,128)(2,1)S(1)} custom-call(s32[2]{0:T(128)S(1)} %pad_add_fusion.place_ref, bf16[640,128]{1,0:T(8,128)(2,1)S(1)} %shard_map.92.own_ref, bf16[640,128]{1,0:T(8,128)(2,1)S(1)} %collective-permute-done.2.zh_ref, bf16[640,128]{1,0:T(8,128)(2,1)S(1)} %collective-permute-done.3.core_ref, ...), custom_call_target="tpu_custom_call" | custom-call | tf_op jit(solution)/shard_map/pallas_call | solution.py:141
  163.1 31.4 %all_to_all.29 = bf16[8,320,320]{2,1,0:T(8,128)(2,1)S(1)} all-to-all(bf16[8,320,320]{2,1,0:T(8,128)(2,1)S(1)} %bitcast.12), channel_id=1, replica_groups=mesh['xh'=2,'xl'=2,'zl'=8,'y'=4,'core'=2,'zh'=2] {'xl','y'}, dimensions={0} | all-to-all | bytes 3276800 | tf_op jit(solution)/shard_map/all_to_all | solution.py:211
  194.5 0.0 copy-start.3
  194.5 0.3 convert_reduce_fusion
  194.8 0.4 copy-done.3
  195.2 0.7 multiply_convert_fusion
  (14 shorter events, 0.2 us)
Async XLA Ops:
  6.5 80.3 %all-gather.4.cloned.1.call-start = ((), (), s32[]{:S(2)}) async-start(), calls=%async_computation.5 | async-start | bytes 2949120 | tf_op jit(solution)/shard_map/all_gather | solution.py:166
  8.3 147.8 %all-gather.6.cloned.1.call-start = ((), (), s32[]{:S(2)}) async-start(), calls=%async_computation.6 | async-start | bytes 1474560 | tf_op jit(solution)/shard_map/all_gather | solution.py:194
  20.2 16.5 %collective-permute-start = (f32[2,320]{1,0:T(2,128)S(1)}, f32[2,320]{1,0:T(2,128)S(1)}, u32[]{:S(2)}, u32[]{:S(2)}) collective-permute-start(f32[2,320]{1,0:T(2,128)S(1)} %reduce_sum.38), channel_id=1, source_target_pairs={{0,1},{1,0},{2,3},{3,2},{4,5},{5,4},{6,7},{7,6},{8,9},{9,8},{10,11... | collective-permute-start | bytes 7688 | tf_op jit(solution)/shard_map/ppermute | solution.py:181
  35.0 2.8 %collective-permute-start.1 = (bf16[160,256]{1,0:T(8,128)(2,1)}, bf16[160,256]{1,0:T(8,128)(2,1)S(1)}, u32[]{:S(2)}, u32[]{:S(2)}) collective-permute-start(bf16[160,256]{1,0:T(8,128)(2,1)} %bitcast.15), channel_id=1, source_target_pairs={{0,0},{1,32},{2,64},{3,96},{16,16},{17,48},{18,80},{19,112},{32,1}... | collective-permute-start | bytes 245768 | tf_op jit(solution)/shard_map/ppermute | solution.py:169
  37.8 37.2 %copy-start.2 = (s32[2560]{0:T(1024)S(1)}, s32[2560]{0:T(1024)}, u32[]{:S(2)}) copy-start(s32[2560]{0:T(1024)} %constant.29.clone) | copy-start | bytes 30724
  37.9 37.2 %copy-start.4 = (f32[256]{0:T(256)S(1)}, f32[256]{0:T(256)}, u32[]{:S(2)}) copy-start(f32[256]{0:T(256)} %param.14) | copy-start | bytes 3076
  54.2 29.9 %all-to-all-start.2 = ((f32[8,1,320]{2,1,0:T(1,128)}), f32[8,1,320]{2,1,0:T(1,128)S(1)}, u32[]{:S(2)}, u32[]{:S(2)}) async-start(f32[8,1,320]{2,1,0:T(1,128)} %broadcast_in_dim.31), calls=%async_computation.2 | async-start | bytes 24576 | tf_op jit(solution)/shard_map/all_to_all | solution.py:183
  86.9 1.7 copy-start.1
  121.0 33.1 %collective-permute-start.2 = (bf16[640,128]{1,0:T(8,128)(2,1)S(1)}, bf16[640,128]{1,0:T(8,128)(2,1)S(1)}, u32[]{:S(2)}, u32[]{:S(2)}) collective-permute-start(bf16[640,128]{1,0:T(8,128)(2,1)S(1)} %shard_map.92.own_ref), channel_id=1, source_target_pairs={{0,1},{1,0},{2,3},{3,2},{4,5},{5,4},{6,7},{7,6},{8,9},{9,8},{10,11... | collective-permute-start | bytes 491528 | tf_op jit(solution)/shard_map/ppermute | solution.py:206
  131.7 24.3 %collective-permute-start.3 = (bf16[640,128]{1,0:T(8,128)(2,1)S(1)}, bf16[640,128]{1,0:T(8,128)(2,1)S(1)}, u32[]{:S(2)}, u32[]{:S(2)}) collective-permute-start(bf16[640,128]{1,0:T(8,128)(2,1)S(1)} %shard_map.92.own_ref), channel_id=1, source_target_pairs={{0,2},{2,0},{1,3},{3,1},{4,6},{6,4},{5,7},{7,5},{8,10},{10,8},{9,1... | collective-permute-start | bytes 491528 | tf_op jit(solution)/shard_map/ppermute | solution.py:207
  154.1 3.3 %collective-permute-start.4 = (bf16[640,128]{1,0:T(8,128)(2,1)S(1)}, bf16[640,128]{1,0:T(8,128)(2,1)S(1)}, u32[]{:S(2)}, u32[]{:S(2)}) collective-permute-start(bf16[640,128]{1,0:T(8,128)(2,1)S(1)} %collective-permute-done.2.zh_ref), channel_id=1, source_target_pairs={{0,2},{2,0},{1,3},{3,1},{4,6},{6,4},{5,7},{7,5},{8,10},{10,8},{9,1... | collective-permute-start | bytes 491528 | tf_op jit(solution)/shard_map/ppermute | solution.py:208
  157.3 1.3 copy-start
  194.5 0.7 copy-start.3
Sparse Core Ops, SparseCore 0:
  9.4 77.3 all-gather.3
  88.9 61.9 all-gather.5

commit v5 on v2

--- a/solution.py
+++ b/solution.py
@@ -19,6 +19,7 @@
 SIZES = (4, 8, 4, 2, 2)
 SWAP = ((0, 1), (1, 0))
 RING = [0, 2, 4, 6, 7, 5, 3, 1]
+LARGE = 112
 
 
 def attention_kernel(
@@ -57,8 +58,8 @@
     out_ref[0, :, heads * HEAD_DIM :] = stats.astype(BF16)
 
 
-def attention(queries, keys_values, inverse, bias, gain, rows):
-    blocks, _, width = queries.shape
+def attention(queries, keys_values, inverse, bias, gain):
+    blocks, rows, width = queries.shape
     keys = keys_values.shape[0]
     heads = width // HEAD_DIM
     return pl.pallas_call(
@@ -111,11 +112,14 @@
     )(parts)
 
 
-def project_kernel(place_ref, own_ref, zh_ref, core_ref, both_ref, weight_ref, out_ref):
+def project_kernel(
+    place_ref, own_ref, zh_ref, core_ref, both_ref, large_ref, small_ref, out_ref
+):
     rows = out_ref.shape[1]
+    columns = out_ref.shape[2] // 2
     core, zh = place_ref[0], place_ref[1]
     for r in range(2):
-        total = jnp.zeros((rows, weight_ref.shape[2]), F32)
+        total = jnp.zeros((rows, columns), F32)
         for ref, a, b in (
             (own_ref, core, zh),
             (zh_ref, core, 1 - zh),
@@ -123,27 +127,29 @@
             (both_ref, 1 - core, 1 - zh),
         ):
             pair = a * 2 + b
-            block = weight_ref[pair if r == 0 else 7 - pair, 0]
+            spot = pair if r == 0 else 7 - pair
+            block = jnp.concatenate([large_ref[0, spot], small_ref[0, spot]])
             total = total + lax.dot_general(
                 ref[...], block, (((1,), (1,)), ((), ())), preferred_element_type=F32
             )
-        out_ref[0, :, r * weight_ref.shape[2] : (r + 1) * weight_ref.shape[2]] = total.astype(BF16)
-
-
-def project(place, pieces, weights):
+        out_ref[0, :, r * columns : (r + 1) * columns] = total.astype(BF16)
+
+
+def project(place, pieces, large, small):
     rows, width = pieces[0].shape
-    blocks, groups, columns, _ = weights.shape
+    groups, blocks = large.shape[:2]
+    columns = large.shape[2] + small.shape[2]
     whole = pl.BlockSpec((rows, width), lambda i: (0, 0))
     return pl.pallas_call(
         project_kernel,
         grid=(groups,),
         in_specs=[pl.BlockSpec(memory_space=pltpu.SMEM)]
         + [whole] * 4
-        + [pl.BlockSpec((blocks, 1, columns, width), lambda i: (0, i, 0, 0))],
+        + [pl.BlockSpec((1,) + w.shape[1:], lambda i: (i, 0, 0, 0)) for w in (large, small)],
         out_specs=pl.BlockSpec((1, rows, 2 * columns), lambda i: (i, 0, 0)),
         out_shape=jax.ShapeDtypeStruct((groups, rows, 2 * columns), BF16),
         compiler_params=pltpu.CompilerParams(vmem_limit_bytes=32 << 20),
-    )(place, *pieces, weights)
+    )(place, *pieces, large, small)
 
 
 def weight_routes():
@@ -162,7 +168,15 @@
     gathered = lax.all_gather(
         jnp.concatenate([keys, values], axis=1), "zl", axis=0, tiled=True, axis_index_groups=[RING]
     )
+    columns = out_weight.shape[1]
     weights = lax.ppermute(out_weight.T, ("zl", "core", "zh"), weight_routes())
+    weights = lax.all_gather(
+        jnp.pad(weights, ((0, 256 - columns), (0, 0))),
+        "zl",
+        axis=0,
+        tiled=False,
+        axis_index_groups=[RING],
+    )
 
     squares = jnp.stack(
         [
@@ -181,23 +195,24 @@
     )
     key_inverse = jnp.concatenate([key_inverse[z] for z in RING])[None, :]
     query_norm = (queries.astype(F32) * inverse[0][:, None] * q_gain[None, :]).astype(BF16)
-    along_x = lax.all_gather(jnp.concatenate([query_norm, weights]), "x", axis=0, tiled=False)
-    weights = lax.all_gather(
-        along_x[:, rows:], "zl", axis=0, tiled=False, axis_index_groups=[RING]
-    )
+    query_all = lax.all_gather(query_norm, "x", axis=0, tiled=False)
 
     limit = valid_count[0] - lax.axis_index("x") * (8 * rows)
     starts = np.repeat(np.asarray(RING, np.int32) * rows, rows)
     position = jnp.asarray(starts + np.tile(np.arange(rows, dtype=np.int32), 8))
     bias = jnp.where(position < limit, 0.0, BIAS).astype(F32)[None, :]
-    parts = attention(along_x, gathered, key_inverse, bias, k_gain[:, None], rows)
+    parts = attention(query_all, gathered, key_inverse, bias, k_gain[:, None])
     parts = lax.all_to_all(parts, "x", 0, 0, tiled=True)
     own = join(parts, width)
+    own, weights = lax.optimization_barrier((own, weights))
+    large = lax.all_gather(weights[:, :LARGE], "x", axis=0, tiled=False)
+    small = lax.all_gather(weights[:, LARGE:columns], "x", axis=0, tiled=False)
     across = lax.ppermute(own, "zh", SWAP)
     beside = lax.ppermute(own, "core", SWAP)
+    across, small = lax.optimization_barrier((across, small))
     both = lax.ppermute(across, "core", SWAP)
     place = jnp.stack([lax.axis_index("core"), lax.axis_index("zh")]).astype(jnp.int32)
-    terms = project(place, (own, across, beside, both), weights)
+    terms = project(place, (own, across, beside, both), large, small)
     terms = lax.all_to_all(terms, "y", 0, 0, tiled=True)
     summed = jnp.sum(terms.astype(F32), axis=0)
     return (gate[None, :] * summed).astype(BF16)

time: 203 us -> 208 us (1.025)
  blocking collectives: 57.5 us -> 66.3 us
  starting transfers between devices: 53.5 us -> 45.9 us
  local copies, waits for them, and re-layouts: 5.17 us -> 8.9 us
    all_gather x1, waiting for transfers between devices: 1.22 us -> 19.7 us  [local(): lax.all_gather(jnp.concatenate([keys, values], axis=1), 'zl', axis=0, til...]
    all_gather x1 -> x2, blocking collectives: 13.7 us -> 30.7 us  [the longest x1 17.2 us: local(): small = lax.all_gather(weights[:, LARGE:columns], 'x', axis=0, tiled=False)]
    all_to_all x1, waiting for transfers between devices: 10.5 us -> 0.01 us  [local(): lax.all_to_all(jnp.broadcast_to(inverse[1][None], (8, rows)), 'zl', 0, 0,...]
    all_to_all x1, starting transfers between devices: 20.3 us -> 10.4 us  [local(): lax.all_to_all(jnp.broadcast_to(inverse[1][None], (8, rows)), 'zl', 0, 0,...]
    all_to_all x1 -> x0, blocking collectives: 9.67 us -> none  [local(): lax.all_to_all(jnp.broadcast_to(squares[None], (8, 2, rows)), ('y', 'core...]
    ppermute x1, waiting for transfers between devices: 8.89 us -> 0.01 us  [local(): across = lax.ppermute(own, 'zh', SWAP)]
    all_to_all x0 -> x1, starting transfers between devices: none -> 4.47 us  [local(): lax.all_to_all(jnp.broadcast_to(squares[None], (8, 2, rows)), ('y', 'core...]
    all_to_all x0 -> x1, waiting for transfers between devices: none -> 3.22 us  [local(): lax.all_to_all(jnp.broadcast_to(squares[None], (8, 2, rows)), ('y', 'core...]
  transfers between devices with their start and end apart: 8 -> 10, of which waited for: 5 -> 6; matrix products, arithmetic and copies ran while one was open for 2% -> 3% of each run, Pallas kernels for 7% -> 7%
where the time goes in v5:
time: 208 us; the launch traced here: 206 us
  blocking collectives  66.3 us (32%)
  waiting for transfers between devices  48.4 us (23%)
  starting transfers between devices  45.9 us (22%)
  Pallas kernels  17.1 us (8%)
  between operations  13.9 us (7%)
  local copies, waits for them, and re-layouts  8.9 us (4%)
  other arithmetic  5.72 us (3%)
    all_gather x1, waiting for transfers between devices, local(): lax.all_gather(jnp.concatenate([keys, values], axis=1), 'zl', axis=0, til...  19.7 us
    all_to_all x1, blocking collectives, local(): terms = lax.all_to_all(terms, 'y', 0, 0, tiled=True)  18.5 us
    all_gather x1, waiting for transfers between devices, local(): lax.all_gather(jnp.pad(weights, ((0, 256 - columns), (0, 0))), 'zl', axis...  17.9 us
    all_gather x1, blocking collectives, local(): small = lax.all_gather(weights[:, LARGE:columns], 'x', axis=0, tiled=False)  17.2 us
    all_to_all x1, blocking collectives, local(): parts = lax.all_to_all(parts, 'x', 0, 0, tiled=True)  17.1 us
    ppermute x1, starting transfers between devices, local(): totals = near + lax.ppermute(near, 'zh', SWAP)  15.7 us
    all_gather x1, blocking collectives, local(): query_all = lax.all_gather(query_norm, 'x', axis=0, tiled=False)  13.5 us
    pallas_call x1, Pallas kernels, attention(): pl.pallas_call(functools.partial(attention_kernel, heads=heads, keys=keys...  12.8 us
  transfers between devices with their start and end apart: 10, of which 6 were waited for; matrix products, arithmetic and copies ran while one was open for 3% of the time, Pallas kernels for 7%

profile of v5, /device:TPU:6, one launch (start us, length us, event | category | flops | bytes accessed | tf_op | source)
XLA Modules:
  0.0 206.2 jit_solution(16682137831887217019)
XLA Ops:
  6.5 0.0 copy-start.2
  6.5 0.0 copy-start.4
  6.5 0.0 all-gather.8.cloned.1.call-start
  6.5 1.8 pad_maximum_fusion
  8.3 0.0 all-gather.8.cloned.1.call-update
  8.3 1.1 fusion
  9.4 1.1 multiply_reduce_fusion
  10.5 0.6 broadcast_in_dim.30
  11.1 4.5 %all-to-all-start = ((f32[8,2,320]{2,1,0:T(2,128)}), f32[8,2,320]{2,1,0:T(2,128)S(1)}, u32[]{:S(2)}, u32[]{:S(2)}) async-start(f32[8,2,320]{2,1,0:T(2,128)} %broadcast_in_dim.30), calls=%async_computation | async-start | bytes 49152 | tf_op jit(solution)/shard_map/all_to_all | solution.py:187
  15.6 1.5 collective-permute-start.1
  17.8 3.2 %all-to-all-done = f32[8,2,320]{2,1,0:T(2,128)S(1)} async-done(((f32[8,2,320]{2,1,0:T(2,128)}), f32[8,2,320]{2,1,0:T(2,128)S(1)}, u32[]{:S(2)}, u32[]{:S(2)}) %all-to-all-start) | async-done | bytes 20512 | tf_op jit(solution)/shard_map/all_to_all | solution.py:187
  21.0 15.7 %collective-permute-start = (f32[2,320]{1,0:T(2,128)S(1)}, f32[2,320]{1,0:T(2,128)S(1)}, u32[]{:S(2)}, u32[]{:S(2)}) collective-permute-start(f32[2,320]{1,0:T(2,128)S(1)} %reduce_sum.38), channel_id=1, source_target_pairs={{0,1},{1,0},{2,3},{3,2},{4,5},{5,4},{6,7},{7,6},{8,9},{9,8},{10,11... | collective-permute-start | bytes 7688 | tf_op jit(solution)/shard_map/ppermute | solution.py:191
  36.7 0.7 compare_select_fusion
  37.5 0.8 copy.14.gain_ref
  38.3 0.3 collective-permute-done
  38.7 0.6 broadcast_in_dim.31
  39.3 10.4 %all-to-all-start.1 = ((f32[8,1,320]{2,1,0:T(1,128)}), f32[8,1,320]{2,1,0:T(1,128)S(1)}, u32[]{:S(2)}, u32[]{:S(2)}) async-start(f32[8,1,320]{2,1,0:T(1,128)} %broadcast_in_dim.31), calls=%async_computation.1 | async-start | bytes 24576 | tf_op jit(solution)/shard_map/all_to_all | solution.py:193
  49.7 0.0 all-gather.10.cloned.1.call-start
  49.7 0.0 collective-permute-done.1
  49.7 0.7 pad.4
  50.4 0.0 all-gather.10.cloned.1.call-update
  50.4 0.0 all-gather.12.cloned.1.call-start
  50.4 0.0 copy-done.2
  50.5 0.0 copy-done.4
  50.5 0.1 fusion.2
  50.6 13.5 %all-gather = bf16[1280,256]{1,0:T(8,128)(2,1)S(1)} all-gather(bf16[320,256]{1,0:T(8,128)(2,1)S(1)} %fusion.2), channel_id=2, replica_groups=mesh['x'=4,'zl'=8,'y'=4,'core'=2,'zh'=2] {'x'}, dimensions={0}, use_global_device_ids=true | all-gather | bytes 819200 | tf_op jit(solution)/shard_map/all_gather | solution.py:198
  64.0 0.0 all-to-all-done.1
  64.1 0.1 concatenate.7
  64.2 19.7 %all-gather.8.cloned.1.call-done.kv_ref = bf16[2560,512]{1,0:T(8,128)(2,1)} async-done(((bf16[320,512]{1,0:T(8,128)(2,1)}), bf16[2560,512]{1,0:T(8,128)(2,1)}) %all-gather.8.cloned.1.call-update) | async-done | bytes 2621456 | tf_op jit(solution)/shard_map/all_gather | solution.py:168
  83.9 0.0 copy-start.1
  83.9 1.7 copy-done.1
  85.6 12.8 %shard_map.91 = bf16[4,320,384]{2,1,0:T(8,128)(2,1)S(1)} custom-call(bf16[4,320,256]{2,1,0:T(8,128)(2,1)S(1)} %bitcast.12, bf16[2560,512]{1,0:T(8,128)(2,1)S(1)} %copy-done.1, f32[1,2560]{1,0:T(1,128)S(1)} %broadcast_in_dim.32.inverse_ref, f32[1,2560]{1,0:T(1,128)S(1)} %broadcast_in_dim.35.bias_ref, f32[256,1]{1,0:T(8,128)S(1)} %copy.14.gain_ref), custom_call_target="tpu_custom_call" | custom-call | flops 6710886400 | bytes 4194304 | tf_op jit(solution)/shard_map/pallas_call | solution.py:65
  98.4 17.1 %all_to_all.21.parts_ref = bf16[4,320,384]{2,1,0:T(8,128)(2,1)S(1)} all-to-all(bf16[4,320,384]{2,1,0:T(8,128)(2,1)S(1)} %shard_map.91), channel_id=1, replica_groups=mesh['x'=4,'zl'=8,'y'=4,'core'=2,'zh'=2] {'x'}, dimensions={0} | all-to-all | bytes 1966080 | tf_op jit(solution)/shard_map/all_to_all | solution.py:205
  115.5 1.4 shard_map.92.own_ref
  116.9 17.9 %all-gather.10.cloned.1.call-done = bf16[2048,256]{1,0:T(8,128)(2,1)} async-done(((bf16[256,256]{1,0:T(8,128)(2,1)}), bf16[2048,256]{1,0:T(8,128)(2,1)}) %all-gather.10.cloned.1.call-update) | async-done | bytes 1048592 | tf_op jit(solution)/shard_map/all_gather | solution.py:173
  134.8 1.8 slice.58
  136.6 0.0 all-gather.12.cloned.1.call-update
  136.7 0.9 slice.57
  137.6 9.8 %collective-permute-start.2 = (bf16[320,256]{1,0:T(8,128)(2,1)S(1)}, bf16[320,256]{1,0:T(8,128)(2,1)S(1)}, u32[]{:S(2)}, u32[]{:S(2)}) collective-permute-start(bf16[320,256]{1,0:T(8,128)(2,1)S(1)} %shard_map.92.own_ref), channel_id=1, source_target_pairs={{0,1},{1,0},{2,3},{3,2},{4,5},{5,4},{6,7},{7,6},{8,9},{9,8},{10,11... | collective-permute-start | bytes 491528 | tf_op jit(solution)/shard_map/ppermute | solution.py:210
  147.5 1.9 collective-permute-start.3
  149.4 17.2 %all-gather.2 = bf16[32,48,256]{2,1,0:T(8,128)(2,1)S(1)} all-gather(bf16[8,48,256]{2,1,0:T(8,128)(2,1)S(1)} %slice.57), channel_id=4, replica_groups=mesh['x'=4,'zl'=8,'y'=4,'core'=2,'zh'=2] {'x'}, dimensions={0}, use_global_device_ids=true | all-gather | bytes 983040 | tf_op jit(solution)/shard_map/all_gather | solution.py:209
  166.6 0.0 collective-permute-done.2.zh_ref
  166.6 1.9 collective-permute-start.4
  168.5 0.1 pad_add_fusion.place_ref
  168.6 0.0 collective-permute-done.3.core_ref
  168.6 1.3 collective-permute-done.4.both_ref
  169.9 5.9 %all-gather.12.cloned.1.call-done = bf16[32,112,256]{2,1,0:T(8,128)(2,1)} async-done(((bf16[8,112,256]{2,1,0:T(8,128)(2,1)}), bf16[32,112,256]{2,1,0:T(8,128)(2,1)}) %all-gather.12.cloned.1.call-update) | async-done | bytes 1835024 | tf_op jit(solution)/shard_map/all_gather | solution.py:208
  175.8 0.0 copy-start
  175.8 1.5 copy-done
  177.3 3.0 %shard_map.93 = bf16[4,320,320]{2,1,0:T(8,128)(2,1)S(1)} custom-call(s32[2]{0:T(128)S(1)} %pad_add_fusion.place_ref, bf16[320,256]{1,0:T(8,128)(2,1)S(1)} %shard_map.92.own_ref, bf16[320,256]{1,0:T(8,128)(2,1)S(1)} %collective-permute-done.2.zh_ref, bf16[320,256]{1,0:T(8,128)(2,1)S(1)} %collective-permute-done.3.core_ref, ...), custom_call_target="tpu_custom_call" | custom-call | tf_op jit(solution)/shard_map/pallas_call | solution.py:143
  180.2 0.0 copy-start.3
  180.3 18.5 %all_to_all.22 = bf16[4,320,320]{2,1,0:T(8,128)(2,1)S(1)} all-to-all(bf16[4,320,320]{2,1,0:T(8,128)(2,1)S(1)} %shard_map.93), channel_id=1, replica_groups=mesh['x'=4,'zl'=8,'y'=4,'core'=2,'zh'=2] {'y'}, dimensions={0} | all-to-all | bytes 1638400 | tf_op jit(solution)/shard_map/all_to_all | solution.py:216
  198.8 0.2 convert_reduce_fusion
  198.9 0.0 copy-done.3
  198.9 0.7 multiply_convert_fusion
  (9 shorter events, 0.1 us)
Async XLA Ops:
  6.5 43.9 %copy-start.2 = (bf16[320,256]{1,0:T(8,128)(2,1)S(1)}, bf16[320,256]{1,0:T(8,128)(2,1)}, u32[]{:S(2)}) copy-start(bf16[320,256]{1,0:T(8,128)(2,1)} %param.9) | copy-start | bytes 491524
  6.5 43.9 %copy-start.4 = (f32[256]{0:T(256)S(1)}, f32[256]{0:T(256)}, u32[]{:S(2)}) copy-start(f32[256]{0:T(256)} %param.13) | copy-start | bytes 3076
  6.5 77.3 %all-gather.8.cloned.1.call-start = ((), (), s32[]{:S(2)}) async-start(), calls=%async_computation.4 | async-start | bytes 2949120 | tf_op jit(solution)/shard_map/all_gather | solution.py:168
  11.1 9.9 %all-to-all-start = ((f32[8,2,320]{2,1,0:T(2,128)}), f32[8,2,320]{2,1,0:T(2,128)S(1)}, u32[]{:S(2)}, u32[]{:S(2)}) async-start(f32[8,2,320]{2,1,0:T(2,128)} %broadcast_in_dim.30), calls=%async_computation | async-start | bytes 49152 | tf_op jit(solution)/shard_map/all_to_all | solution.py:187
  15.6 34.1 %collective-permute-start.1 = (bf16[160,256]{1,0:T(8,128)(2,1)}, bf16[160,256]{1,0:T(8,128)(2,1)S(1)}, u32[]{:S(2)}, u32[]{:S(2)}) collective-permute-start(bf16[160,256]{1,0:T(8,128)(2,1)} %bitcast.16), channel_id=1, source_target_pairs={{0,0},{1,32},{2,64},{3,96},{16,16},{17,48},{18,80},{19,112},{32,1}... | collective-permute-start | bytes 245768 | tf_op jit(solution)/shard_map/ppermute | solution.py:172
  21.0 17.6 %collective-permute-start = (f32[2,320]{1,0:T(2,128)S(1)}, f32[2,320]{1,0:T(2,128)S(1)}, u32[]{:S(2)}, u32[]{:S(2)}) collective-permute-start(f32[2,320]{1,0:T(2,128)S(1)} %reduce_sum.38), channel_id=1, source_target_pairs={{0,1},{1,0},{2,3},{3,2},{4,5},{5,4},{6,7},{7,6},{8,9},{9,8},{10,11... | collective-permute-start | bytes 7688 | tf_op jit(solution)/shard_map/ppermute | solution.py:191
  39.3 24.8 %all-to-all-start.1 = ((f32[8,1,320]{2,1,0:T(1,128)}), f32[8,1,320]{2,1,0:T(1,128)S(1)}, u32[]{:S(2)}, u32[]{:S(2)}) async-start(f32[8,1,320]{2,1,0:T(1,128)} %broadcast_in_dim.31), calls=%async_computation.1 | async-start | bytes 24576 | tf_op jit(solution)/shard_map/all_to_all | solution.py:193
  49.7 85.2 %all-gather.10.cloned.1.call-start = ((), (), s32[]{:S(2)}) async-start(), calls=%async_computation.5 | async-start | bytes 1179648 | tf_op jit(solution)/shard_map/all_gather | solution.py:173
  50.4 125.4 %all-gather.12.cloned.1.call-start = ((), (), s32[]{:S(2)}) async-start(), calls=%async_computation.6 | async-start | bytes 2293760 | tf_op jit(solution)/shard_map/all_gather | solution.py:208
  83.9 1.7 copy-start.1
  137.6 29.0 %collective-permute-start.2 = (bf16[320,256]{1,0:T(8,128)(2,1)S(1)}, bf16[320,256]{1,0:T(8,128)(2,1)S(1)}, u32[]{:S(2)}, u32[]{:S(2)}) collective-permute-start(bf16[320,256]{1,0:T(8,128)(2,1)S(1)} %shard_map.92.own_ref), channel_id=1, source_target_pairs={{0,1},{1,0},{2,3},{3,2},{4,5},{5,4},{6,7},{7,6},{8,9},{9,8},{10,11... | collective-permute-start | bytes 491528 | tf_op jit(solution)/shard_map/ppermute | solution.py:210
  147.5 21.2 %collective-permute-start.3 = (bf16[320,256]{1,0:T(8,128)(2,1)S(1)}, bf16[320,256]{1,0:T(8,128)(2,1)S(1)}, u32[]{:S(2)}, u32[]{:S(2)}) collective-permute-start(bf16[320,256]{1,0:T(8,128)(2,1)S(1)} %shard_map.92.own_ref), channel_id=1, source_target_pairs={{0,2},{2,0},{1,3},{3,1},{4,6},{6,4},{5,7},{7,5},{8,10},{10,8},{9,1... | collective-permute-start | bytes 491528 | tf_op jit(solution)/shard_map/ppermute | solution.py:211
  166.6 3.3 %collective-permute-start.4 = (bf16[320,256]{1,0:T(8,128)(2,1)S(1)}, bf16[320,256]{1,0:T(8,128)(2,1)S(1)}, u32[]{:S(2)}, u32[]{:S(2)}) collective-permute-start(bf16[320,256]{1,0:T(8,128)(2,1)S(1)} %collective-permute-done.2.zh_ref), channel_id=1, source_target_pairs={{0,2},{2,0},{1,3},{3,1},{4,6},{6,4},{5,7},{7,5},{8,10},{10,8},{9,1... | collective-permute-start | bytes 491528 | tf_op jit(solution)/shard_map/ppermute | solution.py:213
  175.8 1.5 copy-start
  180.2 18.7 %copy-start.3 = (f32[320]{0:T(512)S(1)}, f32[320]{0:T(512)}, u32[]{:S(2)}) copy-start(f32[320]{0:T(512)} %param.15) | copy-start | bytes 3844
Sparse Core Ops, SparseCore 0:
  9.4 74.3 all-gather.7
  85.9 48.8 all-gather.9
  136.9 38.8 all-gather.11

commit v6 on v2

--- a/solution.py
+++ b/solution.py
@@ -111,48 +111,68 @@
     )(parts)
 
 
-def project_kernel(place_ref, own_ref, zh_ref, core_ref, both_ref, weight_ref, out_ref):
-    rows = out_ref.shape[1]
+def project_kernel(
+    place_ref, own_ref, core_ref, zh_ref, both_ref, weight_ref, gate_ref, out_ref, total_ref
+):
+    columns = weight_ref.shape[2]
     core, zh = place_ref[0], place_ref[1]
+    step = pl.program_id(0)
     for r in range(2):
-        total = jnp.zeros((rows, weight_ref.shape[2]), F32)
+        total = jnp.zeros((out_ref.shape[0], columns), F32)
         for ref, a, b in (
             (own_ref, core, zh),
+            (core_ref, 1 - core, zh),
             (zh_ref, core, 1 - zh),
-            (core_ref, 1 - core, zh),
             (both_ref, 1 - core, 1 - zh),
         ):
             pair = a * 2 + b
             block = weight_ref[pair if r == 0 else 7 - pair, 0]
             total = total + lax.dot_general(
-                ref[...], block, (((1,), (1,)), ((), ())), preferred_element_type=F32
+                ref[0], block, (((1,), (1,)), ((), ())), preferred_element_type=F32
             )
-        out_ref[0, :, r * weight_ref.shape[2] : (r + 1) * weight_ref.shape[2]] = total.astype(BF16)
-
-
-def project(place, pieces, weights):
-    rows, width = pieces[0].shape
-    blocks, groups, columns, _ = weights.shape
-    whole = pl.BlockSpec((rows, width), lambda i: (0, 0))
+
+        @pl.when(step == 0)
+        def _():
+            total_ref[r] = total
+
+        @pl.when(step > 0)
+        def _():
+            total_ref[r] += total
+
+    @pl.when(step == pl.num_programs(0) - 1)
+    def _():
+        for r in range(2):
+            span = slice(r * columns, (r + 1) * columns)
+            out_ref[:, span] = (total_ref[r] * gate_ref[:, span]).astype(BF16)
+
+
+def project(place, pieces, weights, gate):
+    groups, rows, width = pieces[0].shape
+    blocks, _, columns, _ = weights.shape
     return pl.pallas_call(
         project_kernel,
         grid=(groups,),
         in_specs=[pl.BlockSpec(memory_space=pltpu.SMEM)]
-        + [whole] * 4
-        + [pl.BlockSpec((blocks, 1, columns, width), lambda i: (0, i, 0, 0))],
-        out_specs=pl.BlockSpec((1, rows, 2 * columns), lambda i: (i, 0, 0)),
-        out_shape=jax.ShapeDtypeStruct((groups, rows, 2 * columns), BF16),
+        + [pl.BlockSpec((1, rows, width), lambda i: (i, 0, 0))] * 4
+        + [
+            pl.BlockSpec((blocks, 1, columns, width), lambda i: (0, i, 0, 0)),
+            pl.BlockSpec((1, 2 * columns), lambda i: (0, 0)),
+        ],
+        out_specs=pl.BlockSpec((rows, 2 * columns), lambda i: (0, 0)),
+        out_shape=jax.ShapeDtypeStruct((rows, 2 * columns), BF16),
+        scratch_shapes=[pltpu.VMEM((2, rows, columns), F32)],
         compiler_params=pltpu.CompilerParams(vmem_limit_bytes=32 << 20),
-    )(place, *pieces, weights)
+    )(place, *pieces, weights, gate)
 
 
 def weight_routes():
     routes = []
-    for zl in range(8):
+    for x, zl, y, a, b in np.ndindex(*SIZES):
         c, z, r = zl // 4, zl // 2 % 2, zl % 2
-        for a in range(2):
-            for b in range(2):
-                routes.append(((zl * 2 + a) * 2 + b, ((a * 4 + b * 2 + r) * 2 + c) * 2 + z))
+        target = (y, a * 4 + b * 2 + r, x, c, z)
+        routes.append(
+            (int(np.ravel_multi_index((x, zl, y, a, b), SIZES)), int(np.ravel_multi_index(target, SIZES)))
+        )
     return routes
 
 
@@ -162,7 +182,7 @@
     gathered = lax.all_gather(
         jnp.concatenate([keys, values], axis=1), "zl", axis=0, tiled=True, axis_index_groups=[RING]
     )
-    weights = lax.ppermute(out_weight.T, ("zl", "core", "zh"), weight_routes())
+    weights = lax.ppermute(out_weight.T, AXES, weight_routes())
 
     squares = jnp.stack(
         [
@@ -194,13 +214,12 @@
     parts = lax.all_to_all(parts, "x", 0, 0, tiled=True)
     own = join(parts, width)
     across = lax.ppermute(own, "zh", SWAP)
-    beside = lax.ppermute(own, "core", SWAP)
-    both = lax.ppermute(across, "core", SWAP)
+    own_y = lax.all_gather(own, "y", axis=0, tiled=False)
+    beside_y = lax.ppermute(own_y, "core", SWAP)
+    across_y = lax.all_gather(across, "y", axis=0, tiled=False)
+    both_y = lax.ppermute(across_y, "core", SWAP)
     place = jnp.stack([lax.axis_index("core"), lax.axis_index("zh")]).astype(jnp.int32)
-    terms = project(place, (own, across, beside, both), weights)
-    terms = lax.all_to_all(terms, "y", 0, 0, tiled=True)
-    summed = jnp.sum(terms.astype(F32), axis=0)
-    return (gate[None, :] * summed).astype(BF16)
+    return project(place, (own_y, beside_y, across_y, both_y), weights, gate[None, :])
 
 
 def solution(mesh):

time: 203 us -> 191 us (0.941)
  the two profiles are of different devices: /device:TPU:6 before, /device:TPU:33 now
where the time goes in v6:
time: 191 us; the launch traced here: 190 us
  blocking collectives  69.7 us (36%)
  starting transfers between devices  51.4 us (27%)
  waiting for transfers between devices  24.9 us (13%)
  Pallas kernels  20 us (10%)
  between operations  14.2 us (7%)
  local copies, waits for them, and re-layouts  5.17 us (3%)
  other arithmetic  5.06 us (3%)
    all_gather x1, blocking collectives, local(): lax.all_gather(jnp.concatenate([query_norm, weights]), 'x', axis=0, tiled...  17.2 us
    all_to_all x1, blocking collectives, local(): parts = lax.all_to_all(parts, 'x', 0, 0, tiled=True)  15.7 us
    all_gather x1, blocking collectives, local(): across_y = lax.all_gather(across, 'y', axis=0, tiled=False)  15.5 us
    ppermute x1, starting transfers between devices, local(): totals = near + lax.ppermute(near, 'zh', SWAP)  14.5 us
    pallas_call x1, Pallas kernels, attention(): pl.pallas_call(functools.partial(attention_kernel, heads=heads, keys=keys...  12.8 us
    ppermute x1, starting transfers between devices, local(): across = lax.ppermute(own, 'zh', SWAP)  12.3 us
    all_gather x1, blocking collectives, local(): own_y = lax.all_gather(own, 'y', axis=0, tiled=False)  11.7 us
    ppermute x1, waiting for transfers between devices, local(): weights = lax.ppermute(out_weight.T, AXES, weight_routes())  10.7 us
  transfers between devices with their start and end apart: 8, of which 5 were waited for; matrix products, arithmetic and copies ran while one was open for 3% of the time, Pallas kernels for 7%

profile of v6, /device:TPU:33, one launch (start us, length us, event | category | flops | bytes accessed | tf_op | source)
XLA Modules:
  0.0 190.4 jit_solution(13705147170421525356)
XLA Ops:
  6.5 0.0 copy-start.2
  6.5 0.0 copy-start.4
  6.5 0.0 all-gather.7.cloned.1.call-start
  6.5 1.8 pad_maximum_fusion
  8.3 0.0 all-gather.7.cloned.1.call-update
  8.3 0.0 all-gather.9.cloned.1.call-start
  8.4 1.1 fusion
  9.5 1.1 multiply_reduce_fusion
  10.6 9.6 %all_to_all.16 = f32[8,2,320]{2,1,0:T(2,128)S(1)} all-to-all(f32[8,2,320]{2,1,0:T(2,128)S(1)} %broadcast_in_dim.32), channel_id=1, replica_groups=mesh['x'=4,'zl'=8,'y'=4,'core'=2,'zh'=2] {'y','core'}, dimensions={0} | all-to-all | bytes 40960 | tf_op jit(solution)/shard_map/all_to_all | solution.py:193
  20.2 14.5 %collective-permute-start = (f32[2,320]{1,0:T(2,128)S(1)}, f32[2,320]{1,0:T(2,128)S(1)}, u32[]{:S(2)}, u32[]{:S(2)}) collective-permute-start(f32[2,320]{1,0:T(2,128)S(1)} %reduce_sum.29), channel_id=1, source_target_pairs={{0,1},{1,0},{2,3},{3,2},{4,5},{5,4},{6,7},{7,6},{8,9},{9,8},{10,11... | collective-permute-start | bytes 7688 | tf_op jit(solution)/shard_map/ppermute | solution.py:197
  34.8 4.9 %collective-permute-start.1 = (bf16[160,256]{1,0:T(8,128)(2,1)}, bf16[160,256]{1,0:T(8,128)(2,1)S(1)}, u32[]{:S(2)}, u32[]{:S(2)}) collective-permute-start(bf16[160,256]{1,0:T(8,128)(2,1)} %bitcast.18), channel_id=1, source_target_pairs={{0,0},{1,32},{2,64},{3,96},{4,128},{5,160},{6,192},{7,224},{8,256}... | collective-permute-start | bytes 245768 | tf_op jit(solution)/shard_map/ppermute | solution.py:185
  39.7 0.0 collective-permute-done
  39.7 1.0 fusion.2
  40.7 10.7 %collective-permute-done.1 = bf16[160,256]{1,0:T(8,128)(2,1)S(1)} collective-permute-done((bf16[160,256]{1,0:T(8,128)(2,1)}, bf16[160,256]{1,0:T(8,128)(2,1)S(1)}, u32[]{:S(2)}, u32[]{:S(2)}) %collective-permute-start.1) | collective-permute-done | bytes 81952 | tf_op jit(solution)/shard_map/ppermute | solution.py:185
  51.5 17.2 %all-gather = bf16[1920,256]{1,0:T(8,128)(2,1)S(1)} all-gather(bf16[480,256]{1,0:T(8,128)(2,1)S(1)} %pad_maximum_fusion.1), channel_id=2, replica_groups=mesh['x'=4,'zl'=8,'y'=4,'core'=2,'zh'=2] {'x'}, dimensions={0}, use_global_device_ids=true | all-gather | bytes 1228800 | tf_op jit(solution)/shard_map/all_gather | solution.py:204
  68.7 0.7 slice.65
  69.5 0.0 all-gather.9.cloned.1.call-update
  70.1 0.6 broadcast_in_dim.33
  70.8 6.1 %all-to-all-start.1 = ((f32[8,1,320]{2,1,0:T(1,128)}), f32[8,1,320]{2,1,0:T(1,128)S(1)}, u32[]{:S(2)}, u32[]{:S(2)}) async-start(f32[8,1,320]{2,1,0:T(1,128)} %broadcast_in_dim.33), calls=%async_computation.1 | async-start | bytes 24576 | tf_op jit(solution)/shard_map/all_to_all | solution.py:199
  76.9 0.0 copy-done.2
  76.9 0.0 copy-done.4
  76.9 0.1 copy.14.gain_ref
  77.1 8.1 %all-to-all-done.1 = f32[8,1,320]{2,1,0:T(1,128)S(1)} async-done(((f32[8,1,320]{2,1,0:T(1,128)}), f32[8,1,320]{2,1,0:T(1,128)S(1)}, u32[]{:S(2)}, u32[]{:S(2)}) %all-to-all-start.1) | async-done | bytes 10272 | tf_op jit(solution)/shard_map/all_to_all | solution.py:199
  85.2 0.1 concatenate.11
  85.3 0.6 all-gather.7.cloned.1.call-done.kv_ref
  85.9 0.0 copy-start.1
  85.9 1.7 copy-done.1
  87.6 12.8 %shard_map.91 = bf16[4,320,384]{2,1,0:T(8,128)(2,1)S(1)} custom-call(bf16[4,480,256]{2,1,0:T(8,128)(2,1)S(1)} %bitcast.16, bf16[2560,512]{1,0:T(8,128)(2,1)S(1)} %copy-done.1, f32[1,2560]{1,0:T(1,128)S(1)} %broadcast_in_dim.34.inverse_ref, f32[1,2560]{1,0:T(1,128)S(1)} %broadcast_in_dim.37.bias_ref, f32[256,1]{1,0:T(8,128)S(1)} %copy.14.gain_ref), custom_call_target="tpu_custom_call" | custom-call | flops 6710886400 | bytes 4194304 | tf_op jit(solution)/shard_map/pallas_call | solution.py:64
  100.4 0.0 copy-start.3
  100.4 15.7 %all_to_all.17.parts_ref = bf16[4,320,384]{2,1,0:T(8,128)(2,1)S(1)} all-to-all(bf16[4,320,384]{2,1,0:T(8,128)(2,1)S(1)} %shard_map.91), channel_id=1, replica_groups=mesh['x'=4,'zl'=8,'y'=4,'core'=2,'zh'=2] {'x'}, dimensions={0} | all-to-all | bytes 1966080 | tf_op jit(solution)/shard_map/all_to_all | solution.py:214
  116.2 1.4 shard_map.92
  117.6 12.3 %collective-permute-start.3 = (bf16[320,256]{1,0:T(8,128)(2,1)S(1)}, bf16[320,256]{1,0:T(8,128)(2,1)S(1)}, u32[]{:S(2)}, u32[]{:S(2)}) collective-permute-start(bf16[320,256]{1,0:T(8,128)(2,1)S(1)} %shard_map.92), channel_id=1, source_target_pairs={{0,1},{1,0},{2,3},{3,2},{4,5},{5,4},{6,7},{7,6},{8,9},{9,8},{10,11... | collective-permute-start | bytes 491528 | tf_op jit(solution)/shard_map/ppermute | solution.py:216
  129.9 11.7 %all-gather.1 = bf16[1280,256]{1,0:T(8,128)(2,1)S(1)} all-gather(bf16[320,256]{1,0:T(8,128)(2,1)S(1)} %shard_map.92), channel_id=3, replica_groups=mesh['x'=4,'zl'=8,'y'=4,'core'=2,'zh'=2] {'y'}, dimensions={0}, use_global_device_ids=true | all-gather | bytes 819200 | tf_op jit(solution)/shard_map/all_gather | solution.py:217
  141.5 6.6 %collective-permute-start.2 = (bf16[4,320,256]{2,1,0:T(8,128)(2,1)S(1)}, bf16[4,320,256]{2,1,0:T(8,128)(2,1)S(1)}, u32[]{:S(2)}, u32[]{:S(2)}) collective-permute-start(bf16[4,320,256]{2,1,0:T(8,128)(2,1)S(1)} %bitcast.10), channel_id=1, source_target_pairs={{0,2},{2,0},{1,3},{3,1},{4,6},{6,4},{5,7},{7,5},{8,10},{10,8},{9,1... | collective-permute-start | bytes 1966088 | tf_op jit(solution)/shard_map/ppermute | solution.py:218
  148.1 3.8 %collective-permute-done.3 = bf16[320,256]{1,0:T(8,128)(2,1)S(1)} collective-permute-done((bf16[320,256]{1,0:T(8,128)(2,1)S(1)}, bf16[320,256]{1,0:T(8,128)(2,1)S(1)}, u32[]{:S(2)}, u32[]{:S(2)}) %collective-permute-start.3) | collective-permute-done | bytes 163872 | tf_op jit(solution)/shard_map/ppermute | solution.py:216
  152.0 15.5 %all-gather.2 = bf16[1280,256]{1,0:T(8,128)(2,1)S(1)} all-gather(bf16[320,256]{1,0:T(8,128)(2,1)S(1)} %collective-permute-done.3), channel_id=4, replica_groups=mesh['x'=4,'zl'=8,'y'=4,'core'=2,'zh'=2] {'y'}, dimensions={0}, use_global_device_ids=true | all-gather | bytes 819200 | tf_op jit(solution)/shard_map/all_gather | solution.py:219
  167.4 6.9 %collective-permute-start.4 = (bf16[4,320,256]{2,1,0:T(8,128)(2,1)S(1)}, bf16[4,320,256]{2,1,0:T(8,128)(2,1)S(1)}, u32[]{:S(2)}, u32[]{:S(2)}) collective-permute-start(bf16[4,320,256]{2,1,0:T(8,128)(2,1)S(1)} %bitcast.12), channel_id=1, source_target_pairs={{0,2},{2,0},{1,3},{3,1},{4,6},{6,4},{5,7},{7,5},{8,10},{10,8},{9,1... | collective-permute-start | bytes 1966088 | tf_op jit(solution)/shard_map/ppermute | solution.py:220
  174.3 0.0 copy-done.3
  174.3 0.1 pad_add_fusion.place_ref
  174.4 0.0 all-gather.9.cloned.1.call-done
  174.4 0.0 collective-permute-done.2.core_ref
  174.4 1.6 collective-permute-done.4.both_ref
  176.0 0.0 copy-start
  176.0 1.7 copy-done
  177.8 5.8 %shard_map.93 = bf16[320,320]{1,0:T(8,128)(2,1)} custom-call(s32[2]{0:T(128)S(1)} %pad_add_fusion.place_ref, bf16[4,320,256]{2,1,0:T(8,128)(2,1)S(1)} %bitcast.11, bf16[4,320,256]{2,1,0:T(8,128)(2,1)S(1)} %collective-permute-done.2.core_ref, bf16[4,320,256]{2,1,0:T(8,128)(2,1)S(1)} %bitcast.13, bf16[4,320,256]{2,1,0:T(8,128)(2,1)S(1)} %collective-permute-done.4.both_ref, ...), custom_call_target="tpu_custom_call" | custom-call | tf_op jit(solution)/shard_map/pallas_call | solution.py:152
  (13 shorter events, 0.2 us)
Async XLA Ops:
  6.5 70.4 %copy-start.2 = (s32[2560]{0:T(1024)S(1)}, s32[2560]{0:T(1024)}, u32[]{:S(2)}) copy-start(s32[2560]{0:T(1024)} %constant.25.clone) | copy-start | bytes 30724
  6.5 70.4 %copy-start.4 = (f32[256]{0:T(256)S(1)}, f32[256]{0:T(256)}, u32[]{:S(2)}) copy-start(f32[256]{0:T(256)} %param.14) | copy-start | bytes 3076
  6.5 79.3 %all-gather.7.cloned.1.call-start = ((), (), s32[]{:S(2)}) async-start(), calls=%async_computation.3 | async-start | bytes 2949120 | tf_op jit(solution)/shard_map/all_gather | solution.py:182
  8.3 166.1 %all-gather.9.cloned.1.call-start = ((), (), s32[]{:S(2)}) async-start(), calls=%async_computation.4 | async-start | bytes 2949120 | tf_op jit(solution)/shard_map/all_gather | solution.py:205
  20.2 19.5 %collective-permute-start = (f32[2,320]{1,0:T(2,128)S(1)}, f32[2,320]{1,0:T(2,128)S(1)}, u32[]{:S(2)}, u32[]{:S(2)}) collective-permute-start(f32[2,320]{1,0:T(2,128)S(1)} %reduce_sum.29), channel_id=1, source_target_pairs={{0,1},{1,0},{2,3},{3,2},{4,5},{5,4},{6,7},{7,6},{8,9},{9,8},{10,11... | collective-permute-start | bytes 7688 | tf_op jit(solution)/shard_map/ppermute | solution.py:197
  34.8 16.7 %collective-permute-start.1 = (bf16[160,256]{1,0:T(8,128)(2,1)}, bf16[160,256]{1,0:T(8,128)(2,1)S(1)}, u32[]{:S(2)}, u32[]{:S(2)}) collective-permute-start(bf16[160,256]{1,0:T(8,128)(2,1)} %bitcast.18), channel_id=1, source_target_pairs={{0,0},{1,32},{2,64},{3,96},{4,128},{5,160},{6,192},{7,224},{8,256}... | collective-permute-start | bytes 245768 | tf_op jit(solution)/shard_map/ppermute | solution.py:185
  70.8 14.4 %all-to-all-start.1 = ((f32[8,1,320]{2,1,0:T(1,128)}), f32[8,1,320]{2,1,0:T(1,128)S(1)}, u32[]{:S(2)}, u32[]{:S(2)}) async-start(f32[8,1,320]{2,1,0:T(1,128)} %broadcast_in_dim.33), calls=%async_computation.1 | async-start | bytes 24576 | tf_op jit(solution)/shard_map/all_to_all | solution.py:199
  85.9 1.7 copy-start.1
  100.4 73.9 %copy-start.3 = (f32[320]{0:T(512)S(1)}, f32[320]{0:T(512)}, u32[]{:S(2)}) copy-start(f32[320]{0:T(512)} %param.15) | copy-start | bytes 3844
  117.6 34.4 %collective-permute-start.3 = (bf16[320,256]{1,0:T(8,128)(2,1)S(1)}, bf16[320,256]{1,0:T(8,128)(2,1)S(1)}, u32[]{:S(2)}, u32[]{:S(2)}) collective-permute-start(bf16[320,256]{1,0:T(8,128)(2,1)S(1)} %shard_map.92), channel_id=1, source_target_pairs={{0,1},{1,0},{2,3},{3,2},{4,5},{5,4},{6,7},{7,6},{8,9},{9,8},{10,11... | collective-permute-start | bytes 491528 | tf_op jit(solution)/shard_map/ppermute | solution.py:216
  141.5 32.9 %collective-permute-start.2 = (bf16[4,320,256]{2,1,0:T(8,128)(2,1)S(1)}, bf16[4,320,256]{2,1,0:T(8,128)(2,1)S(1)}, u32[]{:S(2)}, u32[]{:S(2)}) collective-permute-start(bf16[4,320,256]{2,1,0:T(8,128)(2,1)S(1)} %bitcast.10), channel_id=1, source_target_pairs={{0,2},{2,0},{1,3},{3,1},{4,6},{6,4},{5,7},{7,5},{8,10},{10,8},{9,1... | collective-permute-start | bytes 1966088 | tf_op jit(solution)/shard_map/ppermute | solution.py:218
  167.4 8.6 %collective-permute-start.4 = (bf16[4,320,256]{2,1,0:T(8,128)(2,1)S(1)}, bf16[4,320,256]{2,1,0:T(8,128)(2,1)S(1)}, u32[]{:S(2)}, u32[]{:S(2)}) collective-permute-start(bf16[4,320,256]{2,1,0:T(8,128)(2,1)S(1)} %bitcast.12), channel_id=1, source_target_pairs={{0,2},{2,0},{1,3},{3,1},{4,6},{6,4},{5,7},{7,5},{8,10},{10,8},{9,1... | collective-permute-start | bytes 1966088 | tf_op jit(solution)/shard_map/ppermute | solution.py:220
  176.0 1.7 copy-start
Sparse Core Ops, SparseCore 0:
  9.4 76.4 all-gather.6
  88.0 82.1 all-gather.8

commit v7 on v6

--- a/solution.py
+++ b/solution.py
@@ -22,91 +22,105 @@
 
 
 def attention_kernel(
-    q_ref, kv_ref, inverse_ref, bias_ref, gain_ref, out_ref, kt_ref, ve_ref, *, heads, keys
+    q_ref, kv_ref, inverse_ref, bias_ref, gain_ref, out_ref, kt_ref, ve_ref
 ):
-    tile = q_ref.shape[1]
     factor = HEAD_DIM**-0.5 * math.log2(math.e)
-
-    @pl.when(pl.program_id(0) == 0)
-    def _():
-        row = lax.broadcasted_iota(jnp.int32, (HEAD_DIM, keys), 0)
-        bias = jnp.where(row == 0, bias_ref[...], 0.0).astype(BF16)
-        for h in range(heads):
-            columns = slice(h * HEAD_DIM, (h + 1) * HEAD_DIM)
-            raw = kv_ref[:, columns].T.astype(F32)
-            kt_ref[h, :HEAD_DIM, :] = (raw * inverse_ref[...] * gain_ref[columns, :]).astype(BF16)
-            kt_ref[h, HEAD_DIM:, :] = bias
-            ve_ref[h, :, :HEAD_DIM] = kv_ref[:, (heads + h) * HEAD_DIM : (heads + h + 1) * HEAD_DIM]
-            ve_ref[h, :, HEAD_DIM:] = jnp.ones((keys, HEAD_DIM), BF16)
-
-    lane = lax.broadcasted_iota(jnp.int32, (tile, HEAD_DIM), 1)
+    blocks, rows, width = q_ref.shape
+    keys = kv_ref.shape[0]
+    row = lax.broadcasted_iota(jnp.int32, (HEAD_DIM, keys), 0)
+    bias = jnp.where(row == 0, bias_ref[...], 0.0).astype(BF16)
+    for h in range(2):
+        columns = slice(h * HEAD_DIM, (h + 1) * HEAD_DIM)
+        raw = kv_ref[:, columns].T.astype(F32)
+        kt_ref[h, :HEAD_DIM, :] = (raw * inverse_ref[...] * gain_ref[columns, :]).astype(BF16)
+        kt_ref[h, HEAD_DIM:, :] = bias
+        ve_ref[h, :, :HEAD_DIM] = kv_ref[:, (2 + h) * HEAD_DIM : (3 + h) * HEAD_DIM]
+        ve_ref[h, :, HEAD_DIM:] = jnp.ones((keys, HEAD_DIM), BF16)
+
+    lane = lax.broadcasted_iota(jnp.int32, (rows, HEAD_DIM), 1)
     first = jnp.where(lane == 0, 1.0, 0.0).astype(BF16)
-    stats = jnp.zeros((tile, HEAD_DIM), F32)
-    for h in range(heads):
-        query = jnp.concatenate([q_ref[0, :, h * HEAD_DIM : (h + 1) * HEAD_DIM], first], axis=1)
-        scores = jnp.dot(query, kt_ref[h], preferred_element_type=F32)
-        top = (jnp.max(scores, axis=1, keepdims=True) * factor).astype(BF16).astype(F32)
-        weights = jnp.exp2(scores * factor - top).astype(BF16)
-        summed = jnp.dot(weights, ve_ref[h], preferred_element_type=F32)
-        out_ref[0, :, h * HEAD_DIM : (h + 1) * HEAD_DIM] = summed[:, :HEAD_DIM].astype(BF16)
-        mass = summed[:, HEAD_DIM:]
-        high = mass.astype(BF16).astype(F32)
-        stats = jnp.where(lane == 3 * h, top, stats)
-        stats = jnp.where(lane == 3 * h + 1, high, stats)
-        stats = jnp.where(lane == 3 * h + 2, mass - high, stats)
-    out_ref[0, :, heads * HEAD_DIM :] = stats.astype(BF16)
-
-
-def attention(queries, keys_values, inverse, bias, gain, rows):
-    blocks, _, width = queries.shape
+    for b in range(blocks):
+        stats = jnp.zeros((rows, HEAD_DIM), F32)
+        scores = []
+        for h in range(2):
+            query = jnp.concatenate([q_ref[b, :, h * HEAD_DIM : (h + 1) * HEAD_DIM], first], axis=1)
+            scores.append(jnp.dot(query, kt_ref[h], preferred_element_type=F32))
+        for h in range(2):
+            top = (jnp.max(scores[h], axis=1, keepdims=True) * factor).astype(BF16).astype(F32)
+            weights = jnp.exp2(scores[h] * factor - top).astype(BF16)
+            summed = jnp.dot(weights, ve_ref[h], preferred_element_type=F32)
+            out_ref[b, :rows, h * HEAD_DIM : (h + 1) * HEAD_DIM] = summed[:, :HEAD_DIM].astype(BF16)
+            mass = summed[:, HEAD_DIM:]
+            high = mass.astype(BF16).astype(F32)
+            stats = jnp.where(lane == 3 * h, top, stats)
+            stats = jnp.where(lane == 3 * h + 1, high, stats)
+            stats = jnp.where(lane == 3 * h + 2, mass - high, stats)
+        lines = stats.T[:8]
+        rest = jnp.pad(lines[:, width:], ((0, 0), (0, 2 * width - rows)))
+        out_ref[b, rows:, :] = jnp.concatenate([lines[:, :width], rest]).astype(BF16)
+
+
+def attention(queries, keys_values, inverse, bias, gain):
+    blocks, rows, width = queries.shape
     keys = keys_values.shape[0]
-    heads = width // HEAD_DIM
     return pl.pallas_call(
-        functools.partial(attention_kernel, heads=heads, keys=keys),
-        grid=(blocks,),
+        attention_kernel,
+        grid=(1,),
         in_specs=[
-            pl.BlockSpec((1, rows, width), lambda i: (i, 0, 0)),
+            pl.BlockSpec((blocks, rows, width), lambda i: (0, 0, 0)),
             pl.BlockSpec((keys, 2 * width), lambda i: (0, 0)),
             pl.BlockSpec((1, keys), lambda i: (0, 0)),
             pl.BlockSpec((1, keys), lambda i: (0, 0)),
             pl.BlockSpec((width, 1), lambda i: (0, 0)),
         ],
-        out_specs=pl.BlockSpec((1, rows, width + HEAD_DIM), lambda i: (i, 0, 0)),
-        out_shape=jax.ShapeDtypeStruct((blocks, rows, width + HEAD_DIM), BF16),
+        out_specs=pl.BlockSpec((blocks, rows + 16, width), lambda i: (0, 0, 0)),
+        out_shape=jax.ShapeDtypeStruct((blocks, rows + 16, width), BF16),
         scratch_shapes=[
-            pltpu.VMEM((heads, 2 * HEAD_DIM, keys), BF16),
-            pltpu.VMEM((heads, keys, 2 * HEAD_DIM), BF16),
+            pltpu.VMEM((2, 2 * HEAD_DIM, keys), BF16),
+            pltpu.VMEM((2, keys, 2 * HEAD_DIM), BF16),
         ],
         compiler_params=pltpu.CompilerParams(vmem_limit_bytes=48 << 20),
         cost_estimate=pl.CostEstimate(
             flops=8 * blocks * rows * keys * width,
             bytes_accessed=4 << 20,
-            transcendentals=blocks * rows * keys * heads,
+            transcendentals=2 * blocks * rows * keys,
         ),
     )(queries, keys_values, inverse, bias, gain)
 
 
-def join_kernel(parts_ref, out_ref, *, heads):
+def join_kernel(parts_ref, out_ref):
     count = parts_ref.shape[0]
-    base = heads * HEAD_DIM
-    for h in range(heads):
-        tops = [parts_ref[i, :, base + 3 * h : base + 3 * h + 1].astype(F32) for i in range(count)]
+    rows = out_ref.shape[0]
+    lines = []
+    for i in range(count):
+        packed = parts_ref[i, rows:, :].astype(F32)
+        lines.append(jnp.concatenate([packed[:8, :], packed[8:, :128]], axis=1))
+    shares = []
+    for h in range(2):
+        tops = [line[3 * h : 3 * h + 1] for line in lines]
         highest = functools.reduce(jnp.maximum, tops)
-        total = jnp.zeros(out_ref.shape[:1] + (HEAD_DIM,), F32)
-        mass = jnp.zeros_like(highest)
+        weights = [jnp.exp2(top - highest) for top in tops]
+        mass = sum(
+            w * (line[3 * h + 1 : 3 * h + 2] + line[3 * h + 2 : 3 * h + 3])
+            for w, line in zip(weights, lines)
+        )
+        mass = jnp.where(mass == 0.0, 1.0, mass)
+        shares += [w / mass for w in weights]
+    spread = jnp.zeros((HEAD_DIM - 2 * count, lines[0].shape[1]), F32)
+    columns = jnp.concatenate(shares + [spread]).T
+    for h in range(2):
+        span = slice(h * HEAD_DIM, (h + 1) * HEAD_DIM)
+        total = jnp.zeros((rows, HEAD_DIM), F32)
         for i in range(count):
-            share = jnp.exp2(tops[i] - highest)
-            part = parts_ref[i, :, base + 3 * h + 1 : base + 3 * h + 2].astype(F32)
-            part = part + parts_ref[i, :, base + 3 * h + 2 : base + 3 * h + 3].astype(F32)
-            mass = mass + share * part
-            total = total + share * parts_ref[i, :, h * HEAD_DIM : (h + 1) * HEAD_DIM].astype(F32)
-        out_ref[:, h * HEAD_DIM : (h + 1) * HEAD_DIM] = (total * (1.0 / mass)).astype(BF16)
-
-
-def join(parts, width):
+            share = columns[:rows, h * count + i : h * count + i + 1]
+            total = total + share * parts_ref[i, :rows, span].astype(F32)
+        out_ref[:, span] = total.astype(BF16)
+
+
+def join(parts):
     return pl.pallas_call(
-        functools.partial(join_kernel, heads=width // HEAD_DIM),
-        out_shape=jax.ShapeDtypeStruct((parts.shape[1], width), BF16),
+        join_kernel,
+        out_shape=jax.ShapeDtypeStruct((parts.shape[1] - 16, parts.shape[2]), BF16),
         compiler_params=pltpu.CompilerParams(vmem_limit_bytes=32 << 20),
     )(parts)
 
@@ -201,18 +215,18 @@
     )
     key_inverse = jnp.concatenate([key_inverse[z] for z in RING])[None, :]
     query_norm = (queries.astype(F32) * inverse[0][:, None] * q_gain[None, :]).astype(BF16)
-    along_x = lax.all_gather(jnp.concatenate([query_norm, weights]), "x", axis=0, tiled=False)
-    weights = lax.all_gather(
-        along_x[:, rows:], "zl", axis=0, tiled=False, axis_index_groups=[RING]
-    )
+    query_all = lax.all_gather(query_norm, "x", axis=0, tiled=False)
+    query_all, key_inverse, weights = lax.optimization_barrier((query_all, key_inverse, weights))
+    weights = lax.all_gather(weights, "x", axis=0, tiled=False)
+    weights = lax.all_gather(weights, "zl", axis=0, tiled=False, axis_index_groups=[RING])
 
     limit = valid_count[0] - lax.axis_index("x") * (8 * rows)
     starts = np.repeat(np.asarray(RING, np.int32) * rows, rows)
     position = jnp.asarray(starts + np.tile(np.arange(rows, dtype=np.int32), 8))
     bias = jnp.where(position < limit, 0.0, BIAS).astype(F32)[None, :]
-    parts = attention(along_x, gathered, key_inverse, bias, k_gain[:, None], rows)
+    parts = attention(query_all, gathered, key_inverse, bias, k_gain[:, None])
     parts = lax.all_to_all(parts, "x", 0, 0, tiled=True)
-    own = join(parts, width)
+    own = join(parts)
     across = lax.ppermute(own, "zh", SWAP)
     own_y = lax.all_gather(own, "y", axis=0, tiled=False)
     beside_y = lax.ppermute(own_y, "core", SWAP)

time: 191 us -> 186 us (0.974)
  the two profiles are of different devices: /device:TPU:33 before, /device:TPU:6 now
where the time goes in v7:
time: 186 us; the launch traced here: 185 us
  blocking collectives  76.5 us (41%)
  starting transfers between devices  42.8 us (23%)
  waiting for transfers between devices  27.3 us (15%)
  Pallas kernels  14.5 us (8%)
  between operations  14.2 us (8%)
  other arithmetic  5.05 us (3%)
  local copies, waits for them, and re-layouts  4.42 us (2%)
    all_gather x1, waiting for transfers between devices, local(): lax.all_gather(weights, 'zl', axis=0, tiled=False, axis_index_groups=[RING])  16.9 us
    ppermute x1, starting transfers between devices, local(): totals = near + lax.ppermute(near, 'zh', SWAP)  15.7 us
    all_gather x1, blocking collectives, local(): own_y = lax.all_gather(own, 'y', axis=0, tiled=False)  13.8 us
    all_gather x1, blocking collectives, local(): across_y = lax.all_gather(across, 'y', axis=0, tiled=False)  13.5 us
    all_gather x1, blocking collectives, local(): query_all = lax.all_gather(query_norm, 'x', axis=0, tiled=False)  13.4 us
    all_gather x1, blocking collectives, local(): weights = lax.all_gather(weights, 'x', axis=0, tiled=False)  13.1 us
    all_to_all x1, blocking collectives, local(): parts = lax.all_to_all(parts, 'x', 0, 0, tiled=True)  13 us
    ppermute x1, starting transfers between devices, local(): across = lax.ppermute(own, 'zh', SWAP)  12.1 us
  transfers between devices with their start and end apart: 8, of which 2 were waited for; matrix products, arithmetic and copies ran while one was open for 2% of the time, Pallas kernels for 5%

profile of v7, /device:TPU:6, one launch (start us, length us, event | category | flops | bytes accessed | tf_op | source)
XLA Modules:
  0.0 184.7 jit_solution(12170501869508143275)
XLA Ops:
  6.5 0.0 copy-start.2
  6.5 0.0 copy-start.4
  6.5 0.0 all-gather.8.cloned.1.call-start
  6.5 1.8 pad_maximum_fusion
  8.3 0.0 all-gather.8.cloned.1.call-update
  8.3 1.1 fusion
  9.4 1.1 multiply_reduce_fusion
  10.5 9.7 %all_to_all.16 = f32[8,2,320]{2,1,0:T(2,128)S(1)} all-to-all(f32[8,2,320]{2,1,0:T(2,128)S(1)} %broadcast_in_dim.32), channel_id=1, replica_groups=mesh['x'=4,'zl'=8,'y'=4,'core'=2,'zh'=2] {'y','core'}, dimensions={0} | all-to-all | bytes 40960 | tf_op jit(solution)/shard_map/all_to_all | solution.py:207
  20.2 15.7 %collective-permute-start = (f32[2,320]{1,0:T(2,128)S(1)}, f32[2,320]{1,0:T(2,128)S(1)}, u32[]{:S(2)}, u32[]{:S(2)}) collective-permute-start(f32[2,320]{1,0:T(2,128)S(1)} %reduce_sum.29), channel_id=1, source_target_pairs={{0,1},{1,0},{2,3},{3,2},{4,5},{5,4},{6,7},{7,6},{8,9},{9,8},{10,11... | collective-permute-start | bytes 7688 | tf_op jit(solution)/shard_map/ppermute | solution.py:211
  35.9 3.0 %collective-permute-start.1 = (bf16[160,256]{1,0:T(8,128)(2,1)}, bf16[160,256]{1,0:T(8,128)(2,1)S(1)}, u32[]{:S(2)}, u32[]{:S(2)}) collective-permute-start(bf16[160,256]{1,0:T(8,128)(2,1)} %bitcast.19), channel_id=1, source_target_pairs={{0,0},{1,32},{2,64},{3,96},{4,128},{5,160},{6,192},{7,224},{8,256}... | collective-permute-start | bytes 245768 | tf_op jit(solution)/shard_map/ppermute | solution.py:199
  38.9 0.0 collective-permute-done
  39.0 0.6 broadcast_in_dim.33
  39.6 8.1 %all-to-all-start.1 = ((f32[8,1,320]{2,1,0:T(1,128)}), f32[8,1,320]{2,1,0:T(1,128)S(1)}, u32[]{:S(2)}, u32[]{:S(2)}) async-start(f32[8,1,320]{2,1,0:T(1,128)} %broadcast_in_dim.33), calls=%async_computation.1 | async-start | bytes 24576 | tf_op jit(solution)/shard_map/all_to_all | solution.py:213
  47.7 0.0 all-gather.10.cloned.1.call-start
  47.8 1.0 fusion.2
  48.8 13.4 %all-gather = bf16[1280,256]{1,0:T(8,128)(2,1)S(1)} all-gather(bf16[320,256]{1,0:T(8,128)(2,1)S(1)} %fusion.2), channel_id=2, replica_groups=mesh['x'=4,'zl'=8,'y'=4,'core'=2,'zh'=2] {'x'}, dimensions={0}, use_global_device_ids=true | all-gather | bytes 819200 | tf_op jit(solution)/shard_map/all_gather | solution.py:218
  62.2 0.0 all-to-all-done.1
  62.3 0.1 concatenate.6
  62.3 0.0 collective-permute-done.1
  62.4 13.1 %all-gather.3 = bf16[640,256]{1,0:T(8,128)(2,1)} all-gather(bf16[160,256]{1,0:T(8,128)(2,1)S(1)} %collective-permute-done.1), channel_id=5, replica_groups=mesh['x'=4,'zl'=8,'y'=4,'core'=2,'zh'=2] {'x'}, dimensions={0}, use_global_device_ids=true | all-gather | bytes 409600 | tf_op jit(solution)/shard_map/all_gather | solution.py:220
  75.5 0.0 all-gather.10.cloned.1.call-update
  76.2 0.0 copy-done.2
  76.2 0.0 copy-done.4
  76.2 0.1 copy.14.gain_ref
  76.4 10.3 %all-gather.8.cloned.1.call-done.kv_ref = bf16[2560,512]{1,0:T(8,128)(2,1)} async-done(((bf16[320,512]{1,0:T(8,128)(2,1)}), bf16[2560,512]{1,0:T(8,128)(2,1)}) %all-gather.8.cloned.1.call-update) | async-done | bytes 2621456 | tf_op jit(solution)/shard_map/all_gather | solution.py:196
  86.7 0.0 copy-start.1
  86.7 1.7 copy-done.1
  88.4 8.1 %shard_map.91 = bf16[4,336,256]{2,1,0:T(8,128)(2,1)S(1)} custom-call(bf16[4,320,256]{2,1,0:T(8,128)(2,1)S(1)} %bitcast.16, bf16[2560,512]{1,0:T(8,128)(2,1)S(1)} %copy-done.1, f32[1,2560]{1,0:T(1,128)S(1)} %broadcast_in_dim.34.inverse_ref, f32[1,2560]{1,0:T(1,128)S(1)} %broadcast_in_dim.37.bias_ref, f32[256,1]{1,0:T(8,128)S(1)} %copy.14.gain_ref), custom_call_target="tpu_custom_call" | custom-call | flops 6710886400 | bytes 4194304 | tf_op jit(solution)/shard_map/pallas_call | solution.py:66
  96.5 0.0 copy-start.3
  96.5 13.0 %all_to_all.17.parts_ref = bf16[4,336,256]{2,1,0:T(8,128)(2,1)S(1)} all-to-all(bf16[4,336,256]{2,1,0:T(8,128)(2,1)S(1)} %shard_map.91), channel_id=1, replica_groups=mesh['x'=4,'zl'=8,'y'=4,'core'=2,'zh'=2] {'x'}, dimensions={0} | all-to-all | bytes 1376256 | tf_op jit(solution)/shard_map/all_to_all | solution.py:228
  109.6 0.6 shard_map.92
  110.1 12.1 %collective-permute-start.3 = (bf16[320,256]{1,0:T(8,128)(2,1)S(1)}, bf16[320,256]{1,0:T(8,128)(2,1)S(1)}, u32[]{:S(2)}, u32[]{:S(2)}) collective-permute-start(bf16[320,256]{1,0:T(8,128)(2,1)S(1)} %shard_map.92), channel_id=1, source_target_pairs={{0,1},{1,0},{2,3},{3,2},{4,5},{5,4},{6,7},{7,6},{8,9},{9,8},{10,11... | collective-permute-start | bytes 491528 | tf_op jit(solution)/shard_map/ppermute | solution.py:230
  122.2 13.8 %all-gather.1 = bf16[1280,256]{1,0:T(8,128)(2,1)S(1)} all-gather(bf16[320,256]{1,0:T(8,128)(2,1)S(1)} %shard_map.92), channel_id=3, replica_groups=mesh['x'=4,'zl'=8,'y'=4,'core'=2,'zh'=2] {'y'}, dimensions={0}, use_global_device_ids=true | all-gather | bytes 819200 | tf_op jit(solution)/shard_map/all_gather | solution.py:231
  136.0 1.9 %collective-permute-start.2 = (bf16[4,320,256]{2,1,0:T(8,128)(2,1)S(1)}, bf16[4,320,256]{2,1,0:T(8,128)(2,1)S(1)}, u32[]{:S(2)}, u32[]{:S(2)}) collective-permute-start(bf16[4,320,256]{2,1,0:T(8,128)(2,1)S(1)} %bitcast.11), channel_id=1, source_target_pairs={{0,2},{2,0},{1,3},{3,1},{4,6},{6,4},{5,7},{7,5},{8,10},{10,8},{9,1... | collective-permute-start | bytes 1966088 | tf_op jit(solution)/shard_map/ppermute | solution.py:232
  137.9 0.0 collective-permute-done.3
  137.9 13.5 %all-gather.2 = bf16[1280,256]{1,0:T(8,128)(2,1)S(1)} all-gather(bf16[320,256]{1,0:T(8,128)(2,1)S(1)} %collective-permute-done.3), channel_id=4, replica_groups=mesh['x'=4,'zl'=8,'y'=4,'core'=2,'zh'=2] {'y'}, dimensions={0}, use_global_device_ids=true | all-gather | bytes 819200 | tf_op jit(solution)/shard_map/all_gather | solution.py:233
  151.4 1.9 %collective-permute-start.4 = (bf16[4,320,256]{2,1,0:T(8,128)(2,1)S(1)}, bf16[4,320,256]{2,1,0:T(8,128)(2,1)S(1)}, u32[]{:S(2)}, u32[]{:S(2)}) collective-permute-start(bf16[4,320,256]{2,1,0:T(8,128)(2,1)S(1)} %bitcast.13), channel_id=1, source_target_pairs={{0,2},{2,0},{1,3},{3,1},{4,6},{6,4},{5,7},{7,5},{8,10},{10,8},{9,1... | collective-permute-start | bytes 1966088 | tf_op jit(solution)/shard_map/ppermute | solution.py:234
  153.3 0.0 copy-done.3
  153.3 0.1 pad_add_fusion.place_ref
  153.4 16.9 %all-gather.10.cloned.1.call-done = bf16[32,160,256]{2,1,0:T(8,128)(2,1)} async-done(((bf16[4,160,256]{2,1,0:T(8,128)(2,1)}), bf16[32,160,256]{2,1,0:T(8,128)(2,1)}) %all-gather.10.cloned.1.call-update) | async-done | bytes 2621456 | tf_op jit(solution)/shard_map/all_gather | solution.py:221
  170.3 0.0 collective-permute-done.2.core_ref
  170.3 0.0 collective-permute-done.4.both_ref
  170.3 0.0 copy-start
  170.3 1.7 copy-done
  172.1 5.8 %shard_map.93 = bf16[320,320]{1,0:T(8,128)(2,1)} custom-call(s32[2]{0:T(128)S(1)} %pad_add_fusion.place_ref, bf16[4,320,256]{2,1,0:T(8,128)(2,1)S(1)} %bitcast.12, bf16[4,320,256]{2,1,0:T(8,128)(2,1)S(1)} %collective-permute-done.2.core_ref, bf16[4,320,256]{2,1,0:T(8,128)(2,1)S(1)} %bitcast.14, bf16[4,320,256]{2,1,0:T(8,128)(2,1)S(1)} %collective-permute-done.4.both_ref, ...), custom_call_target="tpu_custom_call" | custom-call | tf_op jit(solution)/shard_map/pallas_call | solution.py:166
  (12 shorter events, 0.2 us)
Async XLA Ops:
  6.5 69.6 %copy-start.2 = (s32[2560]{0:T(1024)S(1)}, s32[2560]{0:T(1024)}, u32[]{:S(2)}) copy-start(s32[2560]{0:T(1024)} %constant.25.clone) | copy-start | bytes 30724
  6.5 69.7 %copy-start.4 = (f32[256]{0:T(256)S(1)}, f32[256]{0:T(256)}, u32[]{:S(2)}) copy-start(f32[256]{0:T(256)} %param.14) | copy-start | bytes 3076
  6.5 80.1 %all-gather.8.cloned.1.call-start = ((), (), s32[]{:S(2)}) async-start(), calls=%async_computation.3 | async-start | bytes 2949120 | tf_op jit(solution)/shard_map/all_gather | solution.py:196
  20.2 18.7 %collective-permute-start = (f32[2,320]{1,0:T(2,128)S(1)}, f32[2,320]{1,0:T(2,128)S(1)}, u32[]{:S(2)}, u32[]{:S(2)}) collective-permute-start(f32[2,320]{1,0:T(2,128)S(1)} %reduce_sum.29), channel_id=1, source_target_pairs={{0,1},{1,0},{2,3},{3,2},{4,5},{5,4},{6,7},{7,6},{8,9},{9,8},{10,11... | collective-permute-start | bytes 7688 | tf_op jit(solution)/shard_map/ppermute | solution.py:211
  35.9 26.4 %collective-permute-start.1 = (bf16[160,256]{1,0:T(8,128)(2,1)}, bf16[160,256]{1,0:T(8,128)(2,1)S(1)}, u32[]{:S(2)}, u32[]{:S(2)}) collective-permute-start(bf16[160,256]{1,0:T(8,128)(2,1)} %bitcast.19), channel_id=1, source_target_pairs={{0,0},{1,32},{2,64},{3,96},{4,128},{5,160},{6,192},{7,224},{8,256}... | collective-permute-start | bytes 245768 | tf_op jit(solution)/shard_map/ppermute | solution.py:199
  39.6 22.6 %all-to-all-start.1 = ((f32[8,1,320]{2,1,0:T(1,128)}), f32[8,1,320]{2,1,0:T(1,128)S(1)}, u32[]{:S(2)}, u32[]{:S(2)}) async-start(f32[8,1,320]{2,1,0:T(1,128)} %broadcast_in_dim.33), calls=%async_computation.1 | async-start | bytes 24576 | tf_op jit(solution)/shard_map/all_to_all | solution.py:213
  47.7 122.6 %all-gather.10.cloned.1.call-start = ((), (), s32[]{:S(2)}) async-start(), calls=%async_computation.4 | async-start | bytes 2949120 | tf_op jit(solution)/shard_map/all_gather | solution.py:221
  86.7 1.7 copy-start.1
  96.5 56.8 %copy-start.3 = (f32[320]{0:T(512)S(1)}, f32[320]{0:T(512)}, u32[]{:S(2)}) copy-start(f32[320]{0:T(512)} %param.15) | copy-start | bytes 3844
  110.1 27.8 %collective-permute-start.3 = (bf16[320,256]{1,0:T(8,128)(2,1)S(1)}, bf16[320,256]{1,0:T(8,128)(2,1)S(1)}, u32[]{:S(2)}, u32[]{:S(2)}) collective-permute-start(bf16[320,256]{1,0:T(8,128)(2,1)S(1)} %shard_map.92), channel_id=1, source_target_pairs={{0,1},{1,0},{2,3},{3,2},{4,5},{5,4},{6,7},{7,6},{8,9},{9,8},{10,11... | collective-permute-start | bytes 491528 | tf_op jit(solution)/shard_map/ppermute | solution.py:230
  136.0 34.3 %collective-permute-start.2 = (bf16[4,320,256]{2,1,0:T(8,128)(2,1)S(1)}, bf16[4,320,256]{2,1,0:T(8,128)(2,1)S(1)}, u32[]{:S(2)}, u32[]{:S(2)}) collective-permute-start(bf16[4,320,256]{2,1,0:T(8,128)(2,1)S(1)} %bitcast.11), channel_id=1, source_target_pairs={{0,2},{2,0},{1,3},{3,1},{4,6},{6,4},{5,7},{7,5},{8,10},{10,8},{9,1... | collective-permute-start | bytes 1966088 | tf_op jit(solution)/shard_map/ppermute | solution.py:232
  151.4 18.9 %collective-permute-start.4 = (bf16[4,320,256]{2,1,0:T(8,128)(2,1)S(1)}, bf16[4,320,256]{2,1,0:T(8,128)(2,1)S(1)}, u32[]{:S(2)}, u32[]{:S(2)}) collective-permute-start(bf16[4,320,256]{2,1,0:T(8,128)(2,1)S(1)} %bitcast.13), channel_id=1, source_target_pairs={{0,2},{2,0},{1,3},{3,1},{4,6},{6,4},{5,7},{7,5},{8,10},{10,8},{9,1... | collective-permute-start | bytes 1966088 | tf_op jit(solution)/shard_map/ppermute | solution.py:234
  170.3 1.7 copy-start
Sparse Core Ops, SparseCore 0:
  9.4 77.1 all-gather.7
  88.8 81.5 all-gather.9

commit v8 on v7

v8 whole, which is shorter than its diff:
```python
import functools
import math

import jax
import jax.numpy as jnp
import numpy as np
from jax import lax
from jax.experimental import pallas as pl
from jax.experimental.pallas import tpu as pltpu
from jax.sharding import Mesh
from jax.sharding import PartitionSpec as P

HEAD_DIM = 128
EPSILON = 1e-06
BIAS = -1e30
F32 = jnp.float32
BF16 = jnp.bfloat16
AXES = ("xh", "xl", "zl", "y", "core", "zh")
SIZES = (2, 2, 8, 4, 2, 2)
X = ("xh", "xl")
SWAP = ((0, 1), (1, 0))
RING = [0, 2, 4, 6, 7, 5, 3, 1]
LINES = 32


def attention_kernel(
    q_ref, kv_ref, inverse_ref, bias_ref, gain_ref, out_ref, kt_ref, ve_ref
):
    factor = HEAD_DIM**-0.5 * math.log2(math.e)
    blocks, rows, _ = q_ref.shape
    keys = kv_ref.shape[0]
    row = lax.broadcasted_iota(jnp.int32, (HEAD_DIM, keys), 0)
    bias = jnp.where(row == 0, bias_ref[...], 0.0).astype(BF16)
    for h in range(2):
        columns = slice(h * HEAD_DIM, (h + 1) * HEAD_DIM)
        raw = kv_ref[:, columns].T.astype(F32)
        kt_ref[h, :HEAD_DIM, :] = (raw * inverse_ref[...] * gain_ref[columns, :]).astype(BF16)
        kt_ref[h, HEAD_DIM:, :] = bias
        ve_ref[h, :, :HEAD_DIM] = kv_ref[:, (2 + h) * HEAD_DIM : (3 + h) * HEAD_DIM]
        ve_ref[h, :, HEAD_DIM:] = jnp.ones((keys, HEAD_DIM), BF16)

    lane = lax.broadcasted_iota(jnp.int32, (rows, HEAD_DIM), 1)
    first = jnp.where(lane == 0, 1.0, 0.0).astype(BF16)
    for i in range(blocks // 2):
        stats = [jnp.zeros((rows, HEAD_DIM), F32) for _ in range(2)]
        for j in range(2):
            scores = []
            for h in range(2):
                query = jnp.concatenate(
                    [q_ref[2 * i + j, :, h * HEAD_DIM : (h + 1) * HEAD_DIM], first], axis=1
                )
                scores.append(jnp.dot(query, kt_ref[h], preferred_element_type=F32))
            for h in range(2):
                top = (jnp.max(scores[h], axis=1, keepdims=True) * factor).astype(BF16).astype(F32)
                weights = jnp.exp2(scores[h] * factor - top).astype(BF16)
                summed = jnp.dot(weights, ve_ref[h], preferred_element_type=F32)
                out_ref[2 * i + h, j * rows : (j + 1) * rows, :] = summed[:, :HEAD_DIM].astype(BF16)
                mass = summed[:, HEAD_DIM:]
                high = mass.astype(BF16).astype(F32)
                stats[h] = jnp.where(lane == 3 * j, top, stats[h])
                stats[h] = jnp.where(lane == 3 * j + 1, high, stats[h])
                stats[h] = jnp.where(lane == 3 * j + 2, mass - high, stats[h])
        for h in range(2):
            lines = stats[h].T[:8]
            full = rows // HEAD_DIM
            pieces = [lines[:, n * HEAD_DIM : (n + 1) * HEAD_DIM] for n in range(full)]
            rest = lines[:, full * HEAD_DIM :]
            pieces.append(jnp.pad(rest, ((0, 0), (0, (full + 1) * HEAD_DIM - rows))))
            pieces += [jnp.zeros((8, HEAD_DIM), F32)] * (LINES // 8 - len(pieces))
            out_ref[2 * i + h, 2 * rows :, :] = jnp.concatenate(pieces).astype(BF16)


def attention(queries, keys_values, inverse, bias, gain):
    blocks, rows, width = queries.shape
    keys = keys_values.shape[0]
    shape = (blocks, 2 * rows + LINES, HEAD_DIM)
    return pl.pallas_call(
        attention_kernel,
        grid=(1,),
        in_specs=[
            pl.BlockSpec((blocks, rows, width), lambda i: (0, 0, 0)),
            pl.BlockSpec((keys, 2 * width), lambda i: (0, 0)),
            pl.BlockSpec((1, keys), lambda i: (0, 0)),
            pl.BlockSpec((1, keys), lambda i: (0, 0)),
            pl.BlockSpec((width, 1), lambda i: (0, 0)),
        ],
        out_specs=pl.BlockSpec(shape, lambda i: (0, 0, 0)),
        out_shape=jax.ShapeDtypeStruct(shape, BF16),
        scratch_shapes=[
            pltpu.VMEM((2, 2 * HEAD_DIM, keys), BF16),
            pltpu.VMEM((2, keys, 2 * HEAD_DIM), BF16),
        ],
        compiler_params=pltpu.CompilerParams(vmem_limit_bytes=48 << 20),
        cost_estimate=pl.CostEstimate(
            flops=8 * blocks * rows * keys * width,
            bytes_accessed=4 << 20,
            transcendentals=2 * blocks * rows * keys,
        ),
    )(queries, keys_values, inverse, bias, gain)


def join_kernel(parts_ref, out_ref):
    count = parts_ref.shape[0]
    rows = out_ref.shape[0] // 2
    lines = []
    for i in range(count):
        packed = parts_ref[i, 2 * rows :, :].astype(F32)
        lines.append(jnp.concatenate([packed[8 * n : 8 * n + 8] for n in range(LINES // 8)], axis=1))
    shares = []
    for j in range(2):
        tops = [line[3 * j : 3 * j + 1] for line in lines]
        highest = functools.reduce(jnp.maximum, tops)
        weights = [jnp.exp2(top - highest) for top in tops]
        mass = sum(
            w * (line[3 * j + 1 : 3 * j + 2] + line[3 * j + 2 : 3 * j + 3])
            for w, line in zip(weights, lines)
        )
        mass = jnp.where(mass == 0.0, 1.0, mass)
        shares += [w / mass for w in weights]
    spread = jnp.zeros((HEAD_DIM - 2 * count, lines[0].shape[1]), F32)
    columns = jnp.concatenate(shares + [spread]).T
    for j in range(2):
        span = slice(j * rows, (j + 1) * rows)
        total = jnp.zeros((rows, HEAD_DIM), F32)
        for i in range(count):
            share = columns[:rows, j * count + i : j * count + i + 1]
            total = total + share * parts_ref[i, span, :].astype(F32)
        out_ref[span, :] = total.astype(BF16)


def join(parts):
    return pl.pallas_call(
        join_kernel,
        out_shape=jax.ShapeDtypeStruct((parts.shape[1] - LINES, HEAD_DIM), BF16),
        compiler_params=pltpu.CompilerParams(vmem_limit_bytes=32 << 20),
    )(parts)


def project_kernel(
    place_ref, own_ref, core_ref, zh_ref, both_ref, weight_ref, kept_ref, sent_ref, total_ref
):
    core, zh, half = place_ref[0], place_ref[1], place_ref[2]
    step = pl.program_id(0)
    rows = kept_ref.shape[0]
    pieces, blocks = [], []
    for ref, a, b in (
        (own_ref, core, zh),
        (core_ref, 1 - core, zh),
        (zh_ref, core, 1 - zh),
        (both_ref, 1 - core, 1 - zh),
    ):
        pair = a * 2 + b
        pieces.append(ref[0])
        blocks.append(jnp.concatenate([weight_ref[pair, 0], weight_ref[7 - pair, 0]]))
    total = lax.dot_general(
        jnp.concatenate(pieces, axis=1),
        jnp.concatenate(blocks, axis=1),
        (((1,), (1,)), ((), ())),
        preferred_element_type=F32,
    )

    @pl.when(step == 0)
    def _():
        total_ref[...] = total

    @pl.when(step > 0)
    def _():
        total_ref[...] += total

    @pl.when(step == pl.num_programs(0) - 1)
    def _():
        kept_ref[...] = total_ref[pl.ds(pl.multiple_of(half * rows, 16), rows), :]
        sent_ref[...] = total_ref[pl.ds(pl.multiple_of((1 - half) * rows, 16), rows), :].astype(BF16)


def project(place, pieces, weights):
    groups, rows, width = pieces[0].shape
    blocks, _, columns, _ = weights.shape
    shape = (rows // 2, 2 * columns)
    return pl.pallas_call(
        project_kernel,
        grid=(groups,),
        in_specs=[pl.BlockSpec(memory_space=pltpu.SMEM)]
        + [pl.BlockSpec((1, rows, width), lambda i: (i, 0, 0))] * 4
        + [pl.BlockSpec((blocks, 1, columns, width), lambda i: (0, i, 0, 0))],
        out_specs=[pl.BlockSpec(shape, lambda i: (0, 0))] * 2,
        out_shape=[jax.ShapeDtypeStruct(shape, F32), jax.ShapeDtypeStruct(shape, BF16)],
        scratch_shapes=[pltpu.VMEM((rows, 2 * columns), F32)],
        compiler_params=pltpu.CompilerParams(vmem_limit_bytes=32 << 20),
    )(place, *pieces, weights)


def weight_routes():
    routes = []
    sizes = (4, 8, 4, 2, 2)
    for x, zl, y, a, b in np.ndindex(*sizes):
        c, z, r = zl // 4, zl // 2 % 2, zl % 2
        target = (y, a * 4 + b * 2 + r, x, c, z)
        routes.append(
            (int(np.ravel_multi_index((x, zl, y, a, b), sizes)), int(np.ravel_multi_index(target, sizes)))
        )
    return routes


def local(queries, keys, values, out_weight, q_gain, k_gain, gate, valid_count):
    rows, width = queries.shape
    features = width * 16
    gathered = lax.all_gather(
        jnp.concatenate([keys, values], axis=1), "zl", axis=0, tiled=True, axis_index_groups=[RING]
    )
    weights = lax.ppermute(out_weight.T, AXES, weight_routes())

    squares = jnp.stack(
        [
            jnp.sum(jnp.square(queries.astype(F32)), axis=1),
            jnp.sum(jnp.square(keys.astype(F32)), axis=1),
        ]
    )
    near = lax.all_to_all(
        jnp.broadcast_to(squares[None], (8, 2, rows)), ("y", "core"), 0, 0, tiled=True
    )
    near = jnp.sum(near, axis=0)
    totals = near + lax.ppermute(near, "zh", SWAP)
    inverse = lax.rsqrt(totals / features + EPSILON)
    key_inverse = lax.all_to_all(
        jnp.broadcast_to(inverse[1][None], (8, rows)), "zl", 0, 0, tiled=True
    )
    key_inverse = jnp.concatenate([key_inverse[z] for z in RING])[None, :]
    query_norm = (queries.astype(F32) * inverse[0][:, None] * q_gain[None, :]).astype(BF16)
    query_all = lax.all_gather(query_norm, X, axis=0, tiled=False)
    query_all, key_inverse, weights = lax.optimization_barrier((query_all, key_inverse, weights))
    halves = [weights[:, :HEAD_DIM], weights[:, HEAD_DIM:]]
    weights = lax.all_to_all(jnp.stack(halves + halves), X, 0, 0, tiled=True)
    weights = lax.all_gather(weights, "zl", axis=0, tiled=False, axis_index_groups=[RING])

    place_x = lax.axis_index("xh") * 2 + lax.axis_index("xl")
    limit = valid_count[0] - place_x * (8 * rows)
    starts = np.repeat(np.asarray(RING, np.int32) * rows, rows)
    position = jnp.asarray(starts + np.tile(np.arange(rows, dtype=np.int32), 8))
    bias = jnp.where(position < limit, 0.0, BIAS).astype(F32)[None, :]
    parts = attention(query_all, gathered, key_inverse, bias, k_gain[:, None])
    parts = lax.all_to_all(parts, X, 0, 0, tiled=True)
    own = join(parts)
    across = lax.ppermute(own, "zh", SWAP)
    own_y = lax.all_gather(own, "y", axis=0, tiled=False)
    beside_y = lax.ppermute(own_y, "core", SWAP)
    across_y = lax.all_gather(across, "y", axis=0, tiled=False)
    both_y = lax.ppermute(across_y, "core", SWAP)
    place = jnp.stack([lax.axis_index(n) for n in ("core", "zh", "xl")]).astype(jnp.int32)
    kept, sent = project(place, (own_y, beside_y, across_y, both_y), weights)
    summed = kept + lax.ppermute(sent, "xl", SWAP).astype(F32)
    return (gate[None, :] * summed).astype(BF16)


def solution(mesh):
    fine = Mesh(mesh.devices.reshape(SIZES), AXES)
    tokens, features = ("xh", "xl", "zl"), ("y", "core", "zh")
    placed = (
        P(tokens, features),
        P(tokens, features),
        P(tokens, features),
        P(features, tokens),
        P(features),
        P(features),
        P(features),
        P(),
    )
    return jax.shard_map(
        local, mesh=fine, in_specs=placed, out_specs=P(tokens, features), check_vma=False
    )
```

time: 186 us -> 186 us (level)
  the two profiles are of different devices: /device:TPU:6 before, /device:TPU:96 now
where the time goes in v8:
time: 186 us
  blocking collectives  67.3 us (36%)
  starting transfers between devices  41.8 us (22%)
  waiting for transfers between devices  39.1 us (21%)
  between operations  14.3 us (8%)
  Pallas kernels  12 us (6%)
  other arithmetic  6.5 us (3%)
  local copies, waits for them, and re-layouts  4.67 us (3%)
    all_to_all x1, blocking collectives, local(): parts = lax.all_to_all(parts, X, 0, 0, tiled=True)  15.3 us
    all_gather x1, blocking collectives, local(): query_all = lax.all_gather(query_norm, X, axis=0, tiled=False)  14.4 us
    all_gather x1, blocking collectives, local(): across_y = lax.all_gather(across, 'y', axis=0, tiled=False)  14.4 us
    all_gather x1, blocking collectives, local(): own_y = lax.all_gather(own, 'y', axis=0, tiled=False)  13.6 us
    ppermute x1, starting transfers between devices, local(): totals = near + lax.ppermute(near, 'zh', SWAP)  13 us
    all_gather x1, waiting for transfers between devices, local(): lax.all_gather(jnp.concatenate([keys, values], axis=1), 'zl', axis=0, til...  12.9 us
    ppermute x1, waiting for transfers between devices, local(): across = lax.ppermute(own, 'zh', SWAP)  11 us
    all_to_all x1, starting transfers between devices, local(): lax.all_to_all(jnp.broadcast_to(inverse[1][None], (8, rows)), 'zl', 0, 0,...  11 us
  transfers between devices with their start and end apart: 10, of which 5 were waited for; matrix products, arithmetic and copies ran while one was open for 3% of the time, Pallas kernels for 5%

profile of v8, /device:TPU:96, one launch (start us, length us, event | category | flops | bytes accessed | tf_op | source)
XLA Modules:
  0.0 185.6 jit_solution(6292347217816272384)
XLA Ops:
  6.5 0.0 copy-start.3
  6.5 0.0 copy-start.5
  6.5 0.0 all-gather.7.cloned.1.call-start
  6.5 1.8 pad_maximum_fusion
  8.3 0.0 all-gather.7.cloned.1.call-update
  8.3 1.1 fusion
  9.4 1.1 multiply_reduce_fusion
  10.5 9.7 %all_to_all.21 = f32[8,2,320]{2,1,0:T(2,128)S(1)} all-to-all(f32[8,2,320]{2,1,0:T(2,128)S(1)} %broadcast_in_dim.30), channel_id=1, replica_groups=mesh['xh'=2,'xl'=2,'zl'=8,'y'=4,'core'=2,'zh'=2] {'y','core'}, dimensions={0} | all-to-all | bytes 40960 | tf_op jit(solution)/shard_map/all_to_all | solution.py:219
  20.2 13.0 %collective-permute-start = (f32[2,320]{1,0:T(2,128)S(1)}, f32[2,320]{1,0:T(2,128)S(1)}, u32[]{:S(2)}, u32[]{:S(2)}) collective-permute-start(f32[2,320]{1,0:T(2,128)S(1)} %reduce_sum.29), channel_id=1, source_target_pairs={{0,1},{1,0},{2,3},{3,2},{4,5},{5,4},{6,7},{7,6},{8,9},{9,8},{10,11... | collective-permute-start | bytes 7688 | tf_op jit(solution)/shard_map/ppermute | solution.py:223
  33.2 1.9 %collective-permute-start.1 = (bf16[160,256]{1,0:T(8,128)(2,1)}, bf16[160,256]{1,0:T(8,128)(2,1)S(1)}, u32[]{:S(2)}, u32[]{:S(2)}) collective-permute-start(bf16[160,256]{1,0:T(8,128)(2,1)} %bitcast.22), channel_id=1, source_target_pairs={{0,0},{1,32},{2,64},{3,96},{4,128},{5,160},{6,192},{7,224},{8,256}... | collective-permute-start | bytes 245768 | tf_op jit(solution)/shard_map/ppermute | solution.py:211
  35.2 0.0 collective-permute-done
  35.2 0.6 broadcast_in_dim.31
  35.8 11.0 %all-to-all-start.1 = ((f32[8,1,320]{2,1,0:T(1,128)}), f32[8,1,320]{2,1,0:T(1,128)S(1)}, u32[]{:S(2)}, u32[]{:S(2)}) async-start(f32[8,1,320]{2,1,0:T(1,128)} %broadcast_in_dim.31), calls=%async_computation.1 | async-start | bytes 24576 | tf_op jit(solution)/shard_map/all_to_all | solution.py:225
  46.8 1.0 fusion.2
  47.9 14.4 %all-gather = bf16[1280,256]{1,0:T(8,128)(2,1)S(1)} all-gather(bf16[320,256]{1,0:T(8,128)(2,1)S(1)} %fusion.2), channel_id=2, replica_groups=mesh['xh'=2,'xl'=2,'zl'=8,'y'=4,'core'=2,'zh'=2] {'xh','xl'}, dimensions={0}, use_global_device_ids=true | all-gather | bytes 819200 | tf_op jit(solution)/shard_map/all_gather | solution.py:230
  62.3 0.0 all-to-all-done.1
  62.3 0.1 concatenate.6
  62.4 0.0 collective-permute-done.1
  62.4 0.7 pad_maximum_fusion.1
  63.1 3.3 %all-to-all-start.3 = ((bf16[4,160,128]{2,1,0:T(8,128)(2,1)}), bf16[4,160,128]{2,1,0:T(8,128)(2,1)S(1)}, u32[]{:S(2)}, u32[]{:S(2)}) async-start(bf16[4,160,128]{2,1,0:T(8,128)(2,1)} %pad_maximum_fusion.1), calls=%async_computation.3 | async-start | bytes 327680 | tf_op jit(solution)/shard_map/all_to_all | solution.py:233
  66.5 0.0 all-gather.9.cloned.1.call-start
  67.2 5.4 %all-to-all-done.3 = bf16[4,160,128]{2,1,0:T(8,128)(2,1)S(1)} async-done(((bf16[4,160,128]{2,1,0:T(8,128)(2,1)}), bf16[4,160,128]{2,1,0:T(8,128)(2,1)S(1)}, u32[]{:S(2)}, u32[]{:S(2)}) %all-to-all-start.3) | async-done | bytes 163872 | tf_op jit(solution)/shard_map/all_to_all | solution.py:233
  72.6 0.0 copy-start.2
  72.6 0.7 copy-done.2
  73.3 0.0 all-gather.9.cloned.1.call-update
  73.3 0.0 copy-done.3
  73.3 0.0 copy-done.5
  73.3 0.1 copy.14.gain_ref
  73.5 12.9 %all-gather.7.cloned.1.call-done.kv_ref = bf16[2560,512]{1,0:T(8,128)(2,1)} async-done(((bf16[320,512]{1,0:T(8,128)(2,1)}), bf16[2560,512]{1,0:T(8,128)(2,1)}) %all-gather.7.cloned.1.call-update) | async-done | bytes 2621456 | tf_op jit(solution)/shard_map/all_gather | solution.py:208
  86.4 0.0 copy-start.1
  86.4 1.7 copy-done.1
  88.2 8.1 %shard_map.91 = bf16[4,672,128]{2,1,0:T(8,128)(2,1)S(1)} custom-call(bf16[4,320,256]{2,1,0:T(8,128)(2,1)S(1)} %bitcast.20, bf16[2560,512]{1,0:T(8,128)(2,1)S(1)} %copy-done.1, f32[1,2560]{1,0:T(1,128)S(1)} %broadcast_in_dim.32.inverse_ref, f32[1,2560]{1,0:T(1,128)S(1)} %broadcast_in_dim.35.bias_ref, f32[256,1]{1,0:T(8,128)S(1)} %copy.14.gain_ref), custom_call_target="tpu_custom_call" | custom-call | flops 6710886400 | bytes 4194304 | tf_op jit(solution)/shard_map/pallas_call | solution.py:77
  96.3 15.3 %all_to_all.22.parts_ref = bf16[4,672,128]{2,1,0:T(8,128)(2,1)S(1)} all-to-all(bf16[4,672,128]{2,1,0:T(8,128)(2,1)S(1)} %shard_map.91), channel_id=1, replica_groups=mesh['xh'=2,'xl'=2,'zl'=8,'y'=4,'core'=2,'zh'=2] {'xh','xl'}, dimensions={0} | all-to-all | bytes 1376256 | tf_op jit(solution)/shard_map/all_to_all | solution.py:242
  111.6 0.6 shard_map.92
  112.2 0.0 copy-start.4
  112.2 6.5 %collective-permute-start.3 = (bf16[640,128]{1,0:T(8,128)(2,1)S(1)}, bf16[640,128]{1,0:T(8,128)(2,1)S(1)}, u32[]{:S(2)}, u32[]{:S(2)}) collective-permute-start(bf16[640,128]{1,0:T(8,128)(2,1)S(1)} %shard_map.92), channel_id=1, source_target_pairs={{0,1},{1,0},{2,3},{3,2},{4,5},{5,4},{6,7},{7,6},{8,9},{9,8},{10,11... | collective-permute-start | bytes 491528 | tf_op jit(solution)/shard_map/ppermute | solution.py:244
  118.7 13.6 %all-gather.1 = bf16[2560,128]{1,0:T(8,128)(2,1)S(1)} all-gather(bf16[640,128]{1,0:T(8,128)(2,1)S(1)} %shard_map.92), channel_id=3, replica_groups=mesh['xh'=2,'xl'=2,'zl'=8,'y'=4,'core'=2,'zh'=2] {'y'}, dimensions={0}, use_global_device_ids=true | all-gather | bytes 819200 | tf_op jit(solution)/shard_map/all_gather | solution.py:245
  132.2 1.9 %collective-permute-start.2 = (bf16[4,640,128]{2,1,0:T(8,128)(2,1)S(1)}, bf16[4,640,128]{2,1,0:T(8,128)(2,1)S(1)}, u32[]{:S(2)}, u32[]{:S(2)}) collective-permute-start(bf16[4,640,128]{2,1,0:T(8,128)(2,1)S(1)} %bitcast.15), channel_id=1, source_target_pairs={{0,2},{2,0},{1,3},{3,1},{4,6},{6,4},{5,7},{7,5},{8,10},{10,8},{9,1... | collective-permute-start | bytes 1966088 | tf_op jit(solution)/shard_map/ppermute | solution.py:246
  134.2 11.0 %collective-permute-done.3 = bf16[640,128]{1,0:T(8,128)(2,1)S(1)} collective-permute-done((bf16[640,128]{1,0:T(8,128)(2,1)S(1)}, bf16[640,128]{1,0:T(8,128)(2,1)S(1)}, u32[]{:S(2)}, u32[]{:S(2)}) %collective-permute-start.3) | collective-permute-done | bytes 163872 | tf_op jit(solution)/shard_map/ppermute | solution.py:244
  145.2 14.4 %all-gather.2 = bf16[2560,128]{1,0:T(8,128)(2,1)S(1)} all-gather(bf16[640,128]{1,0:T(8,128)(2,1)S(1)} %collective-permute-done.3), channel_id=4, replica_groups=mesh['xh'=2,'xl'=2,'zl'=8,'y'=4,'core'=2,'zh'=2] {'y'}, dimensions={0}, use_global_device_ids=true | all-gather | bytes 819200 | tf_op jit(solution)/shard_map/all_gather | solution.py:247
  159.5 1.9 %collective-permute-start.4 = (bf16[4,640,128]{2,1,0:T(8,128)(2,1)S(1)}, bf16[4,640,128]{2,1,0:T(8,128)(2,1)S(1)}, u32[]{:S(2)}, u32[]{:S(2)}) collective-permute-start(bf16[4,640,128]{2,1,0:T(8,128)(2,1)S(1)} %bitcast.17), channel_id=1, source_target_pairs={{0,2},{2,0},{1,3},{3,1},{4,6},{6,4},{5,7},{7,5},{8,10},{10,8},{9,1... | collective-permute-start | bytes 1966088 | tf_op jit(solution)/shard_map/ppermute | solution.py:248
  161.5 0.1 pad_add_fusion.place_ref
  161.5 0.0 all-gather.9.cloned.1.call-done
  161.5 0.0 collective-permute-done.2.core_ref
  161.5 2.0 %collective-permute-done.4.both_ref = bf16[4,640,128]{2,1,0:T(8,128)(2,1)S(1)} collective-permute-done((bf16[4,640,128]{2,1,0:T(8,128)(2,1)S(1)}, bf16[4,640,128]{2,1,0:T(8,128)(2,1)S(1)}, u32[]{:S(2)}, u32[]{:S(2)}) %collective-permute-start.4) | collective-permute-done | bytes 655392 | tf_op jit(solution)/shard_map/ppermute | solution.py:248
  163.5 0.0 copy-start
  163.5 1.3 copy-done
  164.8 3.2 %shard_map.93 = (f32[320,320]{1,0:T(8,128)S(1)}, bf16[320,320]{1,0:T(8,128)(2,1)S(1)}) custom-call(s32[3]{0:T(128)S(1)} %pad_add_fusion.place_ref, bf16[4,640,128]{2,1,0:T(8,128)(2,1)S(1)} %bitcast.16, bf16[4,640,128]{2,1,0:T(8,128)(2,1)S(1)} %collective-permute-done.2.core_ref, bf16[4,640,128]{2,1,0:T(8,128)(2,1)S(1)} %bitcast.18, ...), custom_call_target="tpu_custom_call" | custom-call | tf_op jit(solution)/shard_map/pallas_call | solution.py:180
  168.1 2.2 %collective-permute-start.5 = (bf16[320,320]{1,0:T(8,128)(2,1)S(1)}, bf16[320,320]{1,0:T(8,128)(2,1)S(1)}, u32[]{:S(2)}, u32[]{:S(2)}) collective-permute-start(bf16[320,320]{1,0:T(8,128)(2,1)S(1)} %get-tuple-element.14), channel_id=1, source_target_pairs={{0,128},{128,0},{1,129},{129,1},{2,130},{130,2},{3,131},{131,3},{4... | collective-permute-start | bytes 614408 | tf_op jit(solution)/shard_map/ppermute | solution.py:251
  170.2 7.7 %collective-permute-done.5 = bf16[320,320]{1,0:T(8,128)(2,1)S(1)} collective-permute-done((bf16[320,320]{1,0:T(8,128)(2,1)S(1)}, bf16[320,320]{1,0:T(8,128)(2,1)S(1)}, u32[]{:S(2)}, u32[]{:S(2)}) %collective-permute-start.5) | collective-permute-done | bytes 204832 | tf_op jit(solution)/shard_map/ppermute | solution.py:251
  178.0 0.0 copy-done.4
  178.0 0.8 multiply_convert_fusion
  (12 shorter events, 0.2 us)
Async XLA Ops:
  6.5 66.8 %copy-start.3 = (s32[2560]{0:T(1024)S(1)}, s32[2560]{0:T(1024)}, u32[]{:S(2)}) copy-start(s32[2560]{0:T(1024)} %constant.29.clone) | copy-start | bytes 30724
  6.5 66.8 %copy-start.5 = (f32[256]{0:T(256)S(1)}, f32[256]{0:T(256)}, u32[]{:S(2)}) copy-start(f32[256]{0:T(256)} %param.14) | copy-start | bytes 3076
  6.5 79.9 %all-gather.7.cloned.1.call-start = ((), (), s32[]{:S(2)}) async-start(), calls=%async_computation.4 | async-start | bytes 2949120 | tf_op jit(solution)/shard_map/all_gather | solution.py:208
  20.2 15.0 %collective-permute-start = (f32[2,320]{1,0:T(2,128)S(1)}, f32[2,320]{1,0:T(2,128)S(1)}, u32[]{:S(2)}, u32[]{:S(2)}) collective-permute-start(f32[2,320]{1,0:T(2,128)S(1)} %reduce_sum.29), channel_id=1, source_target_pairs={{0,1},{1,0},{2,3},{3,2},{4,5},{5,4},{6,7},{7,6},{8,9},{9,8},{10,11... | collective-permute-start | bytes 7688 | tf_op jit(solution)/shard_map/ppermute | solution.py:223
  33.2 29.2 %collective-permute-start.1 = (bf16[160,256]{1,0:T(8,128)(2,1)}, bf16[160,256]{1,0:T(8,128)(2,1)S(1)}, u32[]{:S(2)}, u32[]{:S(2)}) collective-permute-start(bf16[160,256]{1,0:T(8,128)(2,1)} %bitcast.22), channel_id=1, source_target_pairs={{0,0},{1,32},{2,64},{3,96},{4,128},{5,160},{6,192},{7,224},{8,256}... | collective-permute-start | bytes 245768 | tf_op jit(solution)/shard_map/ppermute | solution.py:211
  35.8 26.5 %all-to-all-start.1 = ((f32[8,1,320]{2,1,0:T(1,128)}), f32[8,1,320]{2,1,0:T(1,128)S(1)}, u32[]{:S(2)}, u32[]{:S(2)}) async-start(f32[8,1,320]{2,1,0:T(1,128)} %broadcast_in_dim.31), calls=%async_computation.1 | async-start | bytes 24576 | tf_op jit(solution)/shard_map/all_to_all | solution.py:225
  63.1 9.5 %all-to-all-start.3 = ((bf16[4,160,128]{2,1,0:T(8,128)(2,1)}), bf16[4,160,128]{2,1,0:T(8,128)(2,1)S(1)}, u32[]{:S(2)}, u32[]{:S(2)}) async-start(bf16[4,160,128]{2,1,0:T(8,128)(2,1)} %pad_maximum_fusion.1), calls=%async_computation.3 | async-start | bytes 327680 | tf_op jit(solution)/shard_map/all_to_all | solution.py:233
  66.5 95.1 %all-gather.9.cloned.1.call-start = ((), (), s32[]{:S(2)}) async-start(), calls=%async_computation.5 | async-start | bytes 1474560 | tf_op jit(solution)/shard_map/all_gather | solution.py:234
  72.6 0.7 copy-start.2
  86.4 1.7 copy-start.1
  112.2 65.8 %copy-start.4 = (f32[320]{0:T(512)S(1)}, f32[320]{0:T(512)}, u32[]{:S(2)}) copy-start(f32[320]{0:T(512)} %param.15) | copy-start | bytes 3844
  112.2 33.0 %collective-permute-start.3 = (bf16[640,128]{1,0:T(8,128)(2,1)S(1)}, bf16[640,128]{1,0:T(8,128)(2,1)S(1)}, u32[]{:S(2)}, u32[]{:S(2)}) collective-permute-start(bf16[640,128]{1,0:T(8,128)(2,1)S(1)} %shard_map.92), channel_id=1, source_target_pairs={{0,1},{1,0},{2,3},{3,2},{4,5},{5,4},{6,7},{7,6},{8,9},{9,8},{10,11... | collective-permute-start | bytes 491528 | tf_op jit(solution)/shard_map/ppermute | solution.py:244
  132.2 29.3 %collective-permute-start.2 = (bf16[4,640,128]{2,1,0:T(8,128)(2,1)S(1)}, bf16[4,640,128]{2,1,0:T(8,128)(2,1)S(1)}, u32[]{:S(2)}, u32[]{:S(2)}) collective-permute-start(bf16[4,640,128]{2,1,0:T(8,128)(2,1)S(1)} %bitcast.15), channel_id=1, source_target_pairs={{0,2},{2,0},{1,3},{3,1},{4,6},{6,4},{5,7},{7,5},{8,10},{10,8},{9,1... | collective-permute-start | bytes 1966088 | tf_op jit(solution)/shard_map/ppermute | solution.py:246
  159.5 4.0 %collective-permute-start.4 = (bf16[4,640,128]{2,1,0:T(8,128)(2,1)S(1)}, bf16[4,640,128]{2,1,0:T(8,128)(2,1)S(1)}, u32[]{:S(2)}, u32[]{:S(2)}) collective-permute-start(bf16[4,640,128]{2,1,0:T(8,128)(2,1)S(1)} %bitcast.17), channel_id=1, source_target_pairs={{0,2},{2,0},{1,3},{3,1},{4,6},{6,4},{5,7},{7,5},{8,10},{10,8},{9,1... | collective-permute-start | bytes 1966088 | tf_op jit(solution)/shard_map/ppermute | solution.py:248
  163.5 1.3 copy-start
  168.1 9.9 %collective-permute-start.5 = (bf16[320,320]{1,0:T(8,128)(2,1)S(1)}, bf16[320,320]{1,0:T(8,128)(2,1)S(1)}, u32[]{:S(2)}, u32[]{:S(2)}) collective-permute-start(bf16[320,320]{1,0:T(8,128)(2,1)S(1)} %get-tuple-element.14), channel_id=1, source_target_pairs={{0,128},{128,0},{1,129},{129,1},{2,130},{130,2},{3,131},{131,3},{4... | collective-permute-start | bytes 614408 | tf_op jit(solution)/shard_map/ppermute | solution.py:251
Sparse Core Ops, SparseCore 0:
  9.4 76.9 all-gather.6
  88.5 61.4 all-gather.8

commit v9 on v7

--- a/solution.py
+++ b/solution.py
@@ -19,6 +19,7 @@
 SIZES = (4, 8, 4, 2, 2)
 SWAP = ((0, 1), (1, 0))
 RING = [0, 2, 4, 6, 7, 5, 3, 1]
+LATE = 112
 
 
 def attention_kernel(
@@ -126,57 +127,66 @@
 
 
 def project_kernel(
-    place_ref, own_ref, core_ref, zh_ref, both_ref, weight_ref, gate_ref, out_ref, total_ref
+    place_ref, own_ref, core_ref, zh_ref, both_ref, late_ref, early_ref, gate_ref, out_ref, total_ref
 ):
-    columns = weight_ref.shape[2]
     core, zh = place_ref[0], place_ref[1]
     step = pl.program_id(0)
-    for r in range(2):
-        total = jnp.zeros((out_ref.shape[0], columns), F32)
-        for ref, a, b in (
-            (own_ref, core, zh),
-            (core_ref, 1 - core, zh),
-            (zh_ref, core, 1 - zh),
-            (both_ref, 1 - core, 1 - zh),
-        ):
-            pair = a * 2 + b
-            block = weight_ref[pair if r == 0 else 7 - pair, 0]
-            total = total + lax.dot_general(
-                ref[0], block, (((1,), (1,)), ((), ())), preferred_element_type=F32
-            )
-
-        @pl.when(step == 0)
-        def _():
-            total_ref[r] = total
-
-        @pl.when(step > 0)
-        def _():
-            total_ref[r] += total
+    few = out_ref.shape[1] // 2 - LATE
+    pieces, blocks = [], []
+    for ref, a, b in (
+        (own_ref, core, zh),
+        (core_ref, 1 - core, zh),
+        (zh_ref, core, 1 - zh),
+        (both_ref, 1 - core, 1 - zh),
+    ):
+        pair = a * 2 + b
+        pieces.append(ref[0])
+        block = []
+        for r in range(2):
+            start = pl.multiple_of(LATE + (2 * pair + r) * few, 16)
+            block += [
+                late_ref[pair if r == 0 else 7 - pair, 0],
+                early_ref[0, pl.ds(start, few), :],
+            ]
+        blocks.append(jnp.concatenate(block))
+    total = lax.dot_general(
+        jnp.concatenate(pieces, axis=1),
+        jnp.concatenate(blocks, axis=1),
+        (((1,), (1,)), ((), ())),
+        preferred_element_type=F32,
+    )
+
+    @pl.when(step == 0)
+    def _():
+        total_ref[...] = total
+
+    @pl.when(step > 0)
+    def _():
+        total_ref[...] += total
 
     @pl.when(step == pl.num_programs(0) - 1)
     def _():
-        for r in range(2):
-            span = slice(r * columns, (r + 1) * columns)
-            out_ref[:, span] = (total_ref[r] * gate_ref[:, span]).astype(BF16)
-
-
-def project(place, pieces, weights, gate):
+        out_ref[...] = (total_ref[...] * gate_ref[...]).astype(BF16)
+
+
+def project(place, pieces, late, early, gate):
     groups, rows, width = pieces[0].shape
-    blocks, _, columns, _ = weights.shape
+    shape = (rows, gate.shape[1])
     return pl.pallas_call(
         project_kernel,
         grid=(groups,),
         in_specs=[pl.BlockSpec(memory_space=pltpu.SMEM)]
         + [pl.BlockSpec((1, rows, width), lambda i: (i, 0, 0))] * 4
         + [
-            pl.BlockSpec((blocks, 1, columns, width), lambda i: (0, i, 0, 0)),
-            pl.BlockSpec((1, 2 * columns), lambda i: (0, 0)),
+            pl.BlockSpec((late.shape[0], 1) + late.shape[2:], lambda i: (0, i, 0, 0)),
+            pl.BlockSpec((1,) + early.shape[1:], lambda i: (i, 0, 0)),
+            pl.BlockSpec((1, gate.shape[1]), lambda i: (0, 0)),
         ],
-        out_specs=pl.BlockSpec((rows, 2 * columns), lambda i: (0, 0)),
-        out_shape=jax.ShapeDtypeStruct((rows, 2 * columns), BF16),
-        scratch_shapes=[pltpu.VMEM((2, rows, columns), F32)],
+        out_specs=pl.BlockSpec(shape, lambda i: (0, 0)),
+        out_shape=jax.ShapeDtypeStruct(shape, BF16),
+        scratch_shapes=[pltpu.VMEM(shape, F32)],
         compiler_params=pltpu.CompilerParams(vmem_limit_bytes=32 << 20),
-    )(place, *pieces, weights, gate)
+    )(place, *pieces, late, early, gate)
 
 
 def weight_routes():
@@ -216,9 +226,17 @@
     key_inverse = jnp.concatenate([key_inverse[z] for z in RING])[None, :]
     query_norm = (queries.astype(F32) * inverse[0][:, None] * q_gain[None, :]).astype(BF16)
     query_all = lax.all_gather(query_norm, "x", axis=0, tiled=False)
-    query_all, key_inverse, weights = lax.optimization_barrier((query_all, key_inverse, weights))
-    weights = lax.all_gather(weights, "x", axis=0, tiled=False)
-    weights = lax.all_gather(weights, "zl", axis=0, tiled=False, axis_index_groups=[RING])
+    columns = out_weight.shape[1]
+    early = lax.all_to_all(
+        jnp.broadcast_to(weights[None, LATE:], (8, columns - LATE, width)), "zl", 0, 0, tiled=True
+    )
+    query_all, key_inverse, early = lax.optimization_barrier((query_all, key_inverse, early))
+    along_x = lax.all_gather(
+        jnp.concatenate([weights[:LATE], early.reshape(-1, width)]), "x", axis=0, tiled=False
+    )
+    late = lax.all_gather(
+        along_x[:, :LATE], "zl", axis=0, tiled=False, axis_index_groups=[RING]
+    )
 
     limit = valid_count[0] - lax.axis_index("x") * (8 * rows)
     starts = np.repeat(np.asarray(RING, np.int32) * rows, rows)
@@ -233,7 +251,7 @@
     across_y = lax.all_gather(across, "y", axis=0, tiled=False)
     both_y = lax.ppermute(across_y, "core", SWAP)
     place = jnp.stack([lax.axis_index("core"), lax.axis_index("zh")]).astype(jnp.int32)
-    return project(place, (own_y, beside_y, across_y, both_y), weights, gate[None, :])
+    return project(place, (own_y, beside_y, across_y, both_y), late, along_x, gate[None, :])
 
 
 def solution(mesh):

time: 186 us -> 186 us (level)
  the two profiles are of different devices: /device:TPU:6 before, /device:TPU:33 now
where the time goes in v9:
time: 186 us
  blocking collectives  77.1 us (41%)
  starting transfers between devices  56 us (30%)
  waiting for transfers between devices  14.7 us (8%)
  between operations  14.2 us (8%)
  Pallas kernels  13.1 us (7%)
  local copies, waits for them, and re-layouts  5.58 us (3%)
  other arithmetic  5.05 us (3%)
    all_gather x1, blocking collectives, local(): lax.all_gather(jnp.concatenate([weights[:LATE], early.reshape(-1, width)]...  16.4 us
    all_gather x1, blocking collectives, local(): query_all = lax.all_gather(query_norm, 'x', axis=0, tiled=False)  14.7 us
    ppermute x1, starting transfers between devices, local(): totals = near + lax.ppermute(near, 'zh', SWAP)  14.5 us
    all_gather x1, blocking collectives, local(): across_y = lax.all_gather(across, 'y', axis=0, tiled=False)  13.4 us
    all_gather x1, blocking collectives, local(): own_y = lax.all_gather(own, 'y', axis=0, tiled=False)  12.6 us
    ppermute x1, starting transfers between devices, local(): across = lax.ppermute(own, 'zh', SWAP)  11.4 us
    all_to_all x1, blocking collectives, local(): parts = lax.all_to_all(parts, 'x', 0, 0, tiled=True)  10.3 us
    all_to_all x1, blocking collectives, local(): lax.all_to_all(jnp.broadcast_to(squares[None], (8, 2, rows)), ('y', 'core...  9.62 us
  transfers between devices with their start and end apart: 9, of which 5 were waited for; matrix products, arithmetic and copies ran while one was open for 3% of the time, Pallas kernels for 5%

profile of v9, /device:TPU:33, one launch (start us, length us, event | category | flops | bytes accessed | tf_op | source)
XLA Modules:
  0.0 185.8 jit_solution(11977945651812888106)
XLA Ops:
  6.5 0.0 all-gather.8.cloned.1.call-start
  6.5 1.7 pad_maximum_fusion
  8.3 0.0 copy-start.2
  8.3 0.0 copy-start.4
  8.3 0.0 all-gather.8.cloned.1.call-update
  8.3 1.1 fusion
  9.4 1.1 multiply_reduce_fusion
  10.5 9.6 %all_to_all.21 = f32[8,2,320]{2,1,0:T(2,128)S(1)} all-to-all(f32[8,2,320]{2,1,0:T(2,128)S(1)} %broadcast_in_dim.38), channel_id=1, replica_groups=mesh['x'=4,'zl'=8,'y'=4,'core'=2,'zh'=2] {'y','core'}, dimensions={0} | all-to-all | bytes 40960 | tf_op jit(solution)/shard_map/all_to_all | solution.py:217
  20.1 14.5 %collective-permute-start = (f32[2,320]{1,0:T(2,128)S(1)}, f32[2,320]{1,0:T(2,128)S(1)}, u32[]{:S(2)}, u32[]{:S(2)}) collective-permute-start(f32[2,320]{1,0:T(2,128)S(1)} %reduce_sum.29), channel_id=1, source_target_pairs={{0,1},{1,0},{2,3},{3,2},{4,5},{5,4},{6,7},{7,6},{8,9},{9,8},{10,11... | collective-permute-start | bytes 7688 | tf_op jit(solution)/shard_map/ppermute | solution.py:221
  34.7 4.9 %collective-permute-start.1 = (bf16[160,256]{1,0:T(8,128)(2,1)}, bf16[160,256]{1,0:T(8,128)(2,1)S(1)}, u32[]{:S(2)}, u32[]{:S(2)}) collective-permute-start(bf16[160,256]{1,0:T(8,128)(2,1)} %bitcast.22), channel_id=1, source_target_pairs={{0,0},{1,32},{2,64},{3,96},{4,128},{5,160},{6,192},{7,224},{8,256}... | collective-permute-start | bytes 245768 | tf_op jit(solution)/shard_map/ppermute | solution.py:209
  39.6 0.0 collective-permute-done
  39.6 0.6 broadcast_in_dim.39
  40.3 5.8 %all-to-all-start.1 = ((f32[8,1,320]{2,1,0:T(1,128)}), f32[8,1,320]{2,1,0:T(1,128)S(1)}, u32[]{:S(2)}, u32[]{:S(2)}) async-start(f32[8,1,320]{2,1,0:T(1,128)} %broadcast_in_dim.39), calls=%async_computation.1 | async-start | bytes 24576 | tf_op jit(solution)/shard_map/all_to_all | solution.py:223
  46.1 5.3 %collective-permute-done.1 = bf16[160,256]{1,0:T(8,128)(2,1)S(1)} collective-permute-done((bf16[160,256]{1,0:T(8,128)(2,1)}, bf16[160,256]{1,0:T(8,128)(2,1)S(1)}, u32[]{:S(2)}, u32[]{:S(2)}) %collective-permute-start.1) | collective-permute-done | bytes 81952 | tf_op jit(solution)/shard_map/ppermute | solution.py:209
  51.4 3.0 %all-to-all-done.1 = f32[8,1,320]{2,1,0:T(1,128)S(1)} async-done(((f32[8,1,320]{2,1,0:T(1,128)}), f32[8,1,320]{2,1,0:T(1,128)S(1)}, u32[]{:S(2)}, u32[]{:S(2)}) %all-to-all-start.1) | async-done | bytes 10272 | tf_op jit(solution)/shard_map/all_to_all | solution.py:223
  54.4 0.7 broadcast_in_dim.41
  55.1 4.6 %all-to-all-start.2 = ((bf16[8,48,256]{2,1,0:T(8,128)(2,1)}), bf16[8,48,256]{2,1,0:T(8,128)(2,1)S(1)}, u32[]{:S(2)}, u32[]{:S(2)}) async-start(bf16[8,48,256]{2,1,0:T(8,128)(2,1)} %broadcast_in_dim.41), calls=%async_computation.2 | async-start | bytes 393216 | tf_op jit(solution)/shard_map/all_to_all | solution.py:230
  59.7 0.0 all-gather.10.cloned.1.call-start
  59.7 1.0 fusion.2
  60.7 14.7 %all-gather = bf16[1280,256]{1,0:T(8,128)(2,1)S(1)} all-gather(bf16[320,256]{1,0:T(8,128)(2,1)S(1)} %fusion.2), channel_id=2, replica_groups=mesh['x'=4,'zl'=8,'y'=4,'core'=2,'zh'=2] {'x'}, dimensions={0}, use_global_device_ids=true | all-gather | bytes 819200 | tf_op jit(solution)/shard_map/all_gather | solution.py:228
  75.4 0.1 concatenate.9
  75.5 1.2 all-to-all-done.2
  76.7 16.4 %all-gather.3 = bf16[1984,256]{1,0:T(8,128)(2,1)S(1)} all-gather(bf16[496,256]{1,0:T(8,128)(2,1)S(1)} %pad_maximum_fusion.1), channel_id=5, replica_groups=mesh['x'=4,'zl'=8,'y'=4,'core'=2,'zh'=2] {'x'}, dimensions={0}, use_global_device_ids=true | all-gather | bytes 1269760 | tf_op jit(solution)/shard_map/all_gather | solution.py:234
  93.1 0.7 slice.75
  93.8 0.0 all-gather.10.cloned.1.call-update
  94.5 0.0 copy-done.2
  94.5 0.0 copy-done.4
  94.5 0.1 copy.14.gain_ref
  94.7 0.0 all-gather.8.cloned.1.call-done.kv_ref
  94.7 0.0 copy-start.1
  94.7 1.7 copy-done.1
  96.4 8.1 %shard_map.91 = bf16[4,336,256]{2,1,0:T(8,128)(2,1)S(1)} custom-call(bf16[4,320,256]{2,1,0:T(8,128)(2,1)S(1)} %bitcast.19, bf16[2560,512]{1,0:T(8,128)(2,1)S(1)} %copy-done.1, f32[1,2560]{1,0:T(1,128)S(1)} %broadcast_in_dim.40.inverse_ref, f32[1,2560]{1,0:T(1,128)S(1)} %broadcast_in_dim.44.bias_ref, f32[256,1]{1,0:T(8,128)S(1)} %copy.14.gain_ref), custom_call_target="tpu_custom_call" | custom-call | flops 6710886400 | bytes 4194304 | tf_op jit(solution)/shard_map/pallas_call | solution.py:67
  104.6 0.0 copy-start.3
  104.6 10.3 %all_to_all.22.parts_ref = bf16[4,336,256]{2,1,0:T(8,128)(2,1)S(1)} all-to-all(bf16[4,336,256]{2,1,0:T(8,128)(2,1)S(1)} %shard_map.91), channel_id=1, replica_groups=mesh['x'=4,'zl'=8,'y'=4,'core'=2,'zh'=2] {'x'}, dimensions={0} | all-to-all | bytes 1376256 | tf_op jit(solution)/shard_map/all_to_all | solution.py:246
  114.9 0.6 shard_map.92
  115.5 11.4 %collective-permute-start.3 = (bf16[320,256]{1,0:T(8,128)(2,1)S(1)}, bf16[320,256]{1,0:T(8,128)(2,1)S(1)}, u32[]{:S(2)}, u32[]{:S(2)}) collective-permute-start(bf16[320,256]{1,0:T(8,128)(2,1)S(1)} %shard_map.92), channel_id=1, source_target_pairs={{0,1},{1,0},{2,3},{3,2},{4,5},{5,4},{6,7},{7,6},{8,9},{9,8},{10,11... | collective-permute-start | bytes 491528 | tf_op jit(solution)/shard_map/ppermute | solution.py:248
  126.9 12.6 %all-gather.1 = bf16[1280,256]{1,0:T(8,128)(2,1)S(1)} all-gather(bf16[320,256]{1,0:T(8,128)(2,1)S(1)} %shard_map.92), channel_id=3, replica_groups=mesh['x'=4,'zl'=8,'y'=4,'core'=2,'zh'=2] {'y'}, dimensions={0}, use_global_device_ids=true | all-gather | bytes 819200 | tf_op jit(solution)/shard_map/all_gather | solution.py:249
  139.6 6.4 %collective-permute-start.2 = (bf16[4,320,256]{2,1,0:T(8,128)(2,1)S(1)}, bf16[4,320,256]{2,1,0:T(8,128)(2,1)S(1)}, u32[]{:S(2)}, u32[]{:S(2)}) collective-permute-start(bf16[4,320,256]{2,1,0:T(8,128)(2,1)S(1)} %bitcast.14), channel_id=1, source_target_pairs={{0,2},{2,0},{1,3},{3,1},{4,6},{6,4},{5,7},{7,5},{8,10},{10,8},{9,1... | collective-permute-start | bytes 1966088 | tf_op jit(solution)/shard_map/ppermute | solution.py:250
  145.9 3.5 %collective-permute-done.3 = bf16[320,256]{1,0:T(8,128)(2,1)S(1)} collective-permute-done((bf16[320,256]{1,0:T(8,128)(2,1)S(1)}, bf16[320,256]{1,0:T(8,128)(2,1)S(1)}, u32[]{:S(2)}, u32[]{:S(2)}) %collective-permute-start.3) | collective-permute-done | bytes 163872 | tf_op jit(solution)/shard_map/ppermute | solution.py:248
  149.4 13.4 %all-gather.2 = bf16[1280,256]{1,0:T(8,128)(2,1)S(1)} all-gather(bf16[320,256]{1,0:T(8,128)(2,1)S(1)} %collective-permute-done.3), channel_id=4, replica_groups=mesh['x'=4,'zl'=8,'y'=4,'core'=2,'zh'=2] {'y'}, dimensions={0}, use_global_device_ids=true | all-gather | bytes 819200 | tf_op jit(solution)/shard_map/all_gather | solution.py:251
  162.9 8.3 %collective-permute-start.4 = (bf16[4,320,256]{2,1,0:T(8,128)(2,1)S(1)}, bf16[4,320,256]{2,1,0:T(8,128)(2,1)}, u32[]{:S(2)}, u32[]{:S(2)}) collective-permute-start(bf16[4,320,256]{2,1,0:T(8,128)(2,1)S(1)} %bitcast.16), channel_id=1, source_target_pairs={{0,2},{2,0},{1,3},{3,1},{4,6},{6,4},{5,7},{7,5},{8,10},{10,8},{9,1... | collective-permute-start | bytes 1966088 | tf_op jit(solution)/shard_map/ppermute | solution.py:252
  171.2 0.0 copy-done.3
  171.2 0.1 pad_add_fusion.place_ref
  171.3 0.0 all-gather.10.cloned.1.call-done
  171.3 0.0 collective-permute-done.2.core_ref
  171.3 1.7 collective-permute-done.4.both_ref
  173.1 0.0 copy-start
  173.1 1.5 copy-done
  174.6 4.4 %shard_map.93 = bf16[320,320]{1,0:T(8,128)(2,1)} custom-call(s32[2]{0:T(128)S(1)} %pad_add_fusion.place_ref, bf16[4,320,256]{2,1,0:T(8,128)(2,1)S(1)} %bitcast.15, bf16[4,320,256]{2,1,0:T(8,128)(2,1)S(1)} %collective-permute-done.2.core_ref, bf16[4,320,256]{2,1,0:T(8,128)(2,1)S(1)} %bitcast.17, bf16[4,320,256]{2,1,0:T(8,128)(2,1)} %collective-permute-done.4.both_ref, ...), custom_call_target="tpu_custom_call" | custom-call | tf_op jit(solution)/shard_map/pallas_call | solution.py:175
  (15 shorter events, 0.2 us)
Async XLA Ops:
  6.5 88.2 %all-gather.8.cloned.1.call-start = ((), (), s32[]{:S(2)}) async-start(), calls=%async_computation.4 | async-start | bytes 2949120 | tf_op jit(solution)/shard_map/all_gather | solution.py:206
  8.3 86.2 %copy-start.2 = (s32[2560]{0:T(1024)S(1)}, s32[2560]{0:T(1024)}, u32[]{:S(2)}) copy-start(s32[2560]{0:T(1024)} %constant.25.clone) | copy-start | bytes 30724
  8.3 86.2 %copy-start.4 = (f32[256]{0:T(256)S(1)}, f32[256]{0:T(256)}, u32[]{:S(2)}) copy-start(f32[256]{0:T(256)} %param.14) | copy-start | bytes 3076
  20.1 19.5 %collective-permute-start = (f32[2,320]{1,0:T(2,128)S(1)}, f32[2,320]{1,0:T(2,128)S(1)}, u32[]{:S(2)}, u32[]{:S(2)}) collective-permute-start(f32[2,320]{1,0:T(2,128)S(1)} %reduce_sum.29), channel_id=1, source_target_pairs={{0,1},{1,0},{2,3},{3,2},{4,5},{5,4},{6,7},{7,6},{8,9},{9,8},{10,11... | collective-permute-start | bytes 7688 | tf_op jit(solution)/shard_map/ppermute | solution.py:221
  34.7 16.7 %collective-permute-start.1 = (bf16[160,256]{1,0:T(8,128)(2,1)}, bf16[160,256]{1,0:T(8,128)(2,1)S(1)}, u32[]{:S(2)}, u32[]{:S(2)}) collective-permute-start(bf16[160,256]{1,0:T(8,128)(2,1)} %bitcast.22), channel_id=1, source_target_pairs={{0,0},{1,32},{2,64},{3,96},{4,128},{5,160},{6,192},{7,224},{8,256}... | collective-permute-start | bytes 245768 | tf_op jit(solution)/shard_map/ppermute | solution.py:209
  40.3 14.1 %all-to-all-start.1 = ((f32[8,1,320]{2,1,0:T(1,128)}), f32[8,1,320]{2,1,0:T(1,128)S(1)}, u32[]{:S(2)}, u32[]{:S(2)}) async-start(f32[8,1,320]{2,1,0:T(1,128)} %broadcast_in_dim.39), calls=%async_computation.1 | async-start | bytes 24576 | tf_op jit(solution)/shard_map/all_to_all | solution.py:223
  55.1 21.6 %all-to-all-start.2 = ((bf16[8,48,256]{2,1,0:T(8,128)(2,1)}), bf16[8,48,256]{2,1,0:T(8,128)(2,1)S(1)}, u32[]{:S(2)}, u32[]{:S(2)}) async-start(bf16[8,48,256]{2,1,0:T(8,128)(2,1)} %broadcast_in_dim.41), calls=%async_computation.2 | async-start | bytes 393216 | tf_op jit(solution)/shard_map/all_to_all | solution.py:230
  59.7 111.6 %all-gather.10.cloned.1.call-start = ((), (), s32[]{:S(2)}) async-start(), calls=%async_computation.5 | async-start | bytes 2064384 | tf_op jit(solution)/shard_map/all_gather | solution.py:237
  94.7 1.7 copy-start.1
  104.6 66.7 %copy-start.3 = (f32[320]{0:T(512)S(1)}, f32[320]{0:T(512)}, u32[]{:S(2)}) copy-start(f32[320]{0:T(512)} %param.15) | copy-start | bytes 3844
  115.5 34.0 %collective-permute-start.3 = (bf16[320,256]{1,0:T(8,128)(2,1)S(1)}, bf16[320,256]{1,0:T(8,128)(2,1)S(1)}, u32[]{:S(2)}, u32[]{:S(2)}) collective-permute-start(bf16[320,256]{1,0:T(8,128)(2,1)S(1)} %shard_map.92), channel_id=1, source_target_pairs={{0,1},{1,0},{2,3},{3,2},{4,5},{5,4},{6,7},{7,6},{8,9},{9,8},{10,11... | collective-permute-start | bytes 491528 | tf_op jit(solution)/shard_map/ppermute | solution.py:248
  139.6 31.8 %collective-permute-start.2 = (bf16[4,320,256]{2,1,0:T(8,128)(2,1)S(1)}, bf16[4,320,256]{2,1,0:T(8,128)(2,1)S(1)}, u32[]{:S(2)}, u32[]{:S(2)}) collective-permute-start(bf16[4,320,256]{2,1,0:T(8,128)(2,1)S(1)} %bitcast.14), channel_id=1, source_target_pairs={{0,2},{2,0},{1,3},{3,1},{4,6},{6,4},{5,7},{7,5},{8,10},{10,8},{9,1... | collective-permute-start | bytes 1966088 | tf_op jit(solution)/shard_map/ppermute | solution.py:250
  162.9 10.2 %collective-permute-start.4 = (bf16[4,320,256]{2,1,0:T(8,128)(2,1)S(1)}, bf16[4,320,256]{2,1,0:T(8,128)(2,1)}, u32[]{:S(2)}, u32[]{:S(2)}) collective-permute-start(bf16[4,320,256]{2,1,0:T(8,128)(2,1)S(1)} %bitcast.16), channel_id=1, source_target_pairs={{0,2},{2,0},{1,3},{3,1},{4,6},{6,4},{5,7},{7,5},{8,10},{10,8},{9,1... | collective-permute-start | bytes 1966088 | tf_op jit(solution)/shard_map/ppermute | solution.py:252
  173.1 1.5 copy-start
Sparse Core Ops, SparseCore 0:
  9.4 83.7 all-gather.7
  95.3 68.4 all-gather.9

commit v10 on v9

--- a/solution.py
+++ b/solution.py
@@ -19,7 +19,7 @@
 SIZES = (4, 8, 4, 2, 2)
 SWAP = ((0, 1), (1, 0))
 RING = [0, 2, 4, 6, 7, 5, 3, 1]
-LATE = 112
+LATE = 128
 
 
 def attention_kernel(
@@ -227,10 +227,10 @@
     query_norm = (queries.astype(F32) * inverse[0][:, None] * q_gain[None, :]).astype(BF16)
     query_all = lax.all_gather(query_norm, "x", axis=0, tiled=False)
     columns = out_weight.shape[1]
+    query_all, key_inverse, weights = lax.optimization_barrier((query_all, key_inverse, weights))
     early = lax.all_to_all(
         jnp.broadcast_to(weights[None, LATE:], (8, columns - LATE, width)), "zl", 0, 0, tiled=True
     )
-    query_all, key_inverse, early = lax.optimization_barrier((query_all, key_inverse, early))
     along_x = lax.all_gather(
         jnp.concatenate([weights[:LATE], early.reshape(-1, width)]), "x", axis=0, tiled=False
     )

time: 186 us -> 186 us (level)
  the two profiles are of different devices: /device:TPU:33 before, /device:TPU:6 now
where the time goes in v10:
time: 186 us; the launch traced here: 184 us
  blocking collectives  74.9 us (40%)
  starting transfers between devices  48.7 us (26%)
  waiting for transfers between devices  23.4 us (13%)
  between operations  14.3 us (8%)
  Pallas kernels  12.4 us (7%)
  local copies, waits for them, and re-layouts  5.67 us (3%)
  other arithmetic  5.06 us (3%)
    ppermute x1, starting transfers between devices, local(): totals = near + lax.ppermute(near, 'zh', SWAP)  15.7 us
    all_to_all x1, waiting for transfers between devices, local(): lax.all_to_all(jnp.broadcast_to(weights[None, LATE:], (8, columns - LATE,...  14.8 us
    all_gather x1, blocking collectives, local(): lax.all_gather(jnp.concatenate([weights[:LATE], early.reshape(-1, width)]...  13.9 us
    all_gather x1, blocking collectives, local(): across_y = lax.all_gather(across, 'y', axis=0, tiled=False)  13.5 us
    all_gather x1, blocking collectives, local(): query_all = lax.all_gather(query_norm, 'x', axis=0, tiled=False)  13.4 us
    all_gather x1, blocking collectives, local(): own_y = lax.all_gather(own, 'y', axis=0, tiled=False)  13.2 us
    all_to_all x1, blocking collectives, local(): parts = lax.all_to_all(parts, 'x', 0, 0, tiled=True)  11.4 us
    all_to_all x1, blocking collectives, local(): lax.all_to_all(jnp.broadcast_to(squares[None], (8, 2, rows)), ('y', 'core...  9.67 us
  transfers between devices with their start and end apart: 9, of which 2 were waited for; matrix products, arithmetic and copies ran while one was open for 3% of the time, Pallas kernels for 5%

profile of v10, /device:TPU:6, one launch (start us, length us, event | category | flops | bytes accessed | tf_op | source)
XLA Modules:
  0.0 184.4 jit_solution(14627760169830441652)
XLA Ops:
  6.5 0.0 copy-start.2
  6.5 0.0 copy-start.4
  6.5 0.0 all-gather.8.cloned.1.call-start
  6.5 1.8 pad_maximum_fusion
  8.3 0.0 all-gather.8.cloned.1.call-update
  8.3 1.1 fusion
  9.4 1.1 multiply_reduce_fusion
  10.5 9.7 %all_to_all.21 = f32[8,2,320]{2,1,0:T(2,128)S(1)} all-to-all(f32[8,2,320]{2,1,0:T(2,128)S(1)} %broadcast_in_dim.38), channel_id=1, replica_groups=mesh['x'=4,'zl'=8,'y'=4,'core'=2,'zh'=2] {'y','core'}, dimensions={0} | all-to-all | bytes 40960 | tf_op jit(solution)/shard_map/all_to_all | solution.py:217
  20.2 15.7 %collective-permute-start = (f32[2,320]{1,0:T(2,128)S(1)}, f32[2,320]{1,0:T(2,128)S(1)}, u32[]{:S(2)}, u32[]{:S(2)}) collective-permute-start(f32[2,320]{1,0:T(2,128)S(1)} %reduce_sum.29), channel_id=1, source_target_pairs={{0,1},{1,0},{2,3},{3,2},{4,5},{5,4},{6,7},{7,6},{8,9},{9,8},{10,11... | collective-permute-start | bytes 7688 | tf_op jit(solution)/shard_map/ppermute | solution.py:221
  35.9 3.0 %collective-permute-start.1 = (bf16[160,256]{1,0:T(8,128)(2,1)}, bf16[160,256]{1,0:T(8,128)(2,1)S(1)}, u32[]{:S(2)}, u32[]{:S(2)}) collective-permute-start(bf16[160,256]{1,0:T(8,128)(2,1)} %bitcast.22), channel_id=1, source_target_pairs={{0,0},{1,32},{2,64},{3,96},{4,128},{5,160},{6,192},{7,224},{8,256}... | collective-permute-start | bytes 245768 | tf_op jit(solution)/shard_map/ppermute | solution.py:209
  38.9 0.0 collective-permute-done
  39.0 0.6 broadcast_in_dim.39
  39.6 8.1 %all-to-all-start.1 = ((f32[8,1,320]{2,1,0:T(1,128)}), f32[8,1,320]{2,1,0:T(1,128)S(1)}, u32[]{:S(2)}, u32[]{:S(2)}) async-start(f32[8,1,320]{2,1,0:T(1,128)} %broadcast_in_dim.39), calls=%async_computation.1 | async-start | bytes 24576 | tf_op jit(solution)/shard_map/all_to_all | solution.py:223
  47.7 1.0 fusion.2
  48.8 13.4 %all-gather = bf16[1280,256]{1,0:T(8,128)(2,1)S(1)} all-gather(bf16[320,256]{1,0:T(8,128)(2,1)S(1)} %fusion.2), channel_id=2, replica_groups=mesh['x'=4,'zl'=8,'y'=4,'core'=2,'zh'=2] {'x'}, dimensions={0}, use_global_device_ids=true | all-gather | bytes 819200 | tf_op jit(solution)/shard_map/all_gather | solution.py:228
  62.2 0.0 all-to-all-done.1
  62.2 0.1 concatenate.9
  62.3 0.0 collective-permute-done.1
  62.3 0.7 broadcast_in_dim.45
  63.0 9.6 %all-to-all-start.3 = ((bf16[8,32,256]{2,1,0:T(8,128)(2,1)}), bf16[8,32,256]{2,1,0:T(8,128)(2,1)S(1)}, u32[]{:S(2)}, u32[]{:S(2)}) async-start(bf16[8,32,256]{2,1,0:T(8,128)(2,1)} %broadcast_in_dim.45), calls=%async_computation.3 | async-start | bytes 262144 | tf_op jit(solution)/shard_map/all_to_all | solution.py:231
  72.6 0.0 all-gather.10.cloned.1.call-start
  72.7 14.8 %all-to-all-done.3 = bf16[8,32,256]{2,1,0:T(8,128)(2,1)S(1)} async-done(((bf16[8,32,256]{2,1,0:T(8,128)(2,1)}), bf16[8,32,256]{2,1,0:T(8,128)(2,1)S(1)}, u32[]{:S(2)}, u32[]{:S(2)}) %all-to-all-start.3) | async-done | bytes 131104 | tf_op jit(solution)/shard_map/all_to_all | solution.py:231
  87.5 13.9 %all-gather.3 = bf16[1536,256]{1,0:T(8,128)(2,1)S(1)} all-gather(bf16[384,256]{1,0:T(8,128)(2,1)S(1)} %pad_maximum_fusion.1), channel_id=5, replica_groups=mesh['x'=4,'zl'=8,'y'=4,'core'=2,'zh'=2] {'x'}, dimensions={0}, use_global_device_ids=true | all-gather | bytes 983040 | tf_op jit(solution)/shard_map/all_gather | solution.py:234
  101.4 0.7 slice.73
  102.1 0.0 all-gather.10.cloned.1.call-update
  102.8 0.0 copy-done.2
  102.8 0.0 copy-done.4
  102.8 0.1 copy.14.gain_ref
  103.0 0.0 all-gather.8.cloned.1.call-done.kv_ref
  103.0 0.0 copy-start.1
  103.0 1.7 copy-done.1
  104.7 8.1 %shard_map.91 = bf16[4,336,256]{2,1,0:T(8,128)(2,1)S(1)} custom-call(bf16[4,320,256]{2,1,0:T(8,128)(2,1)S(1)} %bitcast.19, bf16[2560,512]{1,0:T(8,128)(2,1)S(1)} %copy-done.1, f32[1,2560]{1,0:T(1,128)S(1)} %broadcast_in_dim.40.inverse_ref, f32[1,2560]{1,0:T(1,128)S(1)} %broadcast_in_dim.43.bias_ref, f32[256,1]{1,0:T(8,128)S(1)} %copy.14.gain_ref), custom_call_target="tpu_custom_call" | custom-call | flops 6710886400 | bytes 4194304 | tf_op jit(solution)/shard_map/pallas_call | solution.py:67
  112.9 0.0 copy-start.3
  112.9 11.4 %all_to_all.22.parts_ref = bf16[4,336,256]{2,1,0:T(8,128)(2,1)S(1)} all-to-all(bf16[4,336,256]{2,1,0:T(8,128)(2,1)S(1)} %shard_map.91), channel_id=1, replica_groups=mesh['x'=4,'zl'=8,'y'=4,'core'=2,'zh'=2] {'x'}, dimensions={0} | all-to-all | bytes 1376256 | tf_op jit(solution)/shard_map/all_to_all | solution.py:246
  124.2 0.6 shard_map.92
  124.8 8.4 %collective-permute-start.3 = (bf16[320,256]{1,0:T(8,128)(2,1)S(1)}, bf16[320,256]{1,0:T(8,128)(2,1)S(1)}, u32[]{:S(2)}, u32[]{:S(2)}) collective-permute-start(bf16[320,256]{1,0:T(8,128)(2,1)S(1)} %shard_map.92), channel_id=1, source_target_pairs={{0,1},{1,0},{2,3},{3,2},{4,5},{5,4},{6,7},{7,6},{8,9},{9,8},{10,11... | collective-permute-start | bytes 491528 | tf_op jit(solution)/shard_map/ppermute | solution.py:248
  133.2 13.2 %all-gather.1 = bf16[1280,256]{1,0:T(8,128)(2,1)S(1)} all-gather(bf16[320,256]{1,0:T(8,128)(2,1)S(1)} %shard_map.92), channel_id=3, replica_groups=mesh['x'=4,'zl'=8,'y'=4,'core'=2,'zh'=2] {'y'}, dimensions={0}, use_global_device_ids=true | all-gather | bytes 819200 | tf_op jit(solution)/shard_map/all_gather | solution.py:249
  146.4 1.9 %collective-permute-start.2 = (bf16[4,320,256]{2,1,0:T(8,128)(2,1)S(1)}, bf16[4,320,256]{2,1,0:T(8,128)(2,1)S(1)}, u32[]{:S(2)}, u32[]{:S(2)}) collective-permute-start(bf16[4,320,256]{2,1,0:T(8,128)(2,1)S(1)} %bitcast.14), channel_id=1, source_target_pairs={{0,2},{2,0},{1,3},{3,1},{4,6},{6,4},{5,7},{7,5},{8,10},{10,8},{9,1... | collective-permute-start | bytes 1966088 | tf_op jit(solution)/shard_map/ppermute | solution.py:250
  148.3 0.0 collective-permute-done.3
  148.3 13.5 %all-gather.2 = bf16[1280,256]{1,0:T(8,128)(2,1)S(1)} all-gather(bf16[320,256]{1,0:T(8,128)(2,1)S(1)} %collective-permute-done.3), channel_id=4, replica_groups=mesh['x'=4,'zl'=8,'y'=4,'core'=2,'zh'=2] {'y'}, dimensions={0}, use_global_device_ids=true | all-gather | bytes 819200 | tf_op jit(solution)/shard_map/all_gather | solution.py:251
  161.8 1.9 %collective-permute-start.4 = (bf16[4,320,256]{2,1,0:T(8,128)(2,1)S(1)}, bf16[4,320,256]{2,1,0:T(8,128)(2,1)S(1)}, u32[]{:S(2)}, u32[]{:S(2)}) collective-permute-start(bf16[4,320,256]{2,1,0:T(8,128)(2,1)S(1)} %bitcast.16), channel_id=1, source_target_pairs={{0,2},{2,0},{1,3},{3,1},{4,6},{6,4},{5,7},{7,5},{8,10},{10,8},{9,1... | collective-permute-start | bytes 1966088 | tf_op jit(solution)/shard_map/ppermute | solution.py:252
  163.7 0.0 copy-done.3
  163.7 0.1 pad_add_fusion.place_ref
  163.8 8.5 %all-gather.10.cloned.1.call-done = bf16[32,128,256]{2,1,0:T(8,128)(2,1)} async-done(((bf16[4,128,256]{2,1,0:T(8,128)(2,1)}), bf16[32,128,256]{2,1,0:T(8,128)(2,1)}) %all-gather.10.cloned.1.call-update) | async-done | bytes 2097168 | tf_op jit(solution)/shard_map/all_gather | solution.py:237
  172.3 0.0 collective-permute-done.2.core_ref
  172.3 0.0 collective-permute-done.4.both_ref
  172.3 0.0 copy-start
  172.3 1.6 copy-done
  173.9 3.7 %shard_map.93 = bf16[320,320]{1,0:T(8,128)(2,1)} custom-call(s32[2]{0:T(128)S(1)} %pad_add_fusion.place_ref, bf16[4,320,256]{2,1,0:T(8,128)(2,1)S(1)} %bitcast.15, bf16[4,320,256]{2,1,0:T(8,128)(2,1)S(1)} %collective-permute-done.2.core_ref, bf16[4,320,256]{2,1,0:T(8,128)(2,1)S(1)} %bitcast.17, bf16[4,320,256]{2,1,0:T(8,128)(2,1)S(1)} %collective-permute-done.4.both_ref, ...), custom_call_target="tpu_custom_call" | custom-call | tf_op jit(solution)/shard_map/pallas_call | solution.py:175
  (15 shorter events, 0.2 us)
Async XLA Ops:
  6.5 96.2 %copy-start.2 = (s32[2560]{0:T(1024)S(1)}, s32[2560]{0:T(1024)}, u32[]{:S(2)}) copy-start(s32[2560]{0:T(1024)} %constant.25.clone) | copy-start | bytes 30724
  6.5 96.3 %copy-start.4 = (f32[256]{0:T(256)S(1)}, f32[256]{0:T(256)}, u32[]{:S(2)}) copy-start(f32[256]{0:T(256)} %param.14) | copy-start | bytes 3076
  6.5 96.4 %all-gather.8.cloned.1.call-start = ((), (), s32[]{:S(2)}) async-start(), calls=%async_computation.4 | async-start | bytes 2949120 | tf_op jit(solution)/shard_map/all_gather | solution.py:206
  20.2 18.7 %collective-permute-start = (f32[2,320]{1,0:T(2,128)S(1)}, f32[2,320]{1,0:T(2,128)S(1)}, u32[]{:S(2)}, u32[]{:S(2)}) collective-permute-start(f32[2,320]{1,0:T(2,128)S(1)} %reduce_sum.29), channel_id=1, source_target_pairs={{0,1},{1,0},{2,3},{3,2},{4,5},{5,4},{6,7},{7,6},{8,9},{9,8},{10,11... | collective-permute-start | bytes 7688 | tf_op jit(solution)/shard_map/ppermute | solution.py:221
  35.9 26.4 %collective-permute-start.1 = (bf16[160,256]{1,0:T(8,128)(2,1)}, bf16[160,256]{1,0:T(8,128)(2,1)S(1)}, u32[]{:S(2)}, u32[]{:S(2)}) collective-permute-start(bf16[160,256]{1,0:T(8,128)(2,1)} %bitcast.22), channel_id=1, source_target_pairs={{0,0},{1,32},{2,64},{3,96},{4,128},{5,160},{6,192},{7,224},{8,256}... | collective-permute-start | bytes 245768 | tf_op jit(solution)/shard_map/ppermute | solution.py:209
  39.6 22.6 %all-to-all-start.1 = ((f32[8,1,320]{2,1,0:T(1,128)}), f32[8,1,320]{2,1,0:T(1,128)S(1)}, u32[]{:S(2)}, u32[]{:S(2)}) async-start(f32[8,1,320]{2,1,0:T(1,128)} %broadcast_in_dim.39), calls=%async_computation.1 | async-start | bytes 24576 | tf_op jit(solution)/shard_map/all_to_all | solution.py:223
  63.0 24.5 %all-to-all-start.3 = ((bf16[8,32,256]{2,1,0:T(8,128)(2,1)}), bf16[8,32,256]{2,1,0:T(8,128)(2,1)S(1)}, u32[]{:S(2)}, u32[]{:S(2)}) async-start(bf16[8,32,256]{2,1,0:T(8,128)(2,1)} %broadcast_in_dim.45), calls=%async_computation.3 | async-start | bytes 262144 | tf_op jit(solution)/shard_map/all_to_all | solution.py:231
  72.6 99.7 %all-gather.10.cloned.1.call-start = ((), (), s32[]{:S(2)}) async-start(), calls=%async_computation.5 | async-start | bytes 2359296 | tf_op jit(solution)/shard_map/all_gather | solution.py:237
  103.0 1.7 copy-start.1
  112.9 50.8 %copy-start.3 = (f32[320]{0:T(512)S(1)}, f32[320]{0:T(512)}, u32[]{:S(2)}) copy-start(f32[320]{0:T(512)} %param.15) | copy-start | bytes 3844
  124.8 23.5 %collective-permute-start.3 = (bf16[320,256]{1,0:T(8,128)(2,1)S(1)}, bf16[320,256]{1,0:T(8,128)(2,1)S(1)}, u32[]{:S(2)}, u32[]{:S(2)}) collective-permute-start(bf16[320,256]{1,0:T(8,128)(2,1)S(1)} %shard_map.92), channel_id=1, source_target_pairs={{0,1},{1,0},{2,3},{3,2},{4,5},{5,4},{6,7},{7,6},{8,9},{9,8},{10,11... | collective-permute-start | bytes 491528 | tf_op jit(solution)/shard_map/ppermute | solution.py:248
  146.4 25.9 %collective-permute-start.2 = (bf16[4,320,256]{2,1,0:T(8,128)(2,1)S(1)}, bf16[4,320,256]{2,1,0:T(8,128)(2,1)S(1)}, u32[]{:S(2)}, u32[]{:S(2)}) collective-permute-start(bf16[4,320,256]{2,1,0:T(8,128)(2,1)S(1)} %bitcast.14), channel_id=1, source_target_pairs={{0,2},{2,0},{1,3},{3,1},{4,6},{6,4},{5,7},{7,5},{8,10},{10,8},{9,1... | collective-permute-start | bytes 1966088 | tf_op jit(solution)/shard_map/ppermute | solution.py:250
  161.8 10.5 %collective-permute-start.4 = (bf16[4,320,256]{2,1,0:T(8,128)(2,1)S(1)}, bf16[4,320,256]{2,1,0:T(8,128)(2,1)S(1)}, u32[]{:S(2)}, u32[]{:S(2)}) collective-permute-start(bf16[4,320,256]{2,1,0:T(8,128)(2,1)S(1)} %bitcast.16), channel_id=1, source_target_pairs={{0,2},{2,0},{1,3},{3,1},{4,6},{6,4},{5,7},{7,5},{8,10},{10,8},{9,1... | collective-permute-start | bytes 1966088 | tf_op jit(solution)/shard_map/ppermute | solution.py:252
  172.3 1.6 copy-start
Sparse Core Ops, SparseCore 0:
  9.4 83.0 all-gather.7
  102.2 69.9 all-gather.9

commit v11 on v10

--- a/solution.py
+++ b/solution.py
@@ -227,10 +227,10 @@
     query_norm = (queries.astype(F32) * inverse[0][:, None] * q_gain[None, :]).astype(BF16)
     query_all = lax.all_gather(query_norm, "x", axis=0, tiled=False)
     columns = out_weight.shape[1]
-    query_all, key_inverse, weights = lax.optimization_barrier((query_all, key_inverse, weights))
     early = lax.all_to_all(
         jnp.broadcast_to(weights[None, LATE:], (8, columns - LATE, width)), "zl", 0, 0, tiled=True
     )
+    query_all, key_inverse, early = lax.optimization_barrier((query_all, key_inverse, early))
     along_x = lax.all_gather(
         jnp.concatenate([weights[:LATE], early.reshape(-1, width)]), "x", axis=0, tiled=False
     )

time: 186 us -> 183 us (0.984)
  the two profiles are of different devices: /device:TPU:6 before, /device:TPU:33 now
where the time goes in v11:
time: 183 us; the launch traced here: 182 us
  blocking collectives  77.4 us (42%)
  starting transfers between devices  55.2 us (30%)
  between operations  14.2 us (8%)
  Pallas kernels  12.4 us (7%)
  waiting for transfers between devices  12.2 us (7%)
  local copies, waits for them, and re-layouts  5.67 us (3%)
  other arithmetic  5.06 us (3%)
    all_gather x1, blocking collectives, local(): across_y = lax.all_gather(across, 'y', axis=0, tiled=False)  16.4 us
    all_gather x1, blocking collectives, local(): query_all = lax.all_gather(query_norm, 'x', axis=0, tiled=False)  14.7 us
    ppermute x1, starting transfers between devices, local(): totals = near + lax.ppermute(near, 'zh', SWAP)  14.5 us
    all_gather x1, blocking collectives, local(): own_y = lax.all_gather(own, 'y', axis=0, tiled=False)  13 us
    all_gather x1, blocking collectives, local(): lax.all_gather(jnp.concatenate([weights[:LATE], early.reshape(-1, width)]...  12 us
    all_to_all x1, blocking collectives, local(): parts = lax.all_to_all(parts, 'x', 0, 0, tiled=True)  11.7 us
    ppermute x1, starting transfers between devices, local(): across = lax.ppermute(own, 'zh', SWAP)  10.4 us
    all_to_all x1, blocking collectives, local(): lax.all_to_all(jnp.broadcast_to(squares[None], (8, 2, rows)), ('y', 'core...  9.62 us
  transfers between devices with their start and end apart: 9, of which 5 were waited for; matrix products, arithmetic and copies ran while one was open for 3% of the time, Pallas kernels for 5%

profile of v11, /device:TPU:33, one launch (start us, length us, event | category | flops | bytes accessed | tf_op | source)
XLA Modules:
  0.0 182.2 jit_solution(9229786532903369049)
XLA Ops:
  6.5 0.0 copy-start.2
  6.5 0.0 copy-start.4
  6.5 0.0 all-gather.8.cloned.1.call-start
  6.5 1.8 pad_maximum_fusion
  8.3 0.0 all-gather.8.cloned.1.call-update
  8.3 1.1 fusion
  9.4 1.1 multiply_reduce_fusion
  10.5 9.6 %all_to_all.21 = f32[8,2,320]{2,1,0:T(2,128)S(1)} all-to-all(f32[8,2,320]{2,1,0:T(2,128)S(1)} %broadcast_in_dim.38), channel_id=1, replica_groups=mesh['x'=4,'zl'=8,'y'=4,'core'=2,'zh'=2] {'y','core'}, dimensions={0} | all-to-all | bytes 40960 | tf_op jit(solution)/shard_map/all_to_all | solution.py:217
  20.2 14.5 %collective-permute-start = (f32[2,320]{1,0:T(2,128)S(1)}, f32[2,320]{1,0:T(2,128)S(1)}, u32[]{:S(2)}, u32[]{:S(2)}) collective-permute-start(f32[2,320]{1,0:T(2,128)S(1)} %reduce_sum.29), channel_id=1, source_target_pairs={{0,1},{1,0},{2,3},{3,2},{4,5},{5,4},{6,7},{7,6},{8,9},{9,8},{10,11... | collective-permute-start | bytes 7688 | tf_op jit(solution)/shard_map/ppermute | solution.py:221
  34.7 4.9 %collective-permute-start.1 = (bf16[160,256]{1,0:T(8,128)(2,1)}, bf16[160,256]{1,0:T(8,128)(2,1)S(1)}, u32[]{:S(2)}, u32[]{:S(2)}) collective-permute-start(bf16[160,256]{1,0:T(8,128)(2,1)} %bitcast.22), channel_id=1, source_target_pairs={{0,0},{1,32},{2,64},{3,96},{4,128},{5,160},{6,192},{7,224},{8,256}... | collective-permute-start | bytes 245768 | tf_op jit(solution)/shard_map/ppermute | solution.py:209
  39.6 0.0 collective-permute-done
  39.7 0.6 broadcast_in_dim.39
  40.3 5.8 %all-to-all-start.1 = ((f32[8,1,320]{2,1,0:T(1,128)}), f32[8,1,320]{2,1,0:T(1,128)S(1)}, u32[]{:S(2)}, u32[]{:S(2)}) async-start(f32[8,1,320]{2,1,0:T(1,128)} %broadcast_in_dim.39), calls=%async_computation.1 | async-start | bytes 24576 | tf_op jit(solution)/shard_map/all_to_all | solution.py:223
  46.1 5.3 %collective-permute-done.1 = bf16[160,256]{1,0:T(8,128)(2,1)S(1)} collective-permute-done((bf16[160,256]{1,0:T(8,128)(2,1)}, bf16[160,256]{1,0:T(8,128)(2,1)S(1)}, u32[]{:S(2)}, u32[]{:S(2)}) %collective-permute-start.1) | collective-permute-done | bytes 81952 | tf_op jit(solution)/shard_map/ppermute | solution.py:209
  51.4 3.0 %all-to-all-done.1 = f32[8,1,320]{2,1,0:T(1,128)S(1)} async-done(((f32[8,1,320]{2,1,0:T(1,128)}), f32[8,1,320]{2,1,0:T(1,128)S(1)}, u32[]{:S(2)}, u32[]{:S(2)}) %all-to-all-start.1) | async-done | bytes 10272 | tf_op jit(solution)/shard_map/all_to_all | solution.py:223
  54.4 0.7 broadcast_in_dim.41
  55.1 4.6 %all-to-all-start.2 = ((bf16[8,32,256]{2,1,0:T(8,128)(2,1)}), bf16[8,32,256]{2,1,0:T(8,128)(2,1)S(1)}, u32[]{:S(2)}, u32[]{:S(2)}) async-start(bf16[8,32,256]{2,1,0:T(8,128)(2,1)} %broadcast_in_dim.41), calls=%async_computation.2 | async-start | bytes 262144 | tf_op jit(solution)/shard_map/all_to_all | solution.py:230
  59.7 0.0 all-gather.10.cloned.1.call-start
  59.7 1.0 fusion.2
  60.7 14.7 %all-gather = bf16[1280,256]{1,0:T(8,128)(2,1)S(1)} all-gather(bf16[320,256]{1,0:T(8,128)(2,1)S(1)} %fusion.2), channel_id=2, replica_groups=mesh['x'=4,'zl'=8,'y'=4,'core'=2,'zh'=2] {'x'}, dimensions={0}, use_global_device_ids=true | all-gather | bytes 819200 | tf_op jit(solution)/shard_map/all_gather | solution.py:228
  75.4 0.1 concatenate.9
  75.6 0.0 all-to-all-done.2
  75.6 12.0 %all-gather.3 = bf16[1536,256]{1,0:T(8,128)(2,1)S(1)} all-gather(bf16[384,256]{1,0:T(8,128)(2,1)S(1)} %pad_maximum_fusion.1), channel_id=5, replica_groups=mesh['x'=4,'zl'=8,'y'=4,'core'=2,'zh'=2] {'x'}, dimensions={0}, use_global_device_ids=true | all-gather | bytes 983040 | tf_op jit(solution)/shard_map/all_gather | solution.py:234
  87.6 0.7 slice.75
  88.3 0.0 all-gather.10.cloned.1.call-update
  89.0 0.0 copy-done.2
  89.0 0.0 copy-done.4
  89.0 0.1 copy.14.gain_ref
  89.2 0.7 all-gather.8.cloned.1.call-done.kv_ref
  89.9 0.0 copy-start.1
  89.9 1.7 copy-done.1
  91.6 8.1 %shard_map.91 = bf16[4,336,256]{2,1,0:T(8,128)(2,1)S(1)} custom-call(bf16[4,320,256]{2,1,0:T(8,128)(2,1)S(1)} %bitcast.19, bf16[2560,512]{1,0:T(8,128)(2,1)S(1)} %copy-done.1, f32[1,2560]{1,0:T(1,128)S(1)} %broadcast_in_dim.40.inverse_ref, f32[1,2560]{1,0:T(1,128)S(1)} %broadcast_in_dim.44.bias_ref, f32[256,1]{1,0:T(8,128)S(1)} %copy.14.gain_ref), custom_call_target="tpu_custom_call" | custom-call | flops 6710886400 | bytes 4194304 | tf_op jit(solution)/shard_map/pallas_call | solution.py:67
  99.8 0.0 copy-start.3
  99.8 11.7 %all_to_all.22.parts_ref = bf16[4,336,256]{2,1,0:T(8,128)(2,1)S(1)} all-to-all(bf16[4,336,256]{2,1,0:T(8,128)(2,1)S(1)} %shard_map.91), channel_id=1, replica_groups=mesh['x'=4,'zl'=8,'y'=4,'core'=2,'zh'=2] {'x'}, dimensions={0} | all-to-all | bytes 1376256 | tf_op jit(solution)/shard_map/all_to_all | solution.py:246
  111.5 0.6 shard_map.92
  112.1 10.4 %collective-permute-start.3 = (bf16[320,256]{1,0:T(8,128)(2,1)S(1)}, bf16[320,256]{1,0:T(8,128)(2,1)S(1)}, u32[]{:S(2)}, u32[]{:S(2)}) collective-permute-start(bf16[320,256]{1,0:T(8,128)(2,1)S(1)} %shard_map.92), channel_id=1, source_target_pairs={{0,1},{1,0},{2,3},{3,2},{4,5},{5,4},{6,7},{7,6},{8,9},{9,8},{10,11... | collective-permute-start | bytes 491528 | tf_op jit(solution)/shard_map/ppermute | solution.py:248
  122.5 13.0 %all-gather.1 = bf16[1280,256]{1,0:T(8,128)(2,1)S(1)} all-gather(bf16[320,256]{1,0:T(8,128)(2,1)S(1)} %shard_map.92), channel_id=3, replica_groups=mesh['x'=4,'zl'=8,'y'=4,'core'=2,'zh'=2] {'y'}, dimensions={0}, use_global_device_ids=true | all-gather | bytes 819200 | tf_op jit(solution)/shard_map/all_gather | solution.py:249
  135.5 6.6 %collective-permute-start.2 = (bf16[4,320,256]{2,1,0:T(8,128)(2,1)S(1)}, bf16[4,320,256]{2,1,0:T(8,128)(2,1)S(1)}, u32[]{:S(2)}, u32[]{:S(2)}) collective-permute-start(bf16[4,320,256]{2,1,0:T(8,128)(2,1)S(1)} %bitcast.14), channel_id=1, source_target_pairs={{0,2},{2,0},{1,3},{3,1},{4,6},{6,4},{5,7},{7,5},{8,10},{10,8},{9,1... | collective-permute-start | bytes 1966088 | tf_op jit(solution)/shard_map/ppermute | solution.py:250
  142.1 1.5 collective-permute-done.3
  143.6 16.4 %all-gather.2 = bf16[1280,256]{1,0:T(8,128)(2,1)S(1)} all-gather(bf16[320,256]{1,0:T(8,128)(2,1)S(1)} %collective-permute-done.3), channel_id=4, replica_groups=mesh['x'=4,'zl'=8,'y'=4,'core'=2,'zh'=2] {'y'}, dimensions={0}, use_global_device_ids=true | all-gather | bytes 819200 | tf_op jit(solution)/shard_map/all_gather | solution.py:251
  160.0 8.3 %collective-permute-start.4 = (bf16[4,320,256]{2,1,0:T(8,128)(2,1)S(1)}, bf16[4,320,256]{2,1,0:T(8,128)(2,1)S(1)}, u32[]{:S(2)}, u32[]{:S(2)}) collective-permute-start(bf16[4,320,256]{2,1,0:T(8,128)(2,1)S(1)} %bitcast.16), channel_id=1, source_target_pairs={{0,2},{2,0},{1,3},{3,1},{4,6},{6,4},{5,7},{7,5},{8,10},{10,8},{9,1... | collective-permute-start | bytes 1966088 | tf_op jit(solution)/shard_map/ppermute | solution.py:252
  168.3 0.0 copy-done.3
  168.3 0.1 pad_add_fusion.place_ref
  168.4 0.0 all-gather.10.cloned.1.call-done
  168.4 0.0 collective-permute-done.2.core_ref
  168.4 1.6 collective-permute-done.4.both_ref
  170.0 0.0 copy-start
  170.0 1.6 copy-done
  171.6 3.7 %shard_map.93 = bf16[320,320]{1,0:T(8,128)(2,1)} custom-call(s32[2]{0:T(128)S(1)} %pad_add_fusion.place_ref, bf16[4,320,256]{2,1,0:T(8,128)(2,1)S(1)} %bitcast.15, bf16[4,320,256]{2,1,0:T(8,128)(2,1)S(1)} %collective-permute-done.2.core_ref, bf16[4,320,256]{2,1,0:T(8,128)(2,1)S(1)} %bitcast.17, bf16[4,320,256]{2,1,0:T(8,128)(2,1)S(1)} %collective-permute-done.4.both_ref, ...), custom_call_target="tpu_custom_call" | custom-call | tf_op jit(solution)/shard_map/pallas_call | solution.py:175
  (15 shorter events, 0.2 us)
Async XLA Ops:
  6.5 82.4 %copy-start.2 = (s32[2560]{0:T(1024)S(1)}, s32[2560]{0:T(1024)}, u32[]{:S(2)}) copy-start(s32[2560]{0:T(1024)} %constant.25.clone) | copy-start | bytes 30724
  6.5 82.5 %copy-start.4 = (f32[256]{0:T(256)S(1)}, f32[256]{0:T(256)}, u32[]{:S(2)}) copy-start(f32[256]{0:T(256)} %param.14) | copy-start | bytes 3076
  6.5 83.3 %all-gather.8.cloned.1.call-start = ((), (), s32[]{:S(2)}) async-start(), calls=%async_computation.4 | async-start | bytes 2949120 | tf_op jit(solution)/shard_map/all_gather | solution.py:206
  20.2 19.5 %collective-permute-start = (f32[2,320]{1,0:T(2,128)S(1)}, f32[2,320]{1,0:T(2,128)S(1)}, u32[]{:S(2)}, u32[]{:S(2)}) collective-permute-start(f32[2,320]{1,0:T(2,128)S(1)} %reduce_sum.29), channel_id=1, source_target_pairs={{0,1},{1,0},{2,3},{3,2},{4,5},{5,4},{6,7},{7,6},{8,9},{9,8},{10,11... | collective-permute-start | bytes 7688 | tf_op jit(solution)/shard_map/ppermute | solution.py:221
  34.7 16.7 %collective-permute-start.1 = (bf16[160,256]{1,0:T(8,128)(2,1)}, bf16[160,256]{1,0:T(8,128)(2,1)S(1)}, u32[]{:S(2)}, u32[]{:S(2)}) collective-permute-start(bf16[160,256]{1,0:T(8,128)(2,1)} %bitcast.22), channel_id=1, source_target_pairs={{0,0},{1,32},{2,64},{3,96},{4,128},{5,160},{6,192},{7,224},{8,256}... | collective-permute-start | bytes 245768 | tf_op jit(solution)/shard_map/ppermute | solution.py:209
  40.3 14.1 %all-to-all-start.1 = ((f32[8,1,320]{2,1,0:T(1,128)}), f32[8,1,320]{2,1,0:T(1,128)S(1)}, u32[]{:S(2)}, u32[]{:S(2)}) async-start(f32[8,1,320]{2,1,0:T(1,128)} %broadcast_in_dim.39), calls=%async_computation.1 | async-start | bytes 24576 | tf_op jit(solution)/shard_map/all_to_all | solution.py:223
  55.1 20.5 %all-to-all-start.2 = ((bf16[8,32,256]{2,1,0:T(8,128)(2,1)}), bf16[8,32,256]{2,1,0:T(8,128)(2,1)S(1)}, u32[]{:S(2)}, u32[]{:S(2)}) async-start(bf16[8,32,256]{2,1,0:T(8,128)(2,1)} %broadcast_in_dim.41), calls=%async_computation.2 | async-start | bytes 262144 | tf_op jit(solution)/shard_map/all_to_all | solution.py:230
  59.7 108.8 %all-gather.10.cloned.1.call-start = ((), (), s32[]{:S(2)}) async-start(), calls=%async_computation.5 | async-start | bytes 2359296 | tf_op jit(solution)/shard_map/all_gather | solution.py:237
  89.9 1.7 copy-start.1
  99.8 68.6 %copy-start.3 = (f32[320]{0:T(512)S(1)}, f32[320]{0:T(512)}, u32[]{:S(2)}) copy-start(f32[320]{0:T(512)} %param.15) | copy-start | bytes 3844
  112.1 31.6 %collective-permute-start.3 = (bf16[320,256]{1,0:T(8,128)(2,1)S(1)}, bf16[320,256]{1,0:T(8,128)(2,1)S(1)}, u32[]{:S(2)}, u32[]{:S(2)}) collective-permute-start(bf16[320,256]{1,0:T(8,128)(2,1)S(1)} %shard_map.92), channel_id=1, source_target_pairs={{0,1},{1,0},{2,3},{3,2},{4,5},{5,4},{6,7},{7,6},{8,9},{9,8},{10,11... | collective-permute-start | bytes 491528 | tf_op jit(solution)/shard_map/ppermute | solution.py:248
  135.5 32.9 %collective-permute-start.2 = (bf16[4,320,256]{2,1,0:T(8,128)(2,1)S(1)}, bf16[4,320,256]{2,1,0:T(8,128)(2,1)S(1)}, u32[]{:S(2)}, u32[]{:S(2)}) collective-permute-start(bf16[4,320,256]{2,1,0:T(8,128)(2,1)S(1)} %bitcast.14), channel_id=1, source_target_pairs={{0,2},{2,0},{1,3},{3,1},{4,6},{6,4},{5,7},{7,5},{8,10},{10,8},{9,1... | collective-permute-start | bytes 1966088 | tf_op jit(solution)/shard_map/ppermute | solution.py:250
  160.0 10.0 %collective-permute-start.4 = (bf16[4,320,256]{2,1,0:T(8,128)(2,1)S(1)}, bf16[4,320,256]{2,1,0:T(8,128)(2,1)S(1)}, u32[]{:S(2)}, u32[]{:S(2)}) collective-permute-start(bf16[4,320,256]{2,1,0:T(8,128)(2,1)S(1)} %bitcast.16), channel_id=1, source_target_pairs={{0,2},{2,0},{1,3},{3,1},{4,6},{6,4},{5,7},{7,5},{8,10},{10,8},{9,1... | collective-permute-start | bytes 1966088 | tf_op jit(solution)/shard_map/ppermute | solution.py:252
  170.0 1.6 copy-start
Sparse Core Ops, SparseCore 0:
  9.4 80.4 all-gather.7
  92.0 73.1 all-gather.9

commit v12 on v11

--- a/solution.py
+++ b/solution.py
@@ -185,7 +185,7 @@
         out_specs=pl.BlockSpec(shape, lambda i: (0, 0)),
         out_shape=jax.ShapeDtypeStruct(shape, BF16),
         scratch_shapes=[pltpu.VMEM(shape, F32)],
-        compiler_params=pltpu.CompilerParams(vmem_limit_bytes=32 << 20),
+        compiler_params=pltpu.CompilerParams(vmem_limit_bytes=60 << 20),
     )(place, *pieces, late, early, gate)
 
 

time: 183 us -> 184 us (level)
  the two profiles are of different devices: /device:TPU:33 before, /device:TPU:41 now
where the time goes in v12:
time: 184 us; the launch traced here: 183 us
  blocking collectives  72.1 us (39%)
  starting transfers between devices  57.6 us (31%)
  between operations  14.2 us (8%)
  Pallas kernels  14 us (8%)
  waiting for transfers between devices  13.9 us (8%)
  other arithmetic  5.66 us (3%)
  local copies, waits for them, and re-layouts  5.55 us (3%)
    all_gather x1, blocking collectives, local(): across_y = lax.all_gather(across, 'y', axis=0, tiled=False)  15.1 us
    ppermute x1, starting transfers between devices, local(): totals = near + lax.ppermute(near, 'zh', SWAP)  14.5 us
    all_gather x1, blocking collectives, local(): query_all = lax.all_gather(query_norm, 'x', axis=0, tiled=False)  12.6 us
    all_gather x1, blocking collectives, local(): lax.all_gather(jnp.concatenate([weights[:LATE], early.reshape(-1, width)]...  12.3 us
    all_gather x1, blocking collectives, local(): own_y = lax.all_gather(own, 'y', axis=0, tiled=False)  11.9 us
    ppermute x1, starting transfers between devices, local(): across = lax.ppermute(own, 'zh', SWAP)  11.9 us
    all_to_all x1, blocking collectives, local(): parts = lax.all_to_all(parts, 'x', 0, 0, tiled=True)  11.6 us
    ppermute x1, starting transfers between devices, local(): both_y = lax.ppermute(across_y, 'core', SWAP)  9.01 us
  transfers between devices with their start and end apart: 9, of which 5 were waited for; matrix products, arithmetic and copies ran while one was open for 4% of the time, Pallas kernels for 5%

profile of v12, /device:TPU:41, one launch (start us, length us, event | category | flops | bytes accessed | tf_op | source)
XLA Modules:
  0.0 183.1 jit_solution(6674150251449958313)
XLA Ops:
  6.5 0.0 copy-start.6
  6.5 0.0 copy-start.8
  6.5 0.0 all-gather.8.cloned.1.call-start
  6.5 1.8 pad_maximum_fusion
  8.3 0.0 all-gather.8.cloned.1.call-update
  8.4 1.1 fusion
  9.4 1.1 multiply_reduce_fusion
  10.5 8.6 %all_to_all.21 = f32[8,2,320]{2,1,0:T(2,128)S(1)} all-to-all(f32[8,2,320]{2,1,0:T(2,128)S(1)} %broadcast_in_dim.38), channel_id=1, replica_groups=mesh['x'=4,'zl'=8,'y'=4,'core'=2,'zh'=2] {'y','core'}, dimensions={0} | all-to-all | bytes 40960 | tf_op jit(solution)/shard_map/all_to_all | solution.py:217
  19.2 14.5 %collective-permute-start = (f32[2,320]{1,0:T(2,128)S(1)}, f32[2,320]{1,0:T(2,128)S(1)}, u32[]{:S(2)}, u32[]{:S(2)}) collective-permute-start(f32[2,320]{1,0:T(2,128)S(1)} %reduce_sum.29), channel_id=1, source_target_pairs={{0,1},{1,0},{2,3},{3,2},{4,5},{5,4},{6,7},{7,6},{8,9},{9,8},{10,11... | collective-permute-start | bytes 7688 | tf_op jit(solution)/shard_map/ppermute | solution.py:221
  33.7 6.7 %collective-permute-start.1 = (bf16[160,256]{1,0:T(8,128)(2,1)}, bf16[160,256]{1,0:T(8,128)(2,1)S(1)}, u32[]{:S(2)}, u32[]{:S(2)}) collective-permute-start(bf16[160,256]{1,0:T(8,128)(2,1)} %bitcast.22), channel_id=1, source_target_pairs={{0,0},{1,32},{2,64},{3,96},{4,128},{5,160},{6,192},{7,224},{8,256}... | collective-permute-start | bytes 245768 | tf_op jit(solution)/shard_map/ppermute | solution.py:209
  40.5 0.0 collective-permute-done
  40.5 0.6 broadcast_in_dim.39
  41.1 4.0 %all-to-all-start.1 = ((f32[8,1,320]{2,1,0:T(1,128)}), f32[8,1,320]{2,1,0:T(1,128)S(1)}, u32[]{:S(2)}, u32[]{:S(2)}) async-start(f32[8,1,320]{2,1,0:T(1,128)} %broadcast_in_dim.39), calls=%async_computation.1 | async-start | bytes 24576 | tf_op jit(solution)/shard_map/all_to_all | solution.py:223
  45.1 7.1 %collective-permute-done.1 = bf16[160,256]{1,0:T(8,128)(2,1)S(1)} collective-permute-done((bf16[160,256]{1,0:T(8,128)(2,1)}, bf16[160,256]{1,0:T(8,128)(2,1)S(1)}, u32[]{:S(2)}, u32[]{:S(2)}) %collective-permute-start.1) | collective-permute-done | bytes 81952 | tf_op jit(solution)/shard_map/ppermute | solution.py:209
  52.2 1.2 all-to-all-done.1
  53.4 0.7 broadcast_in_dim.41
  54.1 5.9 %all-to-all-start.2 = ((bf16[8,32,256]{2,1,0:T(8,128)(2,1)}), bf16[8,32,256]{2,1,0:T(8,128)(2,1)S(1)}, u32[]{:S(2)}, u32[]{:S(2)}) async-start(bf16[8,32,256]{2,1,0:T(8,128)(2,1)} %broadcast_in_dim.41), calls=%async_computation.2 | async-start | bytes 262144 | tf_op jit(solution)/shard_map/all_to_all | solution.py:230
  60.0 0.0 all-gather.10.cloned.1.call-start
  60.0 1.0 fusion.2
  61.1 12.6 %all-gather = bf16[1280,256]{1,0:T(8,128)(2,1)S(1)} all-gather(bf16[320,256]{1,0:T(8,128)(2,1)S(1)} %fusion.2), channel_id=2, replica_groups=mesh['x'=4,'zl'=8,'y'=4,'core'=2,'zh'=2] {'x'}, dimensions={0}, use_global_device_ids=true | all-gather | bytes 819200 | tf_op jit(solution)/shard_map/all_gather | solution.py:228
  73.7 0.1 concatenate.9
  73.8 0.0 all-to-all-done.2
  73.9 12.3 %all-gather.3 = bf16[1536,256]{1,0:T(8,128)(2,1)S(1)} all-gather(bf16[384,256]{1,0:T(8,128)(2,1)S(1)} %pad_maximum_fusion.1), channel_id=5, replica_groups=mesh['x'=4,'zl'=8,'y'=4,'core'=2,'zh'=2] {'x'}, dimensions={0}, use_global_device_ids=true | all-gather | bytes 983040 | tf_op jit(solution)/shard_map/all_gather | solution.py:234
  86.1 0.0 copy-start.1
  86.1 0.8 slice.75
  86.9 0.0 all-gather.10.cloned.1.call-update
  87.6 0.0 copy-done.6
  87.6 0.0 copy-done.8
  87.6 0.1 copy.14.gain_ref
  87.8 2.1 %all-gather.8.cloned.1.call-done.kv_ref = bf16[2560,512]{1,0:T(8,128)(2,1)} async-done(((bf16[320,512]{1,0:T(8,128)(2,1)}), bf16[2560,512]{1,0:T(8,128)(2,1)}) %all-gather.8.cloned.1.call-update) | async-done | bytes 2621456 | tf_op jit(solution)/shard_map/all_gather | solution.py:206
  89.9 0.0 copy-start
  89.9 1.7 copy-done
  91.6 8.1 %shard_map.91 = bf16[4,336,256]{2,1,0:T(8,128)(2,1)S(1)} custom-call(bf16[4,320,256]{2,1,0:T(8,128)(2,1)S(1)} %bitcast.12, bf16[2560,512]{1,0:T(8,128)(2,1)S(1)} %copy-done, f32[1,2560]{1,0:T(1,128)S(1)} %broadcast_in_dim.40.inverse_ref, f32[1,2560]{1,0:T(1,128)S(1)} %broadcast_in_dim.44.bias_ref, f32[256,1]{1,0:T(8,128)S(1)} %copy.14.gain_ref), custom_call_target="tpu_custom_call" | custom-call | flops 6710886400 | bytes 4194304 | tf_op jit(solution)/shard_map/pallas_call | solution.py:67
  99.7 0.0 copy-done.1
  99.8 0.0 copy-start.7
  99.8 11.6 %all_to_all.22.parts_ref = bf16[4,336,256]{2,1,0:T(8,128)(2,1)S(1)} all-to-all(bf16[4,336,256]{2,1,0:T(8,128)(2,1)S(1)} %shard_map.91), channel_id=1, replica_groups=mesh['x'=4,'zl'=8,'y'=4,'core'=2,'zh'=2] {'x'}, dimensions={0} | all-to-all | bytes 1376256 | tf_op jit(solution)/shard_map/all_to_all | solution.py:246
  111.3 0.6 shard_map.92
  111.9 11.9 %collective-permute-start.3 = (bf16[320,256]{1,0:T(8,128)(2,1)S(1)}, bf16[320,256]{1,0:T(8,128)(2,1)S(1)}, u32[]{:S(2)}, u32[]{:S(2)}) collective-permute-start(bf16[320,256]{1,0:T(8,128)(2,1)S(1)} %shard_map.92), channel_id=1, source_target_pairs={{0,1},{1,0},{2,3},{3,2},{4,5},{5,4},{6,7},{7,6},{8,9},{9,8},{10,11... | collective-permute-start | bytes 491528 | tf_op jit(solution)/shard_map/ppermute | solution.py:248
  123.8 11.9 %all-gather.1 = bf16[1280,256]{1,0:T(8,128)(2,1)S(1)} all-gather(bf16[320,256]{1,0:T(8,128)(2,1)S(1)} %shard_map.92), channel_id=3, replica_groups=mesh['x'=4,'zl'=8,'y'=4,'core'=2,'zh'=2] {'y'}, dimensions={0}, use_global_device_ids=true | all-gather | bytes 819200 | tf_op jit(solution)/shard_map/all_gather | solution.py:249
  135.7 0.0 copy-start.2
  135.7 5.5 %collective-permute-start.2 = (bf16[4,320,256]{2,1,0:T(8,128)(2,1)S(1)}, bf16[4,320,256]{2,1,0:T(8,128)(2,1)S(1)}, u32[]{:S(2)}, u32[]{:S(2)}) collective-permute-start(bf16[4,320,256]{2,1,0:T(8,128)(2,1)S(1)} %bitcast.15), channel_id=1, source_target_pairs={{0,2},{2,0},{1,3},{3,1},{4,6},{6,4},{5,7},{7,5},{8,10},{10,8},{9,1... | collective-permute-start | bytes 1966088 | tf_op jit(solution)/shard_map/ppermute | solution.py:250
  141.3 3.0 %collective-permute-done.3 = bf16[320,256]{1,0:T(8,128)(2,1)S(1)} collective-permute-done((bf16[320,256]{1,0:T(8,128)(2,1)S(1)}, bf16[320,256]{1,0:T(8,128)(2,1)S(1)}, u32[]{:S(2)}, u32[]{:S(2)}) %collective-permute-start.3) | collective-permute-done | bytes 163872 | tf_op jit(solution)/shard_map/ppermute | solution.py:248
  144.2 15.1 %all-gather.2 = bf16[1280,256]{1,0:T(8,128)(2,1)S(1)} all-gather(bf16[320,256]{1,0:T(8,128)(2,1)S(1)} %collective-permute-done.3), channel_id=4, replica_groups=mesh['x'=4,'zl'=8,'y'=4,'core'=2,'zh'=2] {'y'}, dimensions={0}, use_global_device_ids=true | all-gather | bytes 819200 | tf_op jit(solution)/shard_map/all_gather | solution.py:251
  159.4 0.0 copy-start.3
  159.4 9.0 %collective-permute-start.4 = (bf16[4,320,256]{2,1,0:T(8,128)(2,1)S(1)}, bf16[4,320,256]{2,1,0:T(8,128)(2,1)S(1)}, u32[]{:S(2)}, u32[]{:S(2)}) collective-permute-start(bf16[4,320,256]{2,1,0:T(8,128)(2,1)S(1)} %bitcast.17), channel_id=1, source_target_pairs={{0,2},{2,0},{1,3},{3,1},{4,6},{6,4},{5,7},{7,5},{8,10},{10,8},{9,1... | collective-permute-start | bytes 1966088 | tf_op jit(solution)/shard_map/ppermute | solution.py:252
  168.4 0.0 copy-done.7
  168.4 0.6 broadcast_in_dim.46.gate_ref
  169.0 0.7 pad_add_fusion.place_ref
  169.7 0.0 all-gather.10.cloned.1.call-done
  169.7 0.0 collective-permute-done.2.core_ref
  169.7 0.0 copy-start.4
  169.7 0.4 collective-permute-done.4.both_ref
  170.1 0.0 copy-start.5
  170.1 0.0 copy-done.2
  170.1 0.0 copy-done.3
  170.1 0.4 copy-done.4
  170.5 0.4 copy-done.5
  170.9 5.3 %shard_map.93 = bf16[320,320]{1,0:T(8,128)(2,1)} custom-call(s32[2]{0:T(128)} %pad_add_fusion.place_ref, bf16[4,320,256]{2,1,0:T(8,128)(2,1)} %bitcast.16, bf16[4,320,256]{2,1,0:T(8,128)(2,1)} %copy-done.4, bf16[4,320,256]{2,1,0:T(8,128)(2,1)} %bitcast.18, bf16[4,320,256]{2,1,0:T(8,128)(2,1)} %copy-done.5, bf16[8,4,128,256]{3,2,1,0:T(8,128)(2,1)} %bitcast.19, ...), custom_call_target="tpu_custom_call" | custom-call | tf_op jit(solution)/shard_map/pallas_call | solution.py:175
  (14 shorter events, 0.2 us)
Async XLA Ops:
  6.5 81.0 %copy-start.6 = (s32[2560]{0:T(1024)S(1)}, s32[2560]{0:T(1024)}, u32[]{:S(2)}) copy-start(s32[2560]{0:T(1024)} %constant.25.clone) | copy-start | bytes 30724
  6.5 81.1 %copy-start.8 = (f32[256]{0:T(256)S(1)}, f32[256]{0:T(256)}, u32[]{:S(2)}) copy-start(f32[256]{0:T(256)} %param.14) | copy-start | bytes 3076
  6.5 83.3 %all-gather.8.cloned.1.call-start = ((), (), s32[]{:S(2)}) async-start(), calls=%async_computation.4 | async-start | bytes 2949120 | tf_op jit(solution)/shard_map/all_gather | solution.py:206
  19.2 21.3 %collective-permute-start = (f32[2,320]{1,0:T(2,128)S(1)}, f32[2,320]{1,0:T(2,128)S(1)}, u32[]{:S(2)}, u32[]{:S(2)}) collective-permute-start(f32[2,320]{1,0:T(2,128)S(1)} %reduce_sum.29), channel_id=1, source_target_pairs={{0,1},{1,0},{2,3},{3,2},{4,5},{5,4},{6,7},{7,6},{8,9},{9,8},{10,11... | collective-permute-start | bytes 7688 | tf_op jit(solution)/shard_map/ppermute | solution.py:221
  33.7 18.5 %collective-permute-start.1 = (bf16[160,256]{1,0:T(8,128)(2,1)}, bf16[160,256]{1,0:T(8,128)(2,1)S(1)}, u32[]{:S(2)}, u32[]{:S(2)}) collective-permute-start(bf16[160,256]{1,0:T(8,128)(2,1)} %bitcast.22), channel_id=1, source_target_pairs={{0,0},{1,32},{2,64},{3,96},{4,128},{5,160},{6,192},{7,224},{8,256}... | collective-permute-start | bytes 245768 | tf_op jit(solution)/shard_map/ppermute | solution.py:209
  41.1 12.3 %all-to-all-start.1 = ((f32[8,1,320]{2,1,0:T(1,128)}), f32[8,1,320]{2,1,0:T(1,128)S(1)}, u32[]{:S(2)}, u32[]{:S(2)}) async-start(f32[8,1,320]{2,1,0:T(1,128)} %broadcast_in_dim.39), calls=%async_computation.1 | async-start | bytes 24576 | tf_op jit(solution)/shard_map/all_to_all | solution.py:223
  54.1 19.7 %all-to-all-start.2 = ((bf16[8,32,256]{2,1,0:T(8,128)(2,1)}), bf16[8,32,256]{2,1,0:T(8,128)(2,1)S(1)}, u32[]{:S(2)}, u32[]{:S(2)}) async-start(bf16[8,32,256]{2,1,0:T(8,128)(2,1)} %broadcast_in_dim.41), calls=%async_computation.2 | async-start | bytes 262144 | tf_op jit(solution)/shard_map/all_to_all | solution.py:230
  60.0 109.6 %all-gather.10.cloned.1.call-start = ((), (), s32[]{:S(2)}) async-start(), calls=%async_computation.5 | async-start | bytes 2359296 | tf_op jit(solution)/shard_map/all_gather | solution.py:237
  86.1 13.6 %copy-start.1 = (bf16[1536,256]{1,0:T(8,128)(2,1)}, bf16[1536,256]{1,0:T(8,128)(2,1)S(1)}, u32[]{:S(2)}) copy-start(bf16[1536,256]{1,0:T(8,128)(2,1)S(1)} %all-gather.3) | copy-start | bytes 2359300
  89.9 1.7 copy-start
  99.8 68.7 %copy-start.7 = (f32[320]{0:T(512)S(1)}, f32[320]{0:T(512)}, u32[]{:S(2)}) copy-start(f32[320]{0:T(512)} %param.15) | copy-start | bytes 3844
  111.9 32.3 %collective-permute-start.3 = (bf16[320,256]{1,0:T(8,128)(2,1)S(1)}, bf16[320,256]{1,0:T(8,128)(2,1)S(1)}, u32[]{:S(2)}, u32[]{:S(2)}) collective-permute-start(bf16[320,256]{1,0:T(8,128)(2,1)S(1)} %shard_map.92), channel_id=1, source_target_pairs={{0,1},{1,0},{2,3},{3,2},{4,5},{5,4},{6,7},{7,6},{8,9},{9,8},{10,11... | collective-permute-start | bytes 491528 | tf_op jit(solution)/shard_map/ppermute | solution.py:248
  135.7 34.4 %copy-start.2 = (bf16[1280,256]{1,0:T(8,128)(2,1)}, bf16[1280,256]{1,0:T(8,128)(2,1)S(1)}, u32[]{:S(2)}) copy-start(bf16[1280,256]{1,0:T(8,128)(2,1)S(1)} %all-gather.1) | copy-start | bytes 1966084
  135.7 34.0 %collective-permute-start.2 = (bf16[4,320,256]{2,1,0:T(8,128)(2,1)S(1)}, bf16[4,320,256]{2,1,0:T(8,128)(2,1)S(1)}, u32[]{:S(2)}, u32[]{:S(2)}) collective-permute-start(bf16[4,320,256]{2,1,0:T(8,128)(2,1)S(1)} %bitcast.15), channel_id=1, source_target_pairs={{0,2},{2,0},{1,3},{3,1},{4,6},{6,4},{5,7},{7,5},{8,10},{10,8},{9,1... | collective-permute-start | bytes 1966088 | tf_op jit(solution)/shard_map/ppermute | solution.py:250
  159.4 10.7 %copy-start.3 = (bf16[1280,256]{1,0:T(8,128)(2,1)}, bf16[1280,256]{1,0:T(8,128)(2,1)S(1)}, u32[]{:S(2)}) copy-start(bf16[1280,256]{1,0:T(8,128)(2,1)S(1)} %all-gather.2) | copy-start | bytes 1966084
  159.4 10.7 %collective-permute-start.4 = (bf16[4,320,256]{2,1,0:T(8,128)(2,1)S(1)}, bf16[4,320,256]{2,1,0:T(8,128)(2,1)S(1)}, u32[]{:S(2)}, u32[]{:S(2)}) collective-permute-start(bf16[4,320,256]{2,1,0:T(8,128)(2,1)S(1)} %bitcast.17), channel_id=1, source_target_pairs={{0,2},{2,0},{1,3},{3,1},{4,6},{6,4},{5,7},{7,5},{8,10},{10,8},{9,1... | collective-permute-start | bytes 1966088 | tf_op jit(solution)/shard_map/ppermute | solution.py:252
  169.7 0.9 copy-start.4
  170.1 0.8 copy-start.5
Sparse Core Ops, SparseCore 0:
  9.4 80.3 all-gather.7
  92.0 73.0 all-gather.9
